TPU v7x, 128 devices: a whole 4x4x4 slice. The times are simulated.
128 devices in a mesh: dp: 8 (over z, core), head: 16 (over x, y).
Axes of the slice: x: 4, y: 4, z: 4, core: 2. Of those that a mesh axis runs over, the one named last changes fastest.
Arguments:
- tokens: bfloat16 [16, 1024, 2048], P('dp', 'head'), may hold values from -6 to 6
- cotangent: bfloat16 [16, 1024, 2048], P('dp', 'head'), may hold values from -6 to 6
- seq_lengths: int32 [16], P('dp'), may hold values from 256 to 1024, as said below
- exit_layers: int32 [16, 1024], P('dp'), may hold values from 1 to 24, as said below
- layer_index: int32 [1], replicated, may hold values from 6 to 17
- ln1_gain: float32 [2048], replicated, may hold values from 0.5 to 1.5
- ln1_shift: float32 [2048], replicated, may hold values from -4 to 4
- q_weight: float32 [2048, 2048], P('dp', 'head'), may hold values from -0.1875 to 0.1875
- q_bias: float32 [2048], replicated, may hold values from -4 to 4
- k_weight: float32 [2048, 2048], P('dp', 'head'), may hold values from -0.1875 to 0.1875
- v_weight: float32 [2048, 2048], P('dp', 'head'), may hold values from -0.125 to 0.125
- v_bias: float32 [2048], replicated, may hold values from -4 to 4
- out_weight: float32 [2048, 2048], P('dp', 'head'), may hold values from -0.5 to 0.5
- out_bias: float32 [2048], replicated, may hold values from -4 to 4
- ln2_gain: float32 [2048], replicated, may hold values from 0.5 to 1.5
- ln2_shift: float32 [2048], replicated, may hold values from -4 to 4
- up_weight: float32 [2048, 8192], P('dp', 'head'), may hold values from -0.125 to 0.125
- up_bias: float32 [8192], replicated, may hold values from -6 to 6
- down_weight: float32 [2048, 8192], P('dp', 'head'), may hold values from -0.0625 to 0.0625
- down_bias: float32 [2048], replicated, may hold values from -4 to 4
Outputs:
- result: bfloat16 [16, 1024, 2048], P('dp', 'head')
- grad_tokens: float32 [16, 1024, 2048], P('dp', 'head')
- grad_ln1_gain: float32 [2048], replicated
- grad_ln1_shift: float32 [2048], replicated
- grad_q_weight: float32 [2048, 2048], P('dp', 'head')
- grad_q_bias: float32 [2048], replicated
- grad_k_weight: float32 [2048, 2048], P('dp', 'head')
- grad_v_weight: float32 [2048, 2048], P('dp', 'head')
- grad_v_bias: float32 [2048], replicated
- grad_out_weight: float32 [2048, 2048], P('dp', 'head')
- grad_out_bias: float32 [2048], replicated
- grad_ln2_gain: float32 [2048], replicated
- grad_ln2_shift: float32 [2048], replicated
- grad_up_weight: float32 [2048, 8192], P('dp', 'head')
- grad_up_bias: float32 [8192], replicated
- grad_down_weight: float32 [2048, 8192], P('dp', 'head')
- grad_down_bias: float32 [2048], replicated
Inputs may be any that keep to these rules, and one draw needn't show every extreme that they name: `seq_lengths`: in the 2 sequences of each dp index one has 1024 tokens and exit layer 24 at every position. `exit_layers`: every other sequence's exit layers fall linearly over its own length: max(1, 24 - floor(p * r / length)) at position p, with a whole r of 12 to 23 of its own.
All inputs are finite; a program needn't handle non-finite values.
Results may differ from a plain program's by a relative error of at most 0.022.
Values may be sent and summed in bfloat16 or wider, within the bound.
No kernel may reach another device: no remote copies, remote signals or barrier semaphores. Data moves between devices by JAX's collectives and lax.ppermute only.
A program may use at most 384 MiB of HBM per device.

v0:
```python
from functools import partial

import jax
import jax.numpy as jnp
from jax import lax
from jax.sharding import PartitionSpec as P

HEAD_DIM = 64


def as_sent(array):
    return jax.tree.map(lambda a: a.astype(jnp.bfloat16) if a.dtype == jnp.float32 else a, array)


def product(left_side, right_side):
    return jnp.dot(left_side, right_side, preferred_element_type=jnp.float32)


def product_t(left_side, right_side):
    return lax.dot_general(
        left_side, right_side, (((1,), (1,)), ((), ())), preferred_element_type=jnp.float32
    )


def outer_sum(left_side, right_side):
    return lax.dot_general(
        left_side, right_side, (((0,), (0,)), ((), ())), preferred_element_type=jnp.float32
    )


def norm_parts(values, gain_vec, shift_vec):
    average = jnp.mean(values, -1, keepdims=True)
    centered = values - average
    inverse = lax.rsqrt(jnp.mean(centered * centered, -1, keepdims=True) + 1e-05)
    unit_rows = centered * inverse
    return (centered * inverse * gain_vec + shift_vec, unit_rows, inverse)


def norm_back(gradient, unit_rows, inverse, gain_vec):
    scaled = gradient * gain_vec
    return inverse * (
        scaled
        - jnp.mean(scaled, -1, keepdims=True)
        - unit_rows * jnp.mean(scaled * unit_rows, -1, keepdims=True)
    )


def fetch(master):
    shard_piece = master.astype(jnp.bfloat16)
    shard_piece = lax.all_gather(shard_piece, "head", axis=1, tiled=True)
    return lax.all_gather(shard_piece, "dp", axis=0, tiled=True)


def settle(gradient):
    gradient = lax.psum_scatter(
        gradient.astype(jnp.bfloat16), "head", scatter_dimension=1, tiled=True
    ).astype(jnp.float32)
    return lax.psum_scatter(
        gradient.astype(jnp.bfloat16), "dp", scatter_dimension=0, tiled=True
    ).astype(jnp.float32)


def score_block(q_block, key_heads, live_keys, offset, head_dim):
    span_rows = q_block.shape[0]
    seq_len = key_heads.shape[0]
    q_places = offset + jnp.arange(span_rows)
    k_places = jnp.arange(seq_len)
    allowed = (k_places[None, :] <= q_places[:, None]) & live_keys[None, :]
    scores = jnp.einsum(
        "qhd,khd->hqk", q_block, key_heads, preferred_element_type=jnp.float32
    ) * head_dim ** (-0.5)
    return jnp.where(allowed[None], scores, -1000000000.0)


def attend_forward(packed, head_dim):
    query_rows, key_rows, value_rows, live_keys = packed
    seq_len, col_width = query_rows.shape
    head_count = col_width // head_dim
    span_rows = min(512, seq_len)
    key_heads = key_rows.reshape(seq_len, head_count, head_dim)
    value_heads = value_rows.reshape(seq_len, head_count, head_dim)
    out_blocks = []
    log_blocks = []
    for offset in range(0, seq_len, span_rows):
        q_block = query_rows[offset : offset + span_rows].reshape(span_rows, head_count, head_dim)
        scores = score_block(q_block, key_heads, live_keys, offset, head_dim)
        maximum = jnp.max(scores, -1, keepdims=True)
        exp_terms = jnp.exp(scores - maximum)
        denom = jnp.sum(exp_terms, -1, keepdims=True)
        prob_low = (exp_terms / denom).astype(jnp.bfloat16)
        mixed_heads = jnp.einsum(
            "hqk,khd->qhd", prob_low, value_heads, preferred_element_type=jnp.float32
        )
        out_blocks.append(mixed_heads.reshape(span_rows, col_width))
        log_blocks.append((maximum + jnp.log(denom))[..., 0])
    return (jnp.concatenate(out_blocks, 0), jnp.concatenate(log_blocks, 1))


def attend_backward(packed, head_dim):
    query_rows, key_rows, value_rows, live_keys, log_sums, grad_out = packed
    seq_len, col_width = query_rows.shape
    head_count = col_width // head_dim
    span_rows = min(512, seq_len)
    factor = head_dim ** (-0.5)
    key_heads = key_rows.reshape(seq_len, head_count, head_dim)
    value_heads = value_rows.reshape(seq_len, head_count, head_dim)
    grad_keys = jnp.zeros((seq_len, head_count, head_dim), jnp.float32)
    grad_values = jnp.zeros((seq_len, head_count, head_dim), jnp.float32)
    grad_queries = []
    for offset in range(0, seq_len, span_rows):
        q_block = query_rows[offset : offset + span_rows].reshape(span_rows, head_count, head_dim)
        g_block = grad_out[offset : offset + span_rows].reshape(span_rows, head_count, head_dim)
        scores = score_block(q_block, key_heads, live_keys, offset, head_dim)
        prob_rows = jnp.exp(scores - log_sums[:, offset : offset + span_rows, None])
        d_probs = jnp.einsum(
            "qhd,khd->hqk", g_block, value_heads, preferred_element_type=jnp.float32
        )
        grad_values = grad_values + jnp.einsum(
            "hqk,qhd->khd",
            prob_rows.astype(jnp.bfloat16),
            g_block,
            preferred_element_type=jnp.float32,
        )
        row_inner = jnp.sum(prob_rows * d_probs, -1, keepdims=True)
        d_scores = (prob_rows * (d_probs - row_inner)).astype(jnp.bfloat16)
        grad_queries.append(
            jnp.einsum(
                "hqk,khd->qhd", d_scores, key_heads, preferred_element_type=jnp.float32
            ).reshape(span_rows, col_width)
            * factor
        )
        grad_keys = (
            grad_keys
            + jnp.einsum("hqk,qhd->khd", d_scores, q_block, preferred_element_type=jnp.float32)
            * factor
        )
    return (
        jnp.concatenate(grad_queries, 0).astype(jnp.bfloat16),
        grad_keys.reshape(seq_len, col_width).astype(jnp.bfloat16),
        grad_values.reshape(seq_len, col_width).astype(jnp.bfloat16),
    )


def shards(
    tokens,
    cotangent,
    seq_lengths,
    exit_layers,
    layer_index,
    ln1_gain,
    ln1_shift,
    q_weight,
    q_bias,
    k_weight,
    v_weight,
    v_bias,
    out_weight,
    out_bias,
    ln2_gain,
    ln2_shift,
    up_weight,
    up_bias,
    down_weight,
    down_bias,
):
    seq_count, own_rows, model_dim = tokens.shape
    full_len = exit_layers.shape[1]
    head_index = lax.axis_index("head")
    positions = jnp.arange(full_len)
    live_all = (positions[None, :] < seq_lengths[:, None]) & (exit_layers > layer_index[0])
    live_mine = lax.dynamic_slice_in_dim(live_all, head_index * own_rows, own_rows, 1)
    keep_rows = live_mine.reshape(-1, 1).astype(jnp.float32)
    inputs = tokens.astype(jnp.float32).reshape(-1, model_dim)
    w_query = fetch(q_weight)
    w_key = fetch(k_weight)
    w_value = fetch(v_weight)
    w_out = fetch(out_weight)
    w_up = fetch(up_weight)
    w_down = fetch(down_weight)
    head_cols = w_query.shape[1]
    normed1, unit1, inverse1 = norm_parts(inputs, ln1_gain, ln1_shift)
    lowered1 = normed1.astype(jnp.bfloat16)
    q_low = (product(lowered1, w_query) + q_bias).astype(jnp.bfloat16)
    k_low = product(lowered1, w_key).astype(jnp.bfloat16)
    v_low = (product(lowered1, w_value) + v_bias).astype(jnp.bfloat16)
    q_heads, k_heads, v_heads = (
        lax.all_to_all(
            q_low.reshape(seq_count, own_rows, model_dim),
            "head",
            split_axis=2,
            concat_axis=1,
            tiled=True,
        ),
        lax.all_to_all(
            k_low.reshape(seq_count, own_rows, model_dim),
            "head",
            split_axis=2,
            concat_axis=1,
            tiled=True,
        ),
        lax.all_to_all(
            v_low.reshape(seq_count, own_rows, model_dim),
            "head",
            split_axis=2,
            concat_axis=1,
            tiled=True,
        ),
    )
    mixed_out, log_sums = lax.map(
        partial(attend_forward, head_dim=HEAD_DIM), (q_heads, k_heads, v_heads, live_all)
    )
    mixed_low = mixed_out.astype(jnp.bfloat16)
    attn_src = lax.all_to_all(mixed_low, "head", split_axis=1, concat_axis=2, tiled=True).reshape(
        -1, model_dim
    )
    branch_one = product_t(attn_src, w_out) + out_bias
    middle = inputs + keep_rows * branch_one
    normed2, unit2, inverse2 = norm_parts(middle, ln2_gain, ln2_shift)
    lowered2 = normed2.astype(jnp.bfloat16)
    up_proj = product(lowered2, w_up) + up_bias
    hidden_low = jax.nn.gelu(up_proj, approximate=False).astype(jnp.bfloat16)
    branch_two = product_t(hidden_low, w_down) + down_bias
    result = (middle + keep_rows * branch_two).astype(jnp.bfloat16).reshape(tokens.shape)
    grad_y = cotangent.astype(jnp.float32).reshape(-1, model_dim)
    g_ffn = (keep_rows * grad_y).astype(jnp.bfloat16)
    g_hidden = product(g_ffn, w_down)
    grad_down_weight = settle(outer_sum(g_ffn, hidden_low))
    gelu_value, gelu_pull = jax.vjp(partial(jax.nn.gelu, approximate=False), up_proj)
    g_up = gelu_pull(g_hidden)[0].astype(jnp.bfloat16)
    grad_up_weight = settle(outer_sum(lowered2, g_up))
    g_norm2 = product_t(g_up, w_up)
    grad_mid = grad_y + norm_back(g_norm2, unit2, inverse2, ln2_gain)
    g_attn = (keep_rows * grad_mid).astype(jnp.bfloat16)
    g_heads = product(g_attn, w_out).astype(jnp.bfloat16)
    grad_out_weight = settle(outer_sum(g_attn, attn_src))
    g_heads = lax.all_to_all(
        g_heads.reshape(seq_count, own_rows, model_dim),
        "head",
        split_axis=2,
        concat_axis=1,
        tiled=True,
    )
    d_query, d_key, d_value = lax.map(
        partial(attend_backward, head_dim=HEAD_DIM),
        (q_heads, k_heads, v_heads, live_all, log_sums, g_heads),
    )
    d_query, d_key, d_value = (
        lax.all_to_all(as_sent(d_query), "head", split_axis=1, concat_axis=2, tiled=True).astype(
            d_query.dtype
        ),
        lax.all_to_all(as_sent(d_key), "head", split_axis=1, concat_axis=2, tiled=True).astype(
            d_key.dtype
        ),
        lax.all_to_all(as_sent(d_value), "head", split_axis=1, concat_axis=2, tiled=True).astype(
            d_value.dtype
        ),
    )
    d_query = d_query.reshape(-1, head_cols)
    d_key = d_key.reshape(-1, head_cols)
    d_value = d_value.reshape(-1, head_cols)
    grad_q_weight = settle(outer_sum(lowered1, d_query))
    grad_k_weight = settle(outer_sum(lowered1, d_key))
    grad_v_weight = settle(outer_sum(lowered1, d_value))
    g_norm1 = product_t(d_query, w_query) + product_t(d_key, w_key) + product_t(d_value, w_value)
    grad_tokens = (grad_mid + norm_back(g_norm1, unit1, inverse1, ln1_gain)).reshape(tokens.shape)
    q_bias_sum = jnp.sum(d_query.astype(jnp.float32), 0)
    v_bias_sum = jnp.sum(d_value.astype(jnp.float32), 0)
    up_bias_sum = jnp.sum(g_up.astype(jnp.float32), 0)
    vector_sums = lax.psum(
        (
            jnp.sum(g_norm1 * unit1, 0),
            jnp.sum(g_norm1, 0),
            q_bias_sum,
            v_bias_sum,
            jnp.sum(g_attn.astype(jnp.float32), 0),
            jnp.sum(g_norm2 * unit2, 0),
            jnp.sum(g_norm2, 0),
            up_bias_sum,
            jnp.sum(g_ffn.astype(jnp.float32), 0),
        ),
        ("dp", "head"),
    )
    return (
        result,
        grad_tokens,
        vector_sums[0],
        vector_sums[1],
        grad_q_weight,
        vector_sums[2],
        grad_k_weight,
        grad_v_weight,
        vector_sums[3],
        grad_out_weight,
        vector_sums[4],
        vector_sums[5],
        vector_sums[6],
        grad_up_weight,
        vector_sums[7],
        grad_down_weight,
        vector_sums[8],
    )


def solution(mesh):
    in_specs = (
        P("dp", "head", None),
        P("dp", "head", None),
        P("dp"),
        P("dp", None),
        P(),
        P(),
        P(),
        P("dp", "head"),
        P(),
        P("dp", "head"),
        P("dp", "head"),
        P(),
        P("dp", "head"),
        P(),
        P(),
        P(),
        P("dp", "head"),
        P(),
        P("dp", "head"),
        P(),
    )
    out_specs = (
        P("dp", "head", None),
        P("dp", "head", None),
        P(),
        P(),
        P("dp", "head"),
        P(),
        P("dp", "head"),
        P("dp", "head"),
        P(),
        P("dp", "head"),
        P(),
        P(),
        P(),
        P("dp", "head"),
        P(),
        P("dp", "head"),
        P(),
    )
    return jax.shard_map(shards, mesh=mesh, in_specs=in_specs, out_specs=out_specs, check_vma=False)
```

profile of v0, /device:TPU:1, one launch (start us, length us, event | category | flops | bytes accessed | tf_op | source)
XLA Modules:
  0.0 2056.7 jit_solution(7868815517028312516)
XLA Ops:
  17.4 38.4 %all-gather.13.cloned.1.call-done = bf16[256,2048]{1,0:T(8,128)(2,1)} async-done(((bf16[256,128]{1,0:T(8,128)(2,1)}), bf16[256,2048]{1,0:T(8,128)(2,1)}) %all-gather.13.cloned.1.call-update) | async-done | bytes 1048592 | tf_op jit(solution)/shard_map/all_gather | solution.py:50
  55.9 45.3 %all-gather.17.cloned.1.call-done = bf16[256,2048]{1,0:T(8,128)(2,1)} async-done(((bf16[256,128]{1,0:T(8,128)(2,1)}), bf16[256,2048]{1,0:T(8,128)(2,1)}) %all-gather.17.cloned.1.call-update) | async-done | bytes 1048592 | tf_op jit(solution)/shard_map/all_gather | solution.py:50
  101.2 45.3 %all-gather.21.cloned.1.call-done = bf16[256,2048]{1,0:T(8,128)(2,1)} async-done(((bf16[256,128]{1,0:T(8,128)(2,1)}), bf16[256,2048]{1,0:T(8,128)(2,1)}) %all-gather.21.cloned.1.call-update) | async-done | bytes 1048592 | tf_op jit(solution)/shard_map/all_gather | solution.py:50
  146.6 45.1 %all-gather.25.cloned.1.call-done = bf16[256,2048]{1,0:T(8,128)(2,1)} async-done(((bf16[256,128]{1,0:T(8,128)(2,1)}), bf16[256,2048]{1,0:T(8,128)(2,1)}) %all-gather.25.cloned.1.call-update) | async-done | bytes 1048592 | tf_op jit(solution)/shard_map/all_gather | solution.py:50
  191.8 59.8 %all-gather.29.cloned.1.call-done = bf16[256,8192]{1,0:T(8,128)(2,1)} async-done(((bf16[256,512]{1,0:T(8,128)(2,1)}), bf16[256,8192]{1,0:T(8,128)(2,1)}) %all-gather.29.cloned.1.call-update) | async-done | bytes 4194320 | tf_op jit(solution)/shard_map/all_gather | solution.py:50
  251.7 59.3 %all-gather.33.cloned.1.call-done = bf16[256,8192]{1,0:T(8,128)(2,1)} async-done(((bf16[256,512]{1,0:T(8,128)(2,1)}), bf16[256,8192]{1,0:T(8,128)(2,1)}) %all-gather.33.cloned.1.call-update) | async-done | bytes 4194320 | tf_op jit(solution)/shard_map/all_gather | solution.py:50
  312.2 51.2 %all-gather.15.cloned.1.call-done = bf16[2048,2048]{1,0:T(8,128)(2,1)} async-done(((bf16[256,2048]{1,0:T(8,128)(2,1)}), bf16[2048,2048]{1,0:T(8,128)(2,1)}) %all-gather.15.cloned.1.call-update) | async-done | bytes 8388624 | tf_op jit(solution)/shard_map/all_gather | solution.py:51
  370.4 6.5 all-to-all-start
  376.9 38.2 %all-gather.19.cloned.1.call-done = bf16[2048,2048]{1,0:T(8,128)(2,1)} async-done(((bf16[256,2048]{1,0:T(8,128)(2,1)}), bf16[2048,2048]{1,0:T(8,128)(2,1)}) %all-gather.19.cloned.1.call-update) | async-done | bytes 8388624 | tf_op jit(solution)/shard_map/all_gather | solution.py:51
  422.1 6.5 all-to-all-start.1
  428.6 38.3 %all-gather.23.cloned.1.call-done = bf16[2048,2048]{1,0:T(8,128)(2,1)} async-done(((bf16[256,2048]{1,0:T(8,128)(2,1)}), bf16[2048,2048]{1,0:T(8,128)(2,1)}) %all-gather.23.cloned.1.call-update) | async-done | bytes 8388624 | tf_op jit(solution)/shard_map/all_gather | solution.py:51
  473.8 7.0 all-to-all-start.2
  493.6 48.2 %while.26 = (s32[]{:T(128)}, bf16[2,1024,128]{2,0,1:T(2,128)(2,1)}, f32[2,2,1024]{2,1,0:T(2,128)}, bf16[2,1024,128]{1,2,0:T(8,128)(2,1)}, pred[2,1024]{1,0:T(4,1...) while((s32[]{:T(128)}, bf16[2,1024,128]{2,0,1:T(2,128)(2,1)}, ...), condition=%wide.region_7.8_spmd, body=%wide.region_2.7_spmd.sunk | while | flops 564658688 | bytes 34167952 | solution.py:209
  504.2 12.9 dynamic_update_slice.27
  528.2 12.9 dynamic_update_slice.27
  547.3 7.6 all-to-all-done.3
  555.4 6.6 fusion.72
  562.3 113.9 %all-gather.31.cloned.1.call-done = bf16[2048,8192]{1,0:T(8,128)(2,1)} async-done(((bf16[256,8192]{1,0:T(8,128)(2,1)}), bf16[2048,8192]{1,0:T(8,128)(2,1)}) %all-gather.31.cloned.1.call-update) | async-done | bytes 33554448 | tf_op jit(solution)/shard_map/all_gather | solution.py:51
  676.2 17.5 convolution_add_fusion.1
  693.7 141.1 %all-gather.35.cloned.1.call-done = bf16[2048,8192]{1,0:T(8,128)(2,1)} async-done(((bf16[256,8192]{1,0:T(8,128)(2,1)}), bf16[2048,8192]{1,0:T(8,128)(2,1)}) %all-gather.35.cloned.1.call-update) | async-done | bytes 33554448 | tf_op jit(solution)/shard_map/all_gather | solution.py:51
  834.8 23.3 %convert_reduce_fusion = (f32[8192]{0:T(1024)}, bf16[128,8192]{1,0:T(8,128)(2,1)S(1)}, f32[128,8192]{1,0:T(8,128)}) fusion(f32[128,8192]{1,0:T(8,128)} %convolution_add_fusion.1, bf16[128,2048]{1,0:T(8,128)(2,1)} %fusion.51, bf16[2048,8192]{1,0:T(8,128)(2,1)} %all-gather.35.cloned.1.call-done), kind=kOutput, calls=%fused_computation.81 | convolution fusion | flops 4372553728 | bytes 44597248 | tf_op jit(solution)/shard_map/dot_general | solution.py:16
  858.1 18.7 multiply_reduce_fusion.2
  880.3 5.7 convolution_convert_fusion.2
  886.0 12.3 copy.120
  905.2 7.0 all-to-all-start.4
  912.3 13.8 all-to-all-done.4
  928.6 64.5 %while.27 = (s32[]{:T(128)}, bf16[2,1024,128]{1,2,0:T(8,128)(2,1)}, bf16[2,1024,128]{1,2,0:T(8,128)(2,1)}, bf16[2,1024,128]{1,2,0:T(8,128)(2,1)}, bf16[2,1024,12...) while((s32[]{:T(128)}, bf16[2,1024,128]{1,2,0:T(8,128)(2,1)}, ...), condition=%wide.region_15.16_spmd, body=%wide.region_12.15_spmd.sunk | while | flops 1377171968 | bytes 143998608 | solution.py:243
  1001.8 7.5 all-to-all-done.5
  1017.0 12.4 copy.114
  1030.8 12.5 all_to_all.132
  1050.2 12.4 copy.116
  1064.0 15.4 all_to_all.133
  1087.0 12.4 copy.118
  1101.4 14.0 convolution_convert_fusion.1
  1119.6 13.7 convolution_convert_fusion
  1137.7 67.1 %reduce-scatter.39.cloned.1.call-done = bf16[128,2048]{1,0:T(8,128)(2,1)} async-done(((bf16[2048,2048]{1,0:T(8,128)(2,1)}), bf16[128,2048]{1,0:T(8,128)(2,1)}) %reduce-scatter.39.cloned.1.call-update) | async-done | bytes 524304
  1206.9 85.7 %reduce-scatter.41.cloned.1.call-done = bf16[128,2048]{1,0:T(8,128)(2,1)} async-done(((bf16[2048,2048]{1,0:T(8,128)(2,1)}), bf16[128,2048]{1,0:T(8,128)(2,1)}) %reduce-scatter.41.cloned.1.call-update) | async-done | bytes 524304
  1294.8 196.7 %reduce-scatter.29.cloned.1.call-done = bf16[2048,512]{1,0:T(8,128)(2,1)} async-done(((bf16[2048,8192]{1,0:T(8,128)(2,1)}), bf16[2048,512]{1,0:T(8,128)(2,1)}) %reduce-scatter.29.cloned.1.call-update) | async-done | bytes 2097168 | tf_op jit(solution)/shard_map/reduce_scatter | solution.py:55
  1493.3 195.9 %reduce-scatter.33.cloned.1.call-done = bf16[2048,512]{1,0:T(8,128)(2,1)} async-done(((bf16[2048,8192]{1,0:T(8,128)(2,1)}), bf16[2048,512]{1,0:T(8,128)(2,1)}) %reduce-scatter.33.cloned.1.call-update) | async-done | bytes 2097168 | tf_op jit(solution)/shard_map/reduce_scatter | solution.py:55
  1689.6 17.0 fusion.47
  1708.0 6.4 fusion.58
  1714.5 6.4 convolution_add_fusion.4
  1727.7 23.9 %reduce-scatter.21.cloned.1.call-done = bf16[256,128]{1,0:T(8,128)(2,1)} async-done(((bf16[2048,128]{1,0:T(8,128)(2,1)}), bf16[256,128]{1,0:T(8,128)(2,1)}) %reduce-scatter.21.cloned.1.call-update) | async-done | bytes 65552 | tf_op jit(solution)/shard_map/reduce_scatter | solution.py:58
  1753.1 30.7 %reduce-scatter.23.cloned.1.call-done = bf16[256,128]{1,0:T(8,128)(2,1)} async-done(((bf16[2048,128]{1,0:T(8,128)(2,1)}), bf16[256,128]{1,0:T(8,128)(2,1)}) %reduce-scatter.23.cloned.1.call-update) | async-done | bytes 65552 | tf_op jit(solution)/shard_map/reduce_scatter | solution.py:58
  1785.3 30.8 %reduce-scatter.25.cloned.1.call-done = bf16[256,128]{1,0:T(8,128)(2,1)} async-done(((bf16[2048,128]{1,0:T(8,128)(2,1)}), bf16[256,128]{1,0:T(8,128)(2,1)}) %reduce-scatter.25.cloned.1.call-update) | async-done | bytes 65552 | tf_op jit(solution)/shard_map/reduce_scatter | solution.py:58
  1817.6 33.2 %reduce-scatter.31.cloned.1.call-done = bf16[256,512]{1,0:T(8,128)(2,1)} async-done(((bf16[2048,512]{1,0:T(8,128)(2,1)}), bf16[256,512]{1,0:T(8,128)(2,1)}) %reduce-scatter.31.cloned.1.call-update) | async-done | bytes 262160 | tf_op jit(solution)/shard_map/reduce_scatter | solution.py:58
  1852.6 33.0 %reduce-scatter.35.cloned.1.call-done = bf16[256,512]{1,0:T(8,128)(2,1)} async-done(((bf16[2048,512]{1,0:T(8,128)(2,1)}), bf16[256,512]{1,0:T(8,128)(2,1)}) %reduce-scatter.35.cloned.1.call-update) | async-done | bytes 262160 | tf_op jit(solution)/shard_map/reduce_scatter | solution.py:58
  1887.4 150.7 %all-reduce.3.cloned.1.call-done = (f32[2048]{0:T(1024)}, f32[2048]{0:T(1024)}, f32[2048]{0:T(1024)}, f32[2048]{0:T(1024)}, f32[2048]{0:T(1024)}, /*index=5*/f32...) async-done(((f32[2048]{0:T(1024)}, f32[2048]{0:T(1024)}, f32[2048]{0:T(1024)}, f32[2048]{0:T(1024)}, f32[2048]{0:T(1024)}, /*index=5*/f32[2048]{0:T(1024)}, ...) | async-done | bytes 98320 | tf_op jit(solution)/shard_map/psum | solution.py:269
  (406 shorter events, 228.1 us)
Async XLA Ops:
  7.2 48.6 %all-gather.13.cloned.1.call-start = ((), (), s32[]{:S(2)}) async-start(), calls=%async_computation.20 | async-start | bytes 1114112 | tf_op jit(solution)/shard_map/all_gather | solution.py:50
  8.8 92.3 %all-gather.17.cloned.1.call-start = ((), (), s32[]{:S(2)}) async-start(), calls=%async_computation.22 | async-start | bytes 1114112 | tf_op jit(solution)/shard_map/all_gather | solution.py:50
  10.4 136.1 %all-gather.21.cloned.1.call-start = ((), (), s32[]{:S(2)}) async-start(), calls=%async_computation.24 | async-start | bytes 1114112 | tf_op jit(solution)/shard_map/all_gather | solution.py:50
  12.0 179.6 %all-gather.25.cloned.1.call-start = ((), (), s32[]{:S(2)}) async-start(), calls=%async_computation.26 | async-start | bytes 1114112 | tf_op jit(solution)/shard_map/all_gather | solution.py:50
  13.7 237.9 %all-gather.29.cloned.1.call-start = ((), (), s32[]{:S(2)}) async-start(), calls=%async_computation.28 | async-start | bytes 4456448 | tf_op jit(solution)/shard_map/all_gather | solution.py:50
  15.5 295.5 %all-gather.33.cloned.1.call-start = ((), (), s32[]{:S(2)}) async-start(), calls=%async_computation.30 | async-start | bytes 4456448 | tf_op jit(solution)/shard_map/all_gather | solution.py:50
  17.4 346.1 %all-gather.15.cloned.1.call-start = ((), (), s32[]{:S(2)}) async-start(), calls=%async_computation.21 | async-start | bytes 9437184 | tf_op jit(solution)/shard_map/all_gather | solution.py:51
  55.8 359.3 %all-gather.19.cloned.1.call-start = ((), (), s32[]{:S(2)}) async-start(), calls=%async_computation.23 | async-start | bytes 9437184 | tf_op jit(solution)/shard_map/all_gather | solution.py:51
  101.2 365.7 %all-gather.23.cloned.1.call-start = ((), (), s32[]{:S(2)}) async-start(), calls=%async_computation.25 | async-start | bytes 9437184 | tf_op jit(solution)/shard_map/all_gather | solution.py:51
  146.5 408.9 %all-gather.27.cloned.1.call-start = ((), (), s32[]{:S(2)}) async-start(), calls=%async_computation.27 | async-start | bytes 9437184 | tf_op jit(solution)/shard_map/all_gather | solution.py:51
  191.7 484.5 %all-gather.31.cloned.1.call-start = ((), (), s32[]{:S(2)}) async-start(), calls=%async_computation.29 | async-start | bytes 37748736 | tf_op jit(solution)/shard_map/all_gather | solution.py:51
  251.6 59.4 %copy-start.8 = (bf16[2,64,2048]{2,1,0:T(8,128)(2,1)S(1)}, bf16[2,64,2048]{2,1,0:T(8,128)(2,1)}, u32[]{:S(2)}) copy-start(bf16[2,64,2048]{2,1,0:T(8,128)(2,1)} %param.24) | copy-start | bytes 1572868
  251.6 60.1 %copy-start.43 = (f32[2048]{0:T(1024)S(1)}, f32[2048]{0:T(1024)}, u32[]{:S(2)}) copy-start(f32[2048]{0:T(1024)} %param.29) | copy-start | bytes 24580
  251.6 60.1 %copy-start.47 = (f32[2048]{0:T(1024)S(1)}, f32[2048]{0:T(1024)}, u32[]{:S(2)}) copy-start(f32[2048]{0:T(1024)} %param.30) | copy-start | bytes 24580
  251.6 111.8 %copy-start.53 = (f32[2048]{0:T(1024)S(1)}, f32[2048]{0:T(1024)}, u32[]{:S(2)}) copy-start(f32[2048]{0:T(1024)} %param.35) | copy-start | bytes 24580
  251.6 583.1 %all-gather.35.cloned.1.call-start = ((), (), s32[]{:S(2)}) async-start(), calls=%async_computation.31 | async-start | bytes 37748736 | tf_op jit(solution)/shard_map/all_gather | solution.py:51
  368.1 47.1 %copy-start.54 = (f32[2048]{0:T(1024)S(1)}, f32[2048]{0:T(1024)}, u32[]{:S(2)}) copy-start(f32[2048]{0:T(1024)} %param.32) | copy-start | bytes 24580
  370.4 51.7 %all-to-all-start = ((bf16[16,2,8192]{2,1,0:T(2,128)(2,1)}), bf16[16,2,8192]{2,1,0:T(2,128)(2,1)S(1)}, u32[]{:S(2)}, u32[]{:S(2)}) async-start(bf16[16,2,8192]{2,1,0:T(2,128)(2,1)} %reshape.510), calls=%async_computation | async-start | bytes 1048576 | tf_op jit(solution)/shard_map/all_to_all | solution.py:201
  422.1 51.7 %all-to-all-start.1 = ((bf16[16,2,8192]{2,1,0:T(2,128)(2,1)}), bf16[16,2,8192]{2,1,0:T(2,128)(2,1)S(1)}, u32[]{:S(2)}, u32[]{:S(2)}) async-start(bf16[16,2,8192]{2,1,0:T(2,128)(2,1)} %reshape.512), calls=%async_computation.1 | async-start | bytes 1048576 | tf_op jit(solution)/shard_map/all_to_all | solution.py:187
  473.8 17.3 all-to-all-start.2
  493.6 52.8 %copy-start.20 = (bf16[2,64,2048]{2,1,0:T(8,128)(2,1)S(1)}, bf16[2,64,2048]{2,1,0:T(8,128)(2,1)}, u32[]{:S(2)}) copy-start(bf16[2,64,2048]{2,1,0:T(8,128)(2,1)} %param.25) | copy-start | bytes 1572868
  541.8 13.1 all-to-all-start.3
  546.0 587.4 %reduce-scatter.43.cloned.1.call-start = ((), (), s32[]{:S(2)}) async-start(), calls=%async_computation.43 | async-start | bytes 8912896
  546.4 330.4 %copy-start.57 = (f32[128]{0:T(128)}, f32[128]{0:T(128)S(1)}, u32[]{:S(2)}) copy-start(f32[128]{0:T(128)S(1)} %reshape.499) | copy-start | bytes 1540
  555.4 120.8 %copy-start.39 = (f32[2048]{0:T(1024)S(1)}, f32[2048]{0:T(1024)}, u32[]{:S(2)}) copy-start(f32[2048]{0:T(1024)} %param.38) | copy-start | bytes 24580
  555.4 120.8 %copy-start.41 = (f32[2048]{0:T(1024)S(1)}, f32[2048]{0:T(1024)}, u32[]{:S(2)}) copy-start(f32[2048]{0:T(1024)} %param.39) | copy-start | bytes 24580
  555.4 120.8 %copy-start.50 = (f32[8192]{0:T(1024)S(1)}, f32[8192]{0:T(1024)}, u32[]{:S(2)}) copy-start(f32[8192]{0:T(1024)} %param.41) | copy-start | bytes 98308
  562.0 314.7 %copy-start.4 = (f32[128,2048]{1,0:T(8,128)}, f32[128,2048]{1,0:T(8,128)S(1)}, u32[]{:S(2)}) copy-start(f32[128,2048]{1,0:T(8,128)S(1)} %get-tuple-element.247) | copy-start | bytes 3145732
  562.0 314.7 %copy-start.45 = (f32[128]{0:T(128)}, f32[128]{0:T(128)S(1)}, u32[]{:S(2)}) copy-start(f32[128]{0:T(128)S(1)} %broadcast_multiply_fusion.5) | copy-start | bytes 1540
  562.3 314.5 %copy-start.48 = (f32[128]{0:T(128)}, f32[128]{0:T(128)S(1)}, u32[]{:S(2)}) copy-start(f32[128]{0:T(128)S(1)} %add_rsqrt_fusion.1) | copy-start | bytes 1540
  905.2 20.8 %all-to-all-start.4 = ((bf16[16,2,8192]{2,1,0:T(2,128)(2,1)}), bf16[16,2,8192]{2,1,0:T(2,128)(2,1)S(1)}, u32[]{:S(2)}, u32[]{:S(2)}) async-start(bf16[16,2,8192]{2,1,0:T(2,128)(2,1)} %reshape.516), calls=%async_computation.4 | async-start | bytes 1048576 | tf_op jit(solution)/shard_map/all_to_all | solution.py:236
  928.5 71.8 %copy-start.52 = (f32[2,64]{1,0:T(2,128)S(1)}, f32[2,64]{1,0:T(2,128)}, u32[]{:S(2)}) copy-start(f32[2,64]{1,0:T(2,128)} %copy-done.51) | copy-start | bytes 1540
  995.1 14.2 all-to-all-start.5
  1000.1 135.4 %reduce-scatter.37.cloned.1.call-start = ((), (), s32[]{:S(2)}) async-start(), calls=%async_computation.40 | async-start | bytes 8912896
  1029.4 175.5 %reduce-scatter.39.cloned.1.call-start = ((), (), s32[]{:S(2)}) async-start(), calls=%async_computation.41 | async-start | bytes 8912896
  1062.6 230.0 %reduce-scatter.41.cloned.1.call-start = ((), (), s32[]{:S(2)}) async-start(), calls=%async_computation.42 | async-start | bytes 8912896
  1099.5 391.9 %reduce-scatter.29.cloned.1.call-start = ((), (), s32[]{:S(2)}) async-start(), calls=%async_computation.36 | async-start | bytes 35651584 | tf_op jit(solution)/shard_map/reduce_scatter | solution.py:55
  1115.4 573.8 %reduce-scatter.33.cloned.1.call-start = ((), (), s32[]{:S(2)}) async-start(), calls=%async_computation.38 | async-start | bytes 35651584 | tf_op jit(solution)/shard_map/reduce_scatter | solution.py:55
  1133.3 592.9 %reduce-scatter.27.cloned.1.call-start = ((), (), s32[]{:S(2)}) async-start(), calls=%async_computation.35 | async-start | bytes 589824 | tf_op jit(solution)/shard_map/reduce_scatter | solution.py:58
  1133.4 358.1 %copy-start.65 = (f32[2,64]{1,0:T(2,128)S(1)}, f32[2,64]{1,0:T(2,128)}, u32[]{:S(2)}) copy-start(f32[2,64]{1,0:T(2,128)} %copy-done.64) | copy-start | bytes 1540
  1135.5 616.1 %reduce-scatter.21.cloned.1.call-start = ((), (), s32[]{:S(2)}) async-start(), calls=%async_computation.32 | async-start | bytes 589824 | tf_op jit(solution)/shard_map/reduce_scatter | solution.py:58
  1137.6 551.9 %copy-start.56 = (f32[2048]{0:T(1024)S(1)}, f32[2048]{0:T(1024)}, u32[]{:S(2)}) copy-start(f32[2048]{0:T(1024)} %param.43) | copy-start | bytes 24580
  1137.6 551.9 %copy-start.58 = (f32[128]{0:T(128)S(1)}, f32[128]{0:T(128)}, u32[]{:S(2)}) copy-start(f32[128]{0:T(128)} %copy-done.57) | copy-start | bytes 1540
  1137.7 646.1 %reduce-scatter.23.cloned.1.call-start = ((), (), s32[]{:S(2)}) async-start(), calls=%async_computation.33 | async-start | bytes 589824 | tf_op jit(solution)/shard_map/reduce_scatter | solution.py:58
  1206.9 609.2 %reduce-scatter.25.cloned.1.call-start = ((), (), s32[]{:S(2)}) async-start(), calls=%async_computation.34 | async-start | bytes 589824 | tf_op jit(solution)/shard_map/reduce_scatter | solution.py:58
  1294.7 556.1 %reduce-scatter.31.cloned.1.call-start = ((), (), s32[]{:S(2)}) async-start(), calls=%async_computation.37 | async-start | bytes 2359296 | tf_op jit(solution)/shard_map/reduce_scatter | solution.py:58
  1491.4 394.2 %reduce-scatter.35.cloned.1.call-start = ((), (), s32[]{:S(2)}) async-start(), calls=%async_computation.39 | async-start | bytes 2359296 | tf_op jit(solution)/shard_map/reduce_scatter | solution.py:58
  1689.2 348.9 %all-reduce.3.cloned.1.call-start = ((), (), s32[]{:S(2)}) async-start(), calls=%async_computation.44 | async-start | bytes 196608 | tf_op jit(solution)/shard_map/psum | solution.py:269
  (69 other events, 285.0 us)
Sparse Core Ops, SparseCore 0:
  10.7 45.0 all-gather.12
  58.5 42.6 all-gather.16
  103.8 42.6 all-gather.20
  149.0 42.6 all-gather.24
  194.2 57.3 all-gather.28
  254.1 56.8 all-gather.32
  312.7 50.6 all-gather.14
  365.1 49.9 all-gather.18
  416.9 49.9 all-gather.22
  468.4 49.9 all-gather.26
  520.1 156.0 all-gather.30
  677.7 156.9 all-gather.34
  898.4 88.3 reduce-scatter.42
  1029.5 87.6 reduce-scatter.36
  1120.4 84.3 reduce-scatter.38
  1208.1 84.4 reduce-scatter.40
  1296.0 195.3 reduce-scatter.28
  1494.8 194.3 reduce-scatter.32
  1691.6 27.7 reduce-scatter.26
  1721.7 29.7 reduce-scatter.20
  1753.9 29.7 reduce-scatter.22
  1786.3 29.7 reduce-scatter.24
  1818.5 32.2 reduce-scatter.30
  1853.1 32.4 reduce-scatter.34
  1893.7 144.4 all-reduce.2
where the time goes:
time: 2070 us; the launch traced here: 2060 us
  waiting for transfers between devices  1560 us (75%)
  matrix products  219 us (11%)
  local copies, waits for them, and re-layouts  149 us (7%)
  other arithmetic  48.7 us (2%)
  starting transfers between devices  38.1 us (2%)
  blocking collectives  27.9 us (1%)
    reduce_scatter x2, waiting for transfers between devices, settle(): lax.psum_scatter(gradient.astype(jnp.bfloat16), 'head', scatter_dimension...  393 us
    all_gather x6, waiting for transfers between devices, fetch(): return lax.all_gather(shard_piece, 'dp', axis=0, tiled=True)  383 us
    all_gather x6, waiting for transfers between devices, fetch(): shard_piece = lax.all_gather(shard_piece, 'head', axis=1, tiled=True)  293 us
    unnamed x29, waiting for transfers between devices  153 us
    reduce_scatter x6, waiting for transfers between devices, settle(): lax.psum_scatter(gradient.astype(jnp.bfloat16), 'dp', scatter_dimension=0...  152 us
    psum x1, waiting for transfers between devices, shards(): lax.psum((jnp.sum(g_norm1 * unit1, 0), jnp.sum(g_norm1, 0), q_bias_sum, v...  151 us
    unnamed x133, local copies, waits for them, and re-layouts  85.8 us
    dot_general x6, matrix products, product(): return jnp.dot(left_side, right_side, preferred_element_type=jnp.float32)  59.4 us
  transfers between devices with their start and end apart: 31, of which 25 were waited for; matrix products, arithmetic and copies ran while one was open for 16% of the time, Pallas kernels for 0%

commit v1 on v0

v1 whole, which is shorter than its diff:
```python
from functools import partial

import jax
import jax.numpy as jnp
from jax import lax
from jax.experimental import pallas as pl
from jax.experimental.pallas import tpu as pltpu
from jax.sharding import Mesh
from jax.sharding import PartitionSpec as P

HEAD_DIM = 64
SPAN = 256
LOW = jnp.bfloat16
WIDE = jnp.float32
RING = 4
ROWS = ("z", "c")
COLS = ("x", "y")


def dot(left, right):
    return jnp.dot(left, right, preferred_element_type=WIDE)


def dot_t(left, right):
    return lax.dot_general(left, right, (((1,), (1,)), ((), ())), preferred_element_type=WIDE)


def dot_0(left, right):
    return lax.dot_general(left, right, (((0,), (0,)), ((), ())), preferred_element_type=WIDE)


def call(body, out_shape, grid, in_specs, out_specs, flops, traffic, scratch=(), prefetch=0, vmem=40):
    return pl.pallas_call(
        body,
        out_shape=out_shape,
        grid_spec=pltpu.PrefetchScalarGridSpec(
            num_scalar_prefetch=prefetch,
            grid=grid,
            in_specs=in_specs,
            out_specs=out_specs,
            scratch_shapes=list(scratch),
        ),
        compiler_params=pltpu.CompilerParams(vmem_limit_bytes=vmem * 2**20),
        cost_estimate=pl.CostEstimate(flops=flops, bytes_accessed=traffic, transcendentals=0),
    )


def whole(shape):
    return pl.BlockSpec(shape, lambda *_: (0,) * len(shape))


def struct(shape, dtype):
    return jax.ShapeDtypeStruct(shape, dtype)


def spread(array, axes, size):
    return lax.all_to_all(jnp.broadcast_to(array[None], (size,) + array.shape), axes, 0, 0)


def collect(parts, axes):
    return jnp.sum(lax.all_to_all(parts, axes, 0, 0).astype(WIDE), 0)


def swap(parts, axes):
    return lax.all_to_all(parts, axes, 0, 0)


def gather_weight(shard):
    full = lax.all_gather(shard, ("z", "c", "x"), axis=0)
    return full.reshape((8, 4) + shard.shape)


def settle(gradient):
    total = lax.psum_scatter(
        gradient.reshape((32,) + gradient.shape[2:]), ("z", "c", "x"), scatter_dimension=0
    )
    return total.astype(WIDE)


def qkv_body(rows_ref, weight_ref, bias_ref, out_ref):
    weight = weight_ref[...].reshape(rows_ref.shape[1], -1)
    out_ref[...] = (dot(rows_ref[...], weight) + bias_ref[...]).astype(LOW)


def qkv_project(rows, weight, bias):
    count, width = rows.shape
    zc, xs, piece, cols = weight.shape
    return call(
        qkv_body,
        struct((xs, count, cols), LOW),
        (xs,),
        [
            whole((count, width)),
            pl.BlockSpec((zc, None, piece, cols), lambda i: (0, i, 0, 0)),
            pl.BlockSpec((None, 1, cols), lambda i: (i, 0, 0)),
        ],
        pl.BlockSpec((None, count, cols), lambda i: (i, 0, 0)),
        2 * count * width * xs * cols,
        10 * 2**20,
    )(rows, weight, bias)


def out_body(heads_ref, weight_ref, out_ref, joined):
    @pl.when(pl.program_id(0) == 0)
    def _():
        joined[...] = jnp.concatenate([heads_ref[i] for i in range(RING)], 1)

    weight = jnp.concatenate([weight_ref[i] for i in range(RING)], 1)
    out_ref[...] = dot_t(joined[...], weight).astype(LOW)


def out_project(heads, weight):
    xs, count, cols = heads.shape
    zc, _, piece, _ = weight.shape
    return call(
        out_body,
        struct((count, zc * piece), LOW),
        (zc,),
        [
            whole(heads.shape),
            pl.BlockSpec((None, xs, piece, cols), lambda i: (i, 0, 0, 0)),
        ],
        pl.BlockSpec((count, piece), lambda i: (0, i)),
        2 * count * zc * piece * xs * cols,
        5 * 2**20,
        scratch=[pltpu.VMEM((count, xs * cols), LOW)],
    )(heads, weight)


def heads_grad_body(rows_ref, weight_ref, out_ref):
    weight = weight_ref[...].reshape(rows_ref.shape[1], -1)
    out_ref[...] = dot(rows_ref[...], weight).astype(LOW)


def heads_grad(rows, weight):
    count, width = rows.shape
    zc, xs, piece, cols = weight.shape
    return call(
        heads_grad_body,
        struct((xs, count, cols), LOW),
        (xs,),
        [
            whole((count, width)),
            pl.BlockSpec((zc, None, piece, cols), lambda i: (0, i, 0, 0)),
        ],
        pl.BlockSpec((None, count, cols), lambda i: (i, 0, 0)),
        2 * count * width * xs * cols,
        5 * 2**20,
    )(rows, weight)


def out_weight_body(rows_ref, heads_ref, out_ref):
    out_ref[...] = dot_0(rows_ref[...], heads_ref[...]).astype(LOW).reshape(out_ref.shape)


def out_weight_grad(rows, heads):
    count, width = rows.shape
    xs, _, cols = heads.shape
    piece = width // 8
    return call(
        out_weight_body,
        struct((8, xs, piece, cols), LOW),
        (xs,),
        [whole((count, width)), pl.BlockSpec((None, count, cols), lambda i: (i, 0, 0))],
        pl.BlockSpec((8, None, piece, cols), lambda i: (0, i, 0, 0)),
        2 * count * width * xs * cols,
        5 * 2**20,
    )(rows, heads)


def qkv_grad_body(norm_ref, grad_ref, weight_ref, weight_grad_ref, norm_grad_ref, total):
    step = pl.program_id(0)
    grad = grad_ref[...]
    weight_grad_ref[...] = dot_0(norm_ref[...], grad).astype(LOW).reshape(weight_grad_ref.shape)
    term = dot_t(grad, weight_ref[...].reshape(norm_ref.shape[1], -1))

    @pl.when(step == 0)
    def _():
        total[...] = term

    @pl.when(step > 0)
    def _():
        total[...] += term

    @pl.when(step == RING - 1)
    def _():
        norm_grad_ref[...] = total[...].astype(LOW)


def qkv_grad(norm_rows, grads, weight):
    count, width = norm_rows.shape
    zc, xs, piece, cols = weight.shape
    block = pl.BlockSpec((zc, None, piece, cols), lambda i: (0, i, 0, 0))
    return call(
        qkv_grad_body,
        (struct(weight.shape, LOW), struct((count, width), LOW)),
        (xs,),
        [whole((count, width)), pl.BlockSpec((None, count, cols), lambda i: (i, 0, 0)), block],
        (block, whole((count, width))),
        4 * count * width * xs * cols,
        20 * 2**20,
        scratch=[pltpu.VMEM((count, width), WIDE)],
    )(norm_rows, grads, weight)


def ffn_body(
    norm_ref, cot_ref, up_ref, down_ref, bias_ref,
    branch_ref, norm_grad_ref, weight_grad_ref, bias_grad_ref,
    branch_total, norm_total,
):
    step = pl.program_id(0)
    width = norm_ref.shape[1]
    cols = up_ref.shape[-1]
    up_w = up_ref[...].reshape(width, cols)
    down_w = down_ref[...].reshape(width, cols)
    up = dot(norm_ref[...], up_w) + bias_ref[...]
    normal = 0.5 * (1.0 + lax.erf(up * 0.7071067811865476))
    hidden = (up * normal).astype(LOW)
    slope = normal + up * (jnp.exp(-0.5 * up * up) * 0.3989422804014327)
    grad_up = (dot(cot_ref[...], down_w) * slope).astype(LOW)
    branch = dot_t(hidden, down_w)
    norm_grad = dot_t(grad_up, up_w)

    @pl.when(step == 0)
    def _():
        branch_total[...] = branch
        norm_total[...] = norm_grad

    @pl.when(step > 0)
    def _():
        branch_total[...] += branch
        norm_total[...] += norm_grad

    half = step % 2
    size = weight_grad_ref.shape[-1] // 4
    zc, piece, _ = weight_grad_ref.shape
    weight_grad_ref[:, :, pl.ds(pl.multiple_of(half * size, size), size)] = (
        dot_0(norm_ref[...], grad_up).astype(LOW).reshape(zc, piece, cols)
    )
    weight_grad_ref[:, :, pl.ds(pl.multiple_of((half + 2) * size, size), size)] = (
        dot_0(cot_ref[...], hidden).astype(LOW).reshape(zc, piece, cols)
    )
    bias_grad_ref[...] = jnp.sum(grad_up.astype(WIDE), 0, keepdims=True)

    @pl.when(step == pl.num_programs(0) - 1)
    def _():
        branch_ref[...] = branch_total[...].astype(LOW)
        norm_grad_ref[...] = norm_total[...].astype(LOW)


def feed_forward(norm_rows, cot_rows, weight, bias):
    count, width = norm_rows.shape
    zc, xs, piece, cols = weight.shape
    size = cols // 4
    steps = 2 * xs
    return call(
        ffn_body,
        (
            struct((count, width), LOW),
            struct((count, width), LOW),
            struct(weight.shape, LOW),
            struct((steps, 1, size), WIDE),
        ),
        (steps,),
        [
            whole((count, width)),
            whole((count, width)),
            pl.BlockSpec((zc, None, piece, size), lambda i: (0, i // 2, 0, i % 2)),
            pl.BlockSpec((zc, None, piece, size), lambda i: (0, i // 2, 0, 2 + i % 2)),
            pl.BlockSpec((None, 1, size), lambda i: (i, 0, 0)),
        ],
        (
            whole((count, width)),
            whole((count, width)),
            pl.BlockSpec((zc, None, piece, cols), lambda i: (0, i // 2, 0, 0)),
            pl.BlockSpec((None, 1, size), lambda i: (i, 0, 0)),
        ),
        12 * count * width * steps * size,
        40 * 2**20,
        scratch=[pltpu.VMEM((count, width), WIDE), pltpu.VMEM((count, width), WIDE)],
        vmem=56,
    )(norm_rows, cot_rows, weight, weight, bias)


def only_head(array, head):
    lane = lax.broadcasted_iota(jnp.int32, array.shape, 1)
    return jnp.where(lane // HEAD_DIM == head, array, jnp.zeros_like(array))


def allowed_keys(start, extent, live_count):
    q_place = start + lax.broadcasted_iota(jnp.int32, (SPAN, extent), 0)
    k_place = lax.broadcasted_iota(jnp.int32, (SPAN, extent), 1)
    return k_place <= jnp.minimum(q_place, live_count - 1)


def attend_body(live_ref, qkv_ref, heads_ref, exact_ref, log_ref):
    live_count = live_ref[pl.program_id(0)]
    length = exact_ref.shape[0]
    width = exact_ref.shape[1]
    qkv = qkv_ref[...].reshape(length, 3 * width)
    key = qkv[:, width : 2 * width]
    value = qkv[:, 2 * width :]
    per_x = SPAN // heads_ref.shape[2]
    for span in range(length // SPAN):
        start, extent = span * SPAN, (span + 1) * SPAN
        here = slice(start, extent)

        @pl.when(start < live_count)
        def _():
            query = qkv[here, :width]
            allowed = allowed_keys(start, extent, live_count)
            mixed, logs = [], []
            for head in range(width // HEAD_DIM):
                scores = dot_t(only_head(query, head), key[:extent]) * HEAD_DIM**-0.5
                scores = jnp.where(allowed, scores, -1e9)
                top = jnp.max(scores, 1, keepdims=True)
                terms = jnp.exp(scores - top)
                denom = jnp.sum(terms, 1, keepdims=True)
                mixed.append(dot(terms.astype(LOW), value[:extent]) / denom)
                logs.append(top + jnp.log(denom))
            lane = lax.broadcasted_iota(jnp.int32, (SPAN, width), 1)
            out = jnp.where(lane < HEAD_DIM, mixed[0], mixed[1])
            exact_ref[here] = out
            log_ref[here] = jnp.where(lane < HEAD_DIM, logs[0], logs[1])
            heads_ref[span] = out.astype(LOW).reshape(heads_ref.shape[1:])

        @pl.when(start >= live_count)
        def _():
            exact_ref[here] = jnp.zeros((SPAN, width), WIDE)
            log_ref[here] = jnp.zeros((SPAN, width), WIDE)
            heads_ref[span] = jnp.zeros(heads_ref.shape[1:], LOW)


def row_block(rows, cols):
    return pl.BlockSpec((4, 4, None, rows, cols), lambda s, *_: (0, 0, s, 0, 0))


def attend(live_counts, qkv, width):
    xs, ys, seqs, rows, _ = qkv.shape
    length = xs * ys * rows
    flat = pl.BlockSpec((None, length, width), lambda s, *_: (s, 0, 0))
    return call(
        attend_body,
        (
            struct((xs, ys, seqs, rows, width), LOW),
            struct((seqs, length, width), WIDE),
            struct((seqs, length, width), WIDE),
        ),
        (seqs,),
        [row_block(rows, 3 * width)],
        (row_block(rows, width), flat, flat),
        4 * 10**9,
        4 * 2**20,
        prefetch=1,
    )(live_counts, qkv)


def attend_back_body(
    live_ref, qkv_ref, grad_ref, exact_ref, log_ref, out_ref, sum_ref, key_total, value_total
):
    live_count = live_ref[pl.program_id(0)]
    length, width = exact_ref.shape
    factor = HEAD_DIM**-0.5
    qkv = qkv_ref[...].reshape(length, 3 * width)
    grads = grad_ref[...].reshape(length, width)
    key = qkv[:, width : 2 * width]
    value = qkv[:, 2 * width :]
    key_total[...] = jnp.zeros_like(key_total)
    value_total[...] = jnp.zeros_like(value_total)
    sum_ref[...] = jnp.zeros_like(sum_ref)
    piece = out_ref.shape[1:3]
    for span in range(length // SPAN):
        start, extent = span * SPAN, (span + 1) * SPAN
        here = slice(start, extent)

        @pl.when(start < live_count)
        def _():
            query = qkv[here, :width]
            grad = grads[here]
            inner = grad.astype(WIDE) * exact_ref[here]
            logs = log_ref[here]
            allowed = allowed_keys(start, extent, live_count)
            query_total = jnp.zeros((SPAN, width), WIDE)
            for head in range(width // HEAD_DIM):
                query_h = only_head(query, head)
                grad_h = only_head(grad, head)
                log_h = logs[:, head * HEAD_DIM : head * HEAD_DIM + 1]
                row_inner = jnp.sum(only_head(inner, head), 1, keepdims=True)
                scores = dot_t(query_h, key[:extent]) * factor
                probs = jnp.exp(jnp.where(allowed, scores, -1e9) - log_h)
                d_probs = dot_t(grad_h, value[:extent])
                value_total[:extent] += dot_0(probs.astype(LOW), grad_h)
                d_scores = (probs * (d_probs - row_inner)).astype(LOW)
                query_total += dot(d_scores, only_head(key[:extent], head))
                key_total[:extent] += dot_0(d_scores, query_h)
            out = (query_total * factor).astype(LOW)
            out_ref[span, :, :, :width] = out.reshape(piece + (width,))
            sum_ref[:, :width] += jnp.sum(out.astype(WIDE), 0, keepdims=True)

        @pl.when(start >= live_count)
        def _():
            out_ref[span, :, :, :width] = jnp.zeros(piece + (width,), LOW)

    whole_shape = out_ref.shape[:3] + (width,)
    out_ref[:, :, :, width : 2 * width] = (
        (key_total[...] * factor).astype(LOW).reshape(whole_shape)
    )
    out = value_total[...].astype(LOW)
    out_ref[:, :, :, 2 * width :] = out.reshape(whole_shape)
    sum_ref[:, 2 * width :] = jnp.sum(out.astype(WIDE), 0, keepdims=True)


def attend_back(live_counts, qkv, grads, exact, logs):
    xs, ys, seqs, rows, _ = qkv.shape
    _, length, width = exact.shape
    flat = pl.BlockSpec((None, length, width), lambda s, *_: (s, 0, 0))
    return call(
        attend_back_body,
        (struct(qkv.shape, LOW), struct((seqs, 1, 3 * width), WIDE)),
        (seqs,),
        [row_block(rows, 3 * width), row_block(rows, width), flat, flat],
        (
            row_block(rows, 3 * width),
            pl.BlockSpec((None, 1, 3 * width), lambda s, *_: (s, 0, 0)),
        ),
        8 * 10**9,
        8 * 2**20,
        scratch=[pltpu.VMEM((length, width), WIDE), pltpu.VMEM((length, width), WIDE)],
        prefetch=1,
        vmem=48,
    )(live_counts, qkv, grads, exact, logs)


def norm_parts(values, gain_vec, shift_vec):
    average = jnp.mean(values, -1, keepdims=True)
    centered = values - average
    inverse = lax.rsqrt(jnp.mean(centered * centered, -1, keepdims=True) + 1e-05)
    unit_rows = centered * inverse
    return (unit_rows * gain_vec + shift_vec, unit_rows, inverse)


def norm_back(gradient, unit_rows, inverse, gain_vec):
    scaled = gradient * gain_vec
    return inverse * (
        scaled
        - jnp.mean(scaled, -1, keepdims=True)
        - unit_rows * jnp.mean(scaled * unit_rows, -1, keepdims=True)
    )


def vector_totals(vectors):
    flat = jnp.concatenate([v.reshape(-1) for v in vectors])
    part = collect(flat.reshape(16, -1, 128), COLS)
    part = jnp.sum(spread(part, ROWS, 8), 0)
    flat = spread(part, COLS, 16).reshape(-1)
    totals, start = [], 0
    for v in vectors:
        totals.append(flat[start : start + v.size])
        start += v.size
    return totals


def shards(
    tokens, cotangent, seq_lengths, exit_layers, layer_index,
    ln1_gain, ln1_shift, q_weight, q_bias, k_weight, v_weight, v_bias, out_weight, out_bias,
    ln2_gain, ln2_shift, up_weight, up_bias, down_weight, down_bias,
):
    seqs, own_rows, width = tokens.shape
    own = seqs * own_rows
    full_len = exit_layers.shape[1]
    x_at, y_at = lax.axis_index("x"), lax.axis_index("y")
    head_at = x_at * RING + y_at
    head_cols = q_weight.shape[1]
    ff_cols = up_weight.shape[1]

    positions = jnp.arange(full_len)
    live_all = (positions[None, :] < seq_lengths[:, None]) & (exit_layers > layer_index[0])
    live_counts = jnp.sum(live_all.astype(jnp.int32), 1)
    live_mine = lax.dynamic_slice_in_dim(live_all, head_at * own_rows, own_rows, 1)
    keep = live_mine.reshape(-1, 1).astype(WIDE)

    w_qkv = gather_weight(jnp.concatenate([q_weight, k_weight, v_weight], 1).astype(LOW))
    w_out = gather_weight(out_weight.astype(LOW))
    w_ff = gather_weight(jnp.concatenate([up_weight, down_weight], 1).astype(LOW))

    inputs = tokens.astype(WIDE).reshape(own, width)
    normed1, unit1, inverse1 = norm_parts(inputs, ln1_gain, ln1_shift)
    norm1 = spread(normed1.astype(LOW), "y", RING).reshape(RING * own, width)
    grad_y = cotangent.astype(WIDE).reshape(own, width)
    g_ffn = (keep * grad_y).astype(LOW)
    cot_rows = spread(g_ffn, "y", RING).reshape(RING * own, width)

    def mine(vector, cols):
        return lax.dynamic_index_in_dim(vector.reshape(RING, RING, cols), y_at, 1, False)

    bias = jnp.concatenate(
        [mine(q_bias, head_cols), jnp.zeros((RING, head_cols), WIDE), mine(v_bias, head_cols)], 1
    ).reshape(RING, 1, 3 * head_cols)
    qkv = qkv_project(norm1, w_qkv, bias)
    rows5 = (RING, RING, seqs, own_rows)
    qkv = swap(qkv, "x").reshape(rows5 + (3 * head_cols,))
    heads, exact, logs = attend(live_counts, qkv, head_cols)
    heads = swap(heads.reshape(RING, RING * own, head_cols), "x")
    branch1 = collect(out_project(heads, w_out).reshape(RING, own, width), "y") + out_bias
    middle = inputs + keep * branch1
    normed2, unit2, inverse2 = norm_parts(middle, ln2_gain, ln2_shift)
    norm2 = spread(normed2.astype(LOW), "y", RING).reshape(RING * own, width)

    ff_bias = mine(up_bias, ff_cols).reshape(2 * RING, 1, ff_cols // 2)
    branch2, g_norm2, ff_grad, up_bias_part = feed_forward(norm2, cot_rows, w_ff, ff_bias)
    g_norm2 = collect(g_norm2.reshape(RING, own, width), "y")
    ff_grad = settle(ff_grad)
    grad_mid = grad_y + norm_back(g_norm2, unit2, inverse2, ln2_gain)
    g_attn = (keep * grad_mid).astype(LOW)
    attn_rows = spread(g_attn, "y", RING).reshape(RING * own, width)
    g_heads = swap(heads_grad(attn_rows, w_out), "x").reshape(rows5 + (head_cols,))
    out_grad = settle(out_weight_grad(attn_rows, heads))
    d_qkv, d_sums = attend_back(live_counts, qkv, g_heads, exact, logs)
    d_qkv = swap(d_qkv.reshape(RING, RING * own, 3 * head_cols), "x")
    qkv_weight_grad, g_norm1 = qkv_grad(norm1, d_qkv, w_qkv)
    qkv_weight_grad = settle(qkv_weight_grad)
    g_norm1 = collect(g_norm1.reshape(RING, own, width), "y")
    grad_tokens = (grad_mid + norm_back(g_norm1, unit1, inverse1, ln1_gain)).reshape(tokens.shape)

    branch2 = collect(branch2.reshape(RING, own, width), "y") + down_bias
    result = (middle + keep * branch2).astype(LOW).reshape(tokens.shape)

    d_sums = jnp.sum(d_sums, 0).reshape(3, head_cols)

    def placed(row):
        blank = jnp.zeros((RING * RING, head_cols), WIDE)
        return lax.dynamic_update_slice_in_dim(blank, row[None], head_at, 0)

    up_bias_full = lax.dynamic_update_slice_in_dim(
        jnp.zeros((RING, RING, ff_cols), WIDE), up_bias_part.reshape(RING, 1, ff_cols), y_at, 1
    )
    totals = vector_totals(
        (
            jnp.sum(g_norm1 * unit1, 0),
            jnp.sum(g_norm1, 0),
            placed(d_sums[0]),
            placed(d_sums[2]),
            jnp.sum(g_attn.astype(WIDE), 0),
            jnp.sum(g_norm2 * unit2, 0),
            jnp.sum(g_norm2, 0),
            up_bias_full,
            jnp.sum(g_ffn.astype(WIDE), 0),
        )
    )
    return (
        result,
        grad_tokens,
        totals[0],
        totals[1],
        qkv_weight_grad[:, :head_cols],
        totals[2],
        qkv_weight_grad[:, head_cols : 2 * head_cols],
        qkv_weight_grad[:, 2 * head_cols :],
        totals[3],
        out_grad,
        totals[4],
        totals[5],
        totals[6],
        ff_grad[:, :ff_cols],
        totals[7],
        ff_grad[:, ff_cols:],
        totals[8],
    )


def solution(mesh):
    wide = Mesh(mesh.devices.reshape(4, 2, 4, 4), ("z", "c", "x", "y"))
    act = P(ROWS, COLS, None)
    weight = P(ROWS, COLS)
    vector = P()
    in_specs = (
        act, act, P(ROWS), P(ROWS, None), vector, vector, vector,
        weight, vector, weight, weight, vector, weight, vector, vector, vector,
        weight, vector, weight, vector,
    )
    out_specs = (
        act, act, vector, vector, weight, vector, weight, weight, vector, weight,
        vector, vector, vector, weight, vector, weight, vector,
    )
    return jax.shard_map(
        shards, mesh=wide, in_specs=in_specs, out_specs=out_specs, check_vma=False
    )
```

time: 2070 us -> 622 us (0.30)
  waiting for transfers between devices: 1560 us -> 269 us
  matrix products: 219 us -> 0 us
  blocking collectives: 27.9 us -> 161 us
  local copies, waits for them, and re-layouts: 149 us -> 24.9 us
  Pallas kernels: 0 us -> 93.3 us
  other arithmetic: 48.7 us -> 25.5 us
    all_gather x12 -> x3, waiting for transfers between devices: 676 us -> 16.9 us  [gather_weight(): full = lax.all_gather(shard, ('z', 'c', 'x'), axis=0)]
    reduce_scatter x8 -> x3, waiting for transfers between devices: 544 us -> 134 us  [settle(): lax.psum_scatter(gradient.reshape((32,) + gradient.shape[2:]), ('z', 'c',...]
    dot_general x46 -> x0, matrix products: 219 us -> none  [the longest x6 59.4 us: product(): return jnp.dot(left_side, right_side, preferred_element_type=jnp.float32)]
    unnamed x29 -> x6, waiting for transfers between devices: 153 us -> 0.6 us
    psum x1 -> x0, waiting for transfers between devices: 151 us -> none  [shards(): lax.psum((jnp.sum(g_norm1 * unit1, 0), jnp.sum(g_norm1, 0), q_bias_sum, v...]
    all_to_all x2 -> x8, blocking collectives: 27.9 us -> 161 us  [the longest x3 80.8 us: spread(): lax.all_to_all(jnp.broadcast_to(array[None], (size,) + array.shape), axes...]
    pallas_call x0 -> x8, Pallas kernels: none -> 93.3 us  [the longest x1 45.2 us: feed_forward(): call(ffn_body, (struct((count, width), LOW), struct((count, width), LOW),...]
    all_to_all x6 -> x7, waiting for transfers between devices: 33.5 us -> 118 us  [the longest x3 51.1 us: spread(): lax.all_to_all(jnp.broadcast_to(array[None], (size,) + array.shape), axes...]
  transfers between devices with their start and end apart: 31 -> 13, of which waited for: 25 -> 10; matrix products, arithmetic and copies ran while one was open for 16% -> 4% of each run, Pallas kernels for 0% -> 7%
where the time goes in v1:
time: 622 us; the launch traced here: 620 us
  waiting for transfers between devices  269 us (43%)
  blocking collectives  161 us (26%)
  Pallas kernels  93.3 us (15%)
  starting transfers between devices  30 us (5%)
  other arithmetic  25.5 us (4%)
  local copies, waits for them, and re-layouts  24.9 us (4%)
  between operations  15.3 us (2%)
    reduce_scatter x3, waiting for transfers between devices, settle(): lax.psum_scatter(gradient.reshape((32,) + gradient.shape[2:]), ('z', 'c',...  134 us
    all_to_all x3, blocking collectives, spread(): lax.all_to_all(jnp.broadcast_to(array[None], (size,) + array.shape), axes...  80.8 us
    all_to_all x3, blocking collectives, collect(): return jnp.sum(lax.all_to_all(parts, axes, 0, 0).astype(WIDE), 0)  53.7 us
    all_to_all x3, waiting for transfers between devices, spread(): lax.all_to_all(jnp.broadcast_to(array[None], (size,) + array.shape), axes...  51.1 us
    pallas_call x1, Pallas kernels, feed_forward(): call(ffn_body, (struct((count, width), LOW), struct((count, width), LOW),...  45.2 us
    all_to_all x2, waiting for transfers between devices, collect(): return jnp.sum(lax.all_to_all(parts, axes, 0, 0).astype(WIDE), 0)  38.5 us
    all_to_all x2, waiting for transfers between devices, swap(): return lax.all_to_all(parts, axes, 0, 0)  28.4 us
    all_to_all x2, blocking collectives, swap(): return lax.all_to_all(parts, axes, 0, 0)  26.9 us
  transfers between devices with their start and end apart: 13, of which 10 were waited for; matrix products, arithmetic and copies ran while one was open for 4% of the time, Pallas kernels for 7%

profile of v1, /device:TPU:1, one launch (start us, length us, event | category | flops | bytes accessed | tf_op | source)
XLA Modules:
  0.0 619.7 jit_solution(2474899550330709524)
XLA Ops:
  9.9 1.5 convert_element_type.122
  14.8 1.6 broadcast_in_dim.16
  16.4 5.0 all-to-all-start
  22.2 24.7 %all-to-all-done = bf16[4,128,2048]{2,1,0:T(8,128)(2,1)S(1)} async-done(((bf16[4,128,2048]{2,1,0:T(8,128)(2,1)}), bf16[4,128,2048]{2,1,0:T(8,128)(2,1)S(1)}, u32[]{:S(2)}, u32[]{:S(2)}) %all-to-all-start) | async-done | bytes 2097184 | tf_op jit(solution)/shard_map/all_to_all | solution.py:57
  46.8 16.9 %all-gather.5.cloned.1.call-done = bf16[32,256,384]{2,1,0:T(8,128)(2,1)} async-done(((bf16[1,256,384]{2,1,0:T(8,128)(2,1)}), bf16[32,256,384]{2,1,0:T(8,128)(2,1)}) %all-gather.5.cloned.1.call-update) | async-done | bytes 6291472 | tf_op jit(solution)/shard_map/all_gather | solution.py:69
  63.8 2.8 copy-done.9
  66.5 5.7 shard_map.323
  73.4 3.7 all-to-all-start.1
  78.0 20.4 %all-to-all-done.1 = bf16[4,512,384]{2,1,0:T(8,128)(2,1)S(1)} async-done(((bf16[4,512,384]{2,1,0:T(8,128)(2,1)}), bf16[4,512,384]{2,1,0:T(8,128)(2,1)S(1)}, u32[]{:S(2)}, u32[]{:S(2)}) %all-to-all-start.1) | async-done | bytes 1572896 | tf_op jit(solution)/shard_map/all_to_all | solution.py:65
  98.4 7.0 %shard_map.324 = (bf16[4,4,2,64,128]{4,3,2,1,0:T(8,128)(2,1)}, f32[2,1024,128]{2,1,0:T(8,128)S(1)}, f32[2,1024,128]{2,1,0:T(8,128)S(1)}) custom-call(s32[2]{0:T(128)S(1)} %get-tuple-element.50.live_ref, bf16[4,4,2,64,384]{4,3,2,1,0:T(8,128)(2,1)S(1)} %bitcast.100), custom_call_target="tpu_custom_call" | custom-call | flops 4000000000 | bytes 4194304 | tf_op jit(solution)/shard_map/pallas_call | solution.py:342
  107.3 3.5 all-to-all-start.2
  110.9 8.0 %all-to-all-done.2.heads_ref = bf16[4,512,128]{2,1,0:T(8,128)(2,1)S(1)} async-done(((bf16[4,512,128]{2,1,0:T(8,128)(2,1)}), bf16[4,512,128]{2,1,0:T(8,128)(2,1)S(1)}, u32[]{:S(2)}, u32[]{:S(2)}) %all-to-all-start.2) | async-done | bytes 524320 | tf_op jit(solution)/shard_map/all_to_all | solution.py:65
  118.9 1.6 copy-done
  120.5 4.7 shard_map.325
  125.1 4.5 all-to-all-start.3
  129.8 23.7 %all-to-all-done.3 = bf16[4,128,2048]{2,1,0:T(8,128)(2,1)} async-done(((bf16[4,128,2048]{2,1,0:T(8,128)(2,1)}), bf16[4,128,2048]{2,1,0:T(8,128)(2,1)}, u32[]{:S(2)}, u32[]{:S(2)}) %all-to-all-start.3) | async-done | bytes 2097184 | tf_op jit(solution)/shard_map/all_to_all | solution.py:61
  153.5 2.1 convert_reduce_fusion.5
  156.4 1.6 fusion.1
  158.2 25.9 %all_to_all.75 = bf16[4,128,2048]{2,1,0:T(8,128)(2,1)} all-to-all(bf16[4,128,2048]{2,1,0:T(8,128)(2,1)S(1)} %broadcast_in_dim.18), channel_id=1, replica_groups=mesh['z'=4,'c'=2,'x'=4,'y'=4] {'y'}, dimensions={0} | all-to-all | bytes 4194304 | tf_op jit(solution)/shard_map/all_to_all | solution.py:57
  184.1 1.6 broadcast_in_dim.19
  185.7 4.6 all-to-all-start.5
  191.1 20.9 %all-to-all-done.5 = bf16[4,128,2048]{2,1,0:T(8,128)(2,1)} async-done(((bf16[4,128,2048]{2,1,0:T(8,128)(2,1)}), bf16[4,128,2048]{2,1,0:T(8,128)(2,1)}, u32[]{:S(2)}, u32[]{:S(2)}) %all-to-all-start.5) | async-done | bytes 2097184 | tf_op jit(solution)/shard_map/all_to_all | solution.py:57
  212.0 45.2 %shard_map.326 = (bf16[512,2048]{1,0:T(8,128)(2,1)}, bf16[512,2048]{1,0:T(8,128)(2,1)}, bf16[8,4,256,1024]{3,2,1,0:T(8,128)(2,1)}, f32[8,1,256]{2,1,0:T(1,128)}) custom-call(bf16[512,2048]{1,0:T(8,128)(2,1)} %bitcast.111, bf16[512,2048]{1,0:T(8,128)(2,1)} %bitcast.18.cot_ref, bf16[8,4,256,1024]{3,2,1,0:T(8,128)(2,1)} %bitcast.121, ...), custom_call_target="tpu_custom_call" | custom-call | flops 25769803776 | bytes 41943040 | tf_op jit(solution)/shard_map/pallas_call | solution.py:256
  257.2 24.1 %all_to_all.76 = bf16[4,128,2048]{2,1,0:T(8,128)(2,1)S(1)} all-to-all(bf16[4,128,2048]{2,1,0:T(8,128)(2,1)} %bitcast.112), channel_id=1, replica_groups=mesh['z'=4,'c'=2,'x'=4,'y'=4] {'y'}, dimensions={0} | all-to-all | bytes 4194304 | tf_op jit(solution)/shard_map/all_to_all | solution.py:61
  282.9 1.8 fusion.3
  284.9 22.0 %all_to_all.77 = bf16[4,128,2048]{2,1,0:T(8,128)(2,1)S(1)} all-to-all(bf16[4,128,2048]{2,1,0:T(8,128)(2,1)S(1)} %broadcast_in_dim.20), channel_id=1, replica_groups=mesh['z'=4,'c'=2,'x'=4,'y'=4] {'y'}, dimensions={0} | all-to-all | bytes 4194304 | tf_op jit(solution)/shard_map/all_to_all | solution.py:57
  307.0 3.3 shard_map.330
  310.3 1.3 copy-done.2
  311.8 1.6 copy-done.1
  313.3 3.1 shard_map.327
  316.4 11.8 %all_to_all.78 = bf16[4,512,128]{2,1,0:T(8,128)(2,1)S(1)} all-to-all(bf16[4,512,128]{2,1,0:T(8,128)(2,1)S(1)} %shard_map.327), channel_id=1, replica_groups=mesh['z'=4,'c'=2,'x'=4,'y'=4] {'x'}, dimensions={0} | all-to-all | bytes 1048576 | tf_op jit(solution)/shard_map/all_to_all | solution.py:65
  328.2 9.8 %shard_map.328 = (bf16[4,4,2,64,384]{4,3,2,1,0:T(8,128)(2,1)S(1)}, f32[2,1,384]{2,1,0:T(1,128)S(1)}) custom-call(s32[2]{0:T(128)S(1)} %get-tuple-element.50.live_ref, bf16[4,4,2,64,384]{4,3,2,1,0:T(8,128)(2,1)S(1)} %bitcast.101, bf16[4,4,2,64,128]{4,3,2,1,0:T(8,128)(2,1)S(1)} %bitcast.103, f32[2,1024,128]{2,1,0:T(8,128)S(1)} %copy-done.11, ...), custom_call_target="tpu_custom_call" | custom-call | flops 8000000000 | bytes 8388608 | tf_op jit(solution)/shard_map/pallas_call | solution.py:417
  338.0 15.1 %all_to_all.79.grad_ref = bf16[4,512,384]{2,1,0:T(8,128)(2,1)S(1)} all-to-all(bf16[4,512,384]{2,1,0:T(8,128)(2,1)S(1)} %bitcast.102), channel_id=1, replica_groups=mesh['z'=4,'c'=2,'x'=4,'y'=4] {'x'}, dimensions={0} | all-to-all | bytes 3145728 | tf_op jit(solution)/shard_map/all_to_all | solution.py:65
  353.2 14.6 %shard_map.329 = (bf16[8,4,256,384]{3,2,1,0:T(8,128)(2,1)S(1)}, bf16[512,2048]{1,0:T(8,128)(2,1)}) custom-call(bf16[512,2048]{1,0:T(8,128)(2,1)S(1)} %bitcast.99, bf16[4,512,384]{2,1,0:T(8,128)(2,1)S(1)} %all_to_all.79.grad_ref, bf16[8,4,256,384]{3,2,1,0:T(8,128)(2,1)} %bitcast.104), custom_call_target="tpu_custom_call" | custom-call | flops 6442450944 | bytes 20971520 | tf_op jit(solution)/shard_map/pallas_call | solution.py:194
  367.8 2.6 copy-done.3
  371.0 20.4 %all_to_all.80 = bf16[4,128,2048]{2,1,0:T(8,128)(2,1)S(1)} all-to-all(bf16[4,128,2048]{2,1,0:T(8,128)(2,1)} %bitcast.110), channel_id=1, replica_groups=mesh['z'=4,'c'=2,'x'=4,'y'=4] {'y'}, dimensions={0} | all-to-all | bytes 4194304 | tf_op jit(solution)/shard_map/all_to_all | solution.py:61
  391.4 4.6 all-to-all-start.11
  396.3 1.4 convert_reduce_fusion.4
  398.0 14.8 %all-to-all-done.11 = bf16[4,128,2048]{2,1,0:T(8,128)(2,1)} async-done(((bf16[4,128,2048]{2,1,0:T(8,128)(2,1)}), bf16[4,128,2048]{2,1,0:T(8,128)(2,1)}, u32[]{:S(2)}, u32[]{:S(2)}) %all-to-all-start.11) | async-done | bytes 2097184 | tf_op jit(solution)/shard_map/all_to_all | solution.py:61
  412.9 2.6 convert_reduce_fusion
  417.7 2.5 multiply_reduce_fusion
  420.3 9.3 %all_to_all.81 = f32[16,12,128]{2,1,0:T(8,128)S(1)} all-to-all(f32[16,12,128]{2,1,0:T(8,128)S(1)} %reshape.889), channel_id=1, replica_groups=mesh['z'=4,'c'=2,'x'=4,'y'=4] {'x','y'}, dimensions={0} | all-to-all | bytes 196608 | tf_op jit(solution)/shard_map/all_to_all | solution.py:61
  429.5 33.0 %all_to_all.82 = f32[8,12,128]{2,1,0:T(8,128)S(1)} all-to-all(f32[8,12,128]{2,1,0:T(8,128)S(1)} %broadcast_in_dim.22), channel_id=1, replica_groups=mesh['z'=4,'c'=2,'x'=4,'y'=4] {'z','c'}, dimensions={0} | all-to-all | bytes 98304 | tf_op jit(solution)/shard_map/all_to_all | solution.py:57
  463.2 3.8 all-to-all-start.14
  467.0 1.5 bitcast_convert_fusion.2
  468.5 5.6 all-to-all-done.14
  475.3 16.0 %reduce-scatter.4.cloned.1.call-done = bf16[1,256,384]{2,1,0:T(8,128)(2,1)} async-done(((bf16[32,256,384]{2,1,0:T(8,128)(2,1)}), bf16[1,256,384]{2,1,0:T(8,128)(2,1)}) %reduce-scatter.4.cloned.1.call-update) | async-done | bytes 196624 | tf_op jit(solution)/shard_map/reduce_scatter | solution.py:74
  493.0 117.6 %reduce-scatter.8.cloned.1.call-done = bf16[1,256,1024]{2,1,0:T(8,128)(2,1)} async-done(((bf16[32,256,1024]{2,1,0:T(8,128)(2,1)}), bf16[1,256,1024]{2,1,0:T(8,128)(2,1)}) %reduce-scatter.8.cloned.1.call-update) | async-done | bytes 524304 | tf_op jit(solution)/shard_map/reduce_scatter | solution.py:74
  (147 shorter events, 23.3 us)
Async XLA Ops:
  7.2 56.6 %all-gather.5.cloned.1.call-start = ((), (), s32[]{:S(2)}) async-start(), calls=%async_computation.18 | async-start | bytes 6488064 | tf_op jit(solution)/shard_map/all_gather | solution.py:69
  9.1 4.6 copy-start.14
  9.9 101.0 %all-gather.9.cloned.1.call-start = ((), (), s32[]{:S(2)}) async-start(), calls=%async_computation.23 | async-start | bytes 2162688 | tf_op jit(solution)/shard_map/all_gather | solution.py:69
  11.5 2.9 copy-start.23
  11.5 2.9 copy-start.26
  11.5 200.5 %all-gather.7.cloned.1.call-start = ((), (), s32[]{:S(2)}) async-start(), calls=%async_computation.19 | async-start | bytes 17301504 | tf_op jit(solution)/shard_map/all_gather | solution.py:69
  16.4 30.4 %all-to-all-start = ((bf16[4,128,2048]{2,1,0:T(8,128)(2,1)}), bf16[4,128,2048]{2,1,0:T(8,128)(2,1)S(1)}, u32[]{:S(2)}, u32[]{:S(2)}) async-start(bf16[4,128,2048]{2,1,0:T(8,128)(2,1)} %broadcast_in_dim.16), calls=%async_computation | async-start | bytes 4194304 | tf_op jit(solution)/shard_map/all_to_all | solution.py:57
  46.8 25.4 %copy-start.4 = (bf16[4,128,2048]{2,1,0:T(8,128)(2,1)}, bf16[4,128,2048]{2,1,0:T(8,128)(2,1)S(1)}, u32[]{:S(2)}) copy-start(bf16[4,128,2048]{2,1,0:T(8,128)(2,1)S(1)} %all-to-all-done) | copy-start | bytes 6291460
  63.8 2.8 copy-start.9
  72.3 1.1 copy-start.8
  73.4 4.4 copy-start.29
  73.4 4.4 copy-start.31
  73.4 25.0 %all-to-all-start.1 = ((bf16[4,512,384]{2,1,0:T(8,128)(2,1)}), bf16[4,512,384]{2,1,0:T(8,128)(2,1)S(1)}, u32[]{:S(2)}, u32[]{:S(2)}) async-start(bf16[4,512,384]{2,1,0:T(8,128)(2,1)} %copy-done.8), calls=%async_computation.1 | async-start | bytes 3145728 | tf_op jit(solution)/shard_map/all_to_all | solution.py:65
  98.4 7.0 %copy-start.6 = (bf16[4,512,384]{2,1,0:T(8,128)(2,1)}, bf16[4,512,384]{2,1,0:T(8,128)(2,1)S(1)}, u32[]{:S(2)}) copy-start(bf16[4,512,384]{2,1,0:T(8,128)(2,1)S(1)} %all-to-all-done.1) | copy-start | bytes 4718596
  105.4 1.0 copy-start.10
  106.4 1.0 copy-start.12
  107.3 11.5 %all-to-all-start.2 = ((bf16[4,512,128]{2,1,0:T(8,128)(2,1)}), bf16[4,512,128]{2,1,0:T(8,128)(2,1)S(1)}, u32[]{:S(2)}, u32[]{:S(2)}) async-start(bf16[4,512,128]{2,1,0:T(8,128)(2,1)} %bitcast.12), calls=%async_computation.2 | async-start | bytes 1048576 | tf_op jit(solution)/shard_map/all_to_all | solution.py:65
  118.9 1.6 copy-start
  125.1 28.3 %all-to-all-start.3 = ((bf16[4,128,2048]{2,1,0:T(8,128)(2,1)}), bf16[4,128,2048]{2,1,0:T(8,128)(2,1)}, u32[]{:S(2)}, u32[]{:S(2)}) async-start(bf16[4,128,2048]{2,1,0:T(8,128)(2,1)} %bitcast.14), calls=%async_computation.3 | async-start | bytes 4194304 | tf_op jit(solution)/shard_map/all_to_all | solution.py:61
  129.6 26.0 %copy-start.24 = (f32[2048]{0:T(1024)S(1)}, f32[2048]{0:T(1024)}, u32[]{:S(2)}) copy-start(f32[2048]{0:T(1024)} %param.33) | copy-start | bytes 24580
  155.6 0.8 copy-start.22
  155.6 0.8 copy-start.27
  155.9 2.0 copy-start.17
  185.7 4.8 copy-start.25
  185.7 26.3 %all-to-all-start.5 = ((bf16[4,128,2048]{2,1,0:T(8,128)(2,1)}), bf16[4,128,2048]{2,1,0:T(8,128)(2,1)}, u32[]{:S(2)}, u32[]{:S(2)}) async-start(bf16[4,128,2048]{2,1,0:T(8,128)(2,1)} %broadcast_in_dim.19), calls=%async_computation.5 | async-start | bytes 4194304 | tf_op jit(solution)/shard_map/all_to_all | solution.py:57
  190.2 276.7 %reduce-scatter.6.cloned.1.call-start = ((), (), s32[]{:S(2)}) async-start(), calls=%async_computation.21 | async-start | bytes 2162688 | tf_op jit(solution)/shard_map/reduce_scatter | solution.py:74
  281.2 1.2 copy-start.18
  282.0 2.7 copy-start.15
  310.3 1.4 copy-start.2
  311.7 179.6 %reduce-scatter.4.cloned.1.call-start = ((), (), s32[]{:S(2)}) async-start(), calls=%async_computation.20 | async-start | bytes 6488064 | tf_op jit(solution)/shard_map/reduce_scatter | solution.py:74
  311.8 1.6 copy-start.1
  313.3 14.9 %copy-start.7 = (bf16[4,512,384]{2,1,0:T(8,128)(2,1)S(1)}, bf16[4,512,384]{2,1,0:T(8,128)(2,1)}, u32[]{:S(2)}) copy-start(bf16[4,512,384]{2,1,0:T(8,128)(2,1)} %copy-done.6) | copy-start | bytes 4718596
  313.3 14.9 %copy-start.11 = (f32[2,1024,128]{2,1,0:T(8,128)S(1)}, f32[2,1024,128]{2,1,0:T(8,128)}, u32[]{:S(2)}) copy-start(f32[2,1024,128]{2,1,0:T(8,128)} %copy-done.10) | copy-start | bytes 3145732
  313.3 14.9 %copy-start.13 = (f32[2,1024,128]{2,1,0:T(8,128)S(1)}, f32[2,1024,128]{2,1,0:T(8,128)}, u32[]{:S(2)}) copy-start(f32[2,1024,128]{2,1,0:T(8,128)} %copy-done.12) | copy-start | bytes 3145732
  338.0 15.1 %copy-start.5 = (bf16[4,128,2048]{2,1,0:T(8,128)(2,1)S(1)}, bf16[4,128,2048]{2,1,0:T(8,128)(2,1)}, u32[]{:S(2)}) copy-start(bf16[4,128,2048]{2,1,0:T(8,128)(2,1)} %copy-done.4) | copy-start | bytes 6291460
  367.8 2.7 copy-start.3
  370.4 240.2 %reduce-scatter.8.cloned.1.call-start = ((), (), s32[]{:S(2)}) async-start(), calls=%async_computation.22 | async-start | bytes 17301504 | tf_op jit(solution)/shard_map/reduce_scatter | solution.py:74
  391.4 4.6 copy-start.30
  391.4 21.4 %all-to-all-start.11 = ((bf16[4,128,2048]{2,1,0:T(8,128)(2,1)}), bf16[4,128,2048]{2,1,0:T(8,128)(2,1)}, u32[]{:S(2)}, u32[]{:S(2)}) async-start(bf16[4,128,2048]{2,1,0:T(8,128)(2,1)} %bitcast.30), calls=%async_computation.11 | async-start | bytes 4194304 | tf_op jit(solution)/shard_map/all_to_all | solution.py:61
  415.4 1.3 copy-start.16
  415.4 1.4 copy-start.20
  415.5 1.4 copy-start.28
  415.7 1.6 copy-start.19
  415.7 2.0 copy-start.21
  463.2 10.9 %all-to-all-start.14 = ((f32[16,12,128]{2,1,0:T(8,128)}), f32[16,12,128]{2,1,0:T(8,128)S(1)}, u32[]{:S(2)}, u32[]{:S(2)}) async-start(f32[16,12,128]{2,1,0:T(8,128)} %broadcast_in_dim.23), calls=%async_computation.14 | async-start | bytes 262144 | tf_op jit(solution)/shard_map/all_to_all | solution.py:57
Sparse Core Ops, SparseCore 0:
  10.8 52.8 all-gather.4
  66.6 43.1 all-gather.8
  112.6 71.8 all-gather.6
  311.8 89.4 reduce-scatter.5
  404.9 86.4 reduce-scatter.3
  495.6 114.9 reduce-scatter.7

commit v2 on v1

--- a/solution.py
+++ b/solution.py
@@ -65,6 +65,42 @@
     return lax.all_to_all(parts, axes, 0, 0)
 
 
+def ring(array, step):
+    return lax.ppermute(array, "y", [(i, (i + step) % RING) for i in range(RING)])
+
+
+def ring_gather(rows):
+    half = rows.shape[0] // 2
+    first, second = rows[:half], rows[half:]
+    before_first, after_second = ring(first, 1), ring(second, -1)
+    before_second, after_first = ring(second, 1), ring(first, -1)
+    across_first, across_second = ring(before_first, 1), ring(after_second, -1)
+    return jnp.concatenate(
+        [
+            first, second, before_first, before_second,
+            after_first, after_second, across_first, across_second,
+        ],
+        0,
+    )
+
+
+def ring_sum(rows):
+    own = rows.shape[0] // RING
+    half = own // 2
+    start, before, after, across = (rows[i * own : (i + 1) * own] for i in range(RING))
+    from_before, from_after = ring(across[:half], 1), ring(across[half:], -1)
+    second_after, first_before = ring(after[half:], 1), ring(before[:half], -1)
+    first_after = ring((after[:half].astype(WIDE) + from_before.astype(WIDE)).astype(LOW), 1)
+    second_before = ring((before[half:].astype(WIDE) + from_after.astype(WIDE)).astype(LOW), -1)
+    first = start[:half].astype(WIDE) + first_after.astype(WIDE) + first_before.astype(WIDE)
+    second = start[half:].astype(WIDE) + second_after.astype(WIDE) + second_before.astype(WIDE)
+    return jnp.concatenate([first, second], 0)
+
+
+def after(value, *others):
+    return lax.optimization_barrier((value,) + others)[0]
+
+
 def gather_weight(shard):
     full = lax.all_gather(shard, ("z", "c", "x"), axis=0)
     return full.reshape((8, 4) + shard.shape)
@@ -149,137 +185,139 @@
     )(rows, weight)
 
 
-def out_weight_body(rows_ref, heads_ref, out_ref):
-    out_ref[...] = dot_0(rows_ref[...], heads_ref[...]).astype(LOW).reshape(out_ref.shape)
-
-
-def out_weight_grad(rows, heads):
-    count, width = rows.shape
-    xs, _, cols = heads.shape
+def weight_grad_body(place_ref, norm_ref, qkv_ref, attn_ref, heads_ref, keep_ref, send_ref):
+    cols = qkv_ref.shape[-1]
+    parts = (
+        (dot_0(norm_ref[...], qkv_ref[...]), slice(0, cols)),
+        (dot_0(attn_ref[...], heads_ref[...]), slice(cols, None)),
+    )
+    first = place_ref[0] == 0
+    for value, where in parts:
+        value = value.astype(LOW).reshape(4, 2, -1, value.shape[-1])
+        keep_ref[:, :, where] = jnp.where(first, value[:, 0], value[:, 1])
+        send_ref[:, :, where] = jnp.where(first, value[:, 1], value[:, 0])
+
+
+def weight_grads(core_at, norm_rows, d_qkv, attn_rows, heads):
+    count, width = norm_rows.shape
+    xs, _, qkv_cols = d_qkv.shape
+    cols = heads.shape[-1]
     piece = width // 8
-    return call(
-        out_weight_body,
-        struct((8, xs, piece, cols), LOW),
+    half = struct((4, xs, piece, qkv_cols + cols), LOW)
+    block = pl.BlockSpec((4, None, piece, qkv_cols + cols), lambda i, *_: (0, i, 0, 0))
+    return call(
+        weight_grad_body,
+        (half, half),
         (xs,),
-        [whole((count, width)), pl.BlockSpec((None, count, cols), lambda i: (i, 0, 0))],
-        pl.BlockSpec((8, None, piece, cols), lambda i: (0, i, 0, 0)),
-        2 * count * width * xs * cols,
-        5 * 2**20,
-    )(rows, heads)
-
-
-def qkv_grad_body(norm_ref, grad_ref, weight_ref, weight_grad_ref, norm_grad_ref, total):
-    step = pl.program_id(0)
-    grad = grad_ref[...]
-    weight_grad_ref[...] = dot_0(norm_ref[...], grad).astype(LOW).reshape(weight_grad_ref.shape)
-    term = dot_t(grad, weight_ref[...].reshape(norm_ref.shape[1], -1))
-
-    @pl.when(step == 0)
+        [
+            whole((count, width)),
+            pl.BlockSpec((None, count, qkv_cols), lambda i, *_: (i, 0, 0)),
+            whole((count, width)),
+            pl.BlockSpec((None, count, cols), lambda i, *_: (i, 0, 0)),
+        ],
+        (block, block),
+        2 * count * width * xs * (cols + qkv_cols),
+        20 * 2**20,
+        prefetch=1,
+        vmem=48,
+    )(core_at, norm_rows, d_qkv, attn_rows, heads)
+
+
+def add_up(total, term):
+    @pl.when(pl.program_id(0) == 0)
     def _():
         total[...] = term
 
-    @pl.when(step > 0)
+    @pl.when(pl.program_id(0) > 0)
     def _():
         total[...] += term
 
-    @pl.when(step == RING - 1)
+
+def ffn_first_body(
+    norm_ref, cot_ref, up_ref, down_ref, bias_ref,
+    hidden_ref, grad_up_ref, norm_grad_ref, bias_grad_ref, total,
+):
+    width, cols = norm_ref.shape[1], up_ref.shape[-1]
+    up_w = up_ref[...].reshape(width, cols)
+    up = dot(norm_ref[...], up_w) + bias_ref[...]
+    normal = 0.5 * (1.0 + lax.erf(up * 0.7071067811865476))
+    hidden_ref[...] = (up * normal).astype(LOW)
+    slope = normal + up * (jnp.exp(-0.5 * up * up) * 0.3989422804014327)
+    grad_up = (dot(cot_ref[...], down_ref[...].reshape(width, cols)) * slope).astype(LOW)
+    grad_up_ref[...] = grad_up
+    bias_grad_ref[...] = jnp.sum(grad_up.astype(WIDE), 0, keepdims=True)
+    add_up(total, dot_t(grad_up, up_w))
+
+    @pl.when(pl.program_id(0) == pl.num_programs(0) - 1)
     def _():
         norm_grad_ref[...] = total[...].astype(LOW)
 
 
-def qkv_grad(norm_rows, grads, weight):
+def ffn_first(norm_rows, cot_rows, weight, bias):
     count, width = norm_rows.shape
     zc, xs, piece, cols = weight.shape
-    block = pl.BlockSpec((zc, None, piece, cols), lambda i: (0, i, 0, 0))
-    return call(
-        qkv_grad_body,
-        (struct(weight.shape, LOW), struct((count, width), LOW)),
+    size = cols // 2
+    rows = whole((count, width))
+    vector = pl.BlockSpec((None, 1, size), lambda i: (i, 0, 0))
+    wide = pl.BlockSpec((count, size), lambda i: (0, i))
+    return call(
+        ffn_first_body,
+        (
+            struct((count, xs * size), LOW),
+            struct((count, xs * size), LOW),
+            struct((count, width), LOW),
+            struct((xs, 1, size), WIDE),
+        ),
         (xs,),
-        [whole((count, width)), pl.BlockSpec((None, count, cols), lambda i: (i, 0, 0)), block],
-        (block, whole((count, width))),
-        4 * count * width * xs * cols,
-        20 * 2**20,
+        [
+            rows,
+            rows,
+            pl.BlockSpec((zc, None, piece, size), lambda i: (0, i, 0, 0)),
+            pl.BlockSpec((zc, None, piece, size), lambda i: (0, i, 0, 1)),
+            vector,
+        ],
+        (wide, wide, rows, vector),
+        6 * count * width * xs * size,
+        25 * 2**20,
         scratch=[pltpu.VMEM((count, width), WIDE)],
-    )(norm_rows, grads, weight)
-
-
-def ffn_body(
-    norm_ref, cot_ref, up_ref, down_ref, bias_ref,
-    branch_ref, norm_grad_ref, weight_grad_ref, bias_grad_ref,
-    branch_total, norm_total,
+        vmem=56,
+    )(norm_rows, cot_rows, weight, weight, bias)
+
+
+def ffn_second_body(
+    norm_ref, cot_ref, hidden_ref, grad_up_ref, down_ref, branch_ref, weight_grad_ref, total
 ):
-    step = pl.program_id(0)
-    width = norm_ref.shape[1]
-    cols = up_ref.shape[-1]
-    up_w = up_ref[...].reshape(width, cols)
-    down_w = down_ref[...].reshape(width, cols)
-    up = dot(norm_ref[...], up_w) + bias_ref[...]
-    normal = 0.5 * (1.0 + lax.erf(up * 0.7071067811865476))
-    hidden = (up * normal).astype(LOW)
-    slope = normal + up * (jnp.exp(-0.5 * up * up) * 0.3989422804014327)
-    grad_up = (dot(cot_ref[...], down_w) * slope).astype(LOW)
-    branch = dot_t(hidden, down_w)
-    norm_grad = dot_t(grad_up, up_w)
-
-    @pl.when(step == 0)
+    width, cols = norm_ref.shape[1], down_ref.shape[-1]
+    zc, piece, _ = weight_grad_ref.shape
+    hidden = hidden_ref[...]
+    weight_grad_ref[:, :, :cols] = (
+        dot_0(norm_ref[...], grad_up_ref[...]).astype(LOW).reshape(zc, piece, cols)
+    )
+    weight_grad_ref[:, :, cols:] = dot_0(cot_ref[...], hidden).astype(LOW).reshape(zc, piece, cols)
+    add_up(total, dot_t(hidden, down_ref[...].reshape(width, cols)))
+
+    @pl.when(pl.program_id(0) == pl.num_programs(0) - 1)
     def _():
-        branch_total[...] = branch
-        norm_total[...] = norm_grad
-
-    @pl.when(step > 0)
-    def _():
-        branch_total[...] += branch
-        norm_total[...] += norm_grad
-
-    half = step % 2
-    size = weight_grad_ref.shape[-1] // 4
-    zc, piece, _ = weight_grad_ref.shape
-    weight_grad_ref[:, :, pl.ds(pl.multiple_of(half * size, size), size)] = (
-        dot_0(norm_ref[...], grad_up).astype(LOW).reshape(zc, piece, cols)
-    )
-    weight_grad_ref[:, :, pl.ds(pl.multiple_of((half + 2) * size, size), size)] = (
-        dot_0(cot_ref[...], hidden).astype(LOW).reshape(zc, piece, cols)
-    )
-    bias_grad_ref[...] = jnp.sum(grad_up.astype(WIDE), 0, keepdims=True)
-
-    @pl.when(step == pl.num_programs(0) - 1)
-    def _():
-        branch_ref[...] = branch_total[...].astype(LOW)
-        norm_grad_ref[...] = norm_total[...].astype(LOW)
-
-
-def feed_forward(norm_rows, cot_rows, weight, bias):
+        branch_ref[...] = total[...].astype(LOW)
+
+
+def ffn_second(norm_rows, cot_rows, hidden, grad_up, weight):
     count, width = norm_rows.shape
     zc, xs, piece, cols = weight.shape
-    size = cols // 4
-    steps = 2 * xs
-    return call(
-        ffn_body,
-        (
-            struct((count, width), LOW),
-            struct((count, width), LOW),
-            struct(weight.shape, LOW),
-            struct((steps, 1, size), WIDE),
-        ),
-        (steps,),
-        [
-            whole((count, width)),
-            whole((count, width)),
-            pl.BlockSpec((zc, None, piece, size), lambda i: (0, i // 2, 0, i % 2)),
-            pl.BlockSpec((zc, None, piece, size), lambda i: (0, i // 2, 0, 2 + i % 2)),
-            pl.BlockSpec((None, 1, size), lambda i: (i, 0, 0)),
-        ],
-        (
-            whole((count, width)),
-            whole((count, width)),
-            pl.BlockSpec((zc, None, piece, cols), lambda i: (0, i // 2, 0, 0)),
-            pl.BlockSpec((None, 1, size), lambda i: (i, 0, 0)),
-        ),
-        12 * count * width * steps * size,
+    size = cols // 2
+    rows = whole((count, width))
+    wide = pl.BlockSpec((count, size), lambda i: (0, i))
+    return call(
+        ffn_second_body,
+        (struct((count, width), LOW), struct(weight.shape, LOW)),
+        (xs,),
+        [rows, rows, wide, wide, pl.BlockSpec((zc, None, piece, size), lambda i: (0, i, 0, 1))],
+        (rows, pl.BlockSpec((zc, None, piece, cols), lambda i: (0, i, 0, 0))),
+        6 * count * width * xs * size,
         40 * 2**20,
-        scratch=[pltpu.VMEM((count, width), WIDE), pltpu.VMEM((count, width), WIDE)],
+        scratch=[pltpu.VMEM((count, width), WIDE)],
         vmem=56,
-    )(norm_rows, cot_rows, weight, weight, bias)
+    )(norm_rows, cot_rows, hidden, grad_up, weight)
 
 
 def only_head(array, head):
@@ -293,14 +331,33 @@
     return k_place <= jnp.minimum(q_place, live_count - 1)
 
 
-def attend_body(live_ref, qkv_ref, heads_ref, exact_ref, log_ref):
+def slot_of(place, own):
+    apart = (place - own + RING) % RING
+    return jnp.where(apart == 0, 0, jnp.where(apart == RING - 1, 1, apart + 1))
+
+
+def load_ordered(blocks_ref, own, into):
+    rows = blocks_ref.shape[2]
+    for x in range(RING):
+        for y in range(RING):
+            at = (x * RING + y) * rows
+            into[at : at + rows] = blocks_ref[x, slot_of(y, own)]
+
+
+def store_ordered(blocks_ref, x, own, cols, value):
+    rows = blocks_ref.shape[2]
+    for y in range(RING):
+        blocks_ref[x, slot_of(y, own), :, cols] = value[y * rows : (y + 1) * rows]
+
+
+def attend_body(live_ref, qkv_ref, heads_ref, exact_ref, log_ref, qkv):
     live_count = live_ref[pl.program_id(0)]
+    own = live_ref[pl.num_programs(0)]
     length = exact_ref.shape[0]
     width = exact_ref.shape[1]
-    qkv = qkv_ref[...].reshape(length, 3 * width)
+    load_ordered(qkv_ref, own, qkv)
     key = qkv[:, width : 2 * width]
     value = qkv[:, 2 * width :]
-    per_x = SPAN // heads_ref.shape[2]
     for span in range(length // SPAN):
         start, extent = span * SPAN, (span + 1) * SPAN
         here = slice(start, extent)
@@ -322,7 +379,7 @@
             out = jnp.where(lane < HEAD_DIM, mixed[0], mixed[1])
             exact_ref[here] = out
             log_ref[here] = jnp.where(lane < HEAD_DIM, logs[0], logs[1])
-            heads_ref[span] = out.astype(LOW).reshape(heads_ref.shape[1:])
+            store_ordered(heads_ref, span, own, slice(None), out.astype(LOW))
 
         @pl.when(start >= live_count)
         def _():
@@ -351,24 +408,26 @@
         (row_block(rows, width), flat, flat),
         4 * 10**9,
         4 * 2**20,
+        scratch=[pltpu.VMEM((length, 3 * width), LOW)],
         prefetch=1,
     )(live_counts, qkv)
 
 
 def attend_back_body(
-    live_ref, qkv_ref, grad_ref, exact_ref, log_ref, out_ref, sum_ref, key_total, value_total
+    live_ref, qkv_ref, grad_ref, exact_ref, log_ref, out_ref, sum_ref,
+    key_total, value_total, qkv, grads,
 ):
     live_count = live_ref[pl.program_id(0)]
+    own = live_ref[pl.num_programs(0)]
     length, width = exact_ref.shape
     factor = HEAD_DIM**-0.5
-    qkv = qkv_ref[...].reshape(length, 3 * width)
-    grads = grad_ref[...].reshape(length, width)
+    load_ordered(qkv_ref, own, qkv)
+    load_ordered(grad_ref, own, grads)
     key = qkv[:, width : 2 * width]
     value = qkv[:, 2 * width :]
     key_total[...] = jnp.zeros_like(key_total)
     value_total[...] = jnp.zeros_like(value_total)
     sum_ref[...] = jnp.zeros_like(sum_ref)
-    piece = out_ref.shape[1:3]
     for span in range(length // SPAN):
         start, extent = span * SPAN, (span + 1) * SPAN
         here = slice(start, extent)
@@ -394,20 +453,20 @@
                 query_total += dot(d_scores, only_head(key[:extent], head))
                 key_total[:extent] += dot_0(d_scores, query_h)
             out = (query_total * factor).astype(LOW)
-            out_ref[span, :, :, :width] = out.reshape(piece + (width,))
+            store_ordered(out_ref, span, own, slice(0, width), out)
             sum_ref[:, :width] += jnp.sum(out.astype(WIDE), 0, keepdims=True)
 
         @pl.when(start >= live_count)
         def _():
-            out_ref[span, :, :, :width] = jnp.zeros(piece + (width,), LOW)
-
-    whole_shape = out_ref.shape[:3] + (width,)
-    out_ref[:, :, :, width : 2 * width] = (
-        (key_total[...] * factor).astype(LOW).reshape(whole_shape)
-    )
-    out = value_total[...].astype(LOW)
-    out_ref[:, :, :, 2 * width :] = out.reshape(whole_shape)
-    sum_ref[:, 2 * width :] = jnp.sum(out.astype(WIDE), 0, keepdims=True)
+            out_ref[span, :, :, :width] = jnp.zeros(out_ref.shape[1:3] + (width,), LOW)
+
+    key_grad = (key_total[...] * factor).astype(LOW)
+    value_grad = value_total[...].astype(LOW)
+    for span in range(RING):
+        here = slice(span * SPAN, (span + 1) * SPAN)
+        store_ordered(out_ref, span, own, slice(width, 2 * width), key_grad[here])
+        store_ordered(out_ref, span, own, slice(2 * width, None), value_grad[here])
+    sum_ref[:, 2 * width :] = jnp.sum(value_grad.astype(WIDE), 0, keepdims=True)
 
 
 def attend_back(live_counts, qkv, grads, exact, logs):
@@ -425,7 +484,12 @@
         ),
         8 * 10**9,
         8 * 2**20,
-        scratch=[pltpu.VMEM((length, width), WIDE), pltpu.VMEM((length, width), WIDE)],
+        scratch=[
+            pltpu.VMEM((length, width), WIDE),
+            pltpu.VMEM((length, width), WIDE),
+            pltpu.VMEM((length, 3 * width), LOW),
+            pltpu.VMEM((length, width), LOW),
+        ],
         prefetch=1,
         vmem=48,
     )(live_counts, qkv, grads, exact, logs)
@@ -448,16 +512,31 @@
     )
 
 
+def split_back(flat, vectors):
+    pieces, start = [], 0
+    for v in vectors:
+        pieces.append(flat[start : start + v.size])
+        start += v.size
+    return pieces
+
+
 def vector_totals(vectors):
     flat = jnp.concatenate([v.reshape(-1) for v in vectors])
     part = collect(flat.reshape(16, -1, 128), COLS)
     part = jnp.sum(spread(part, ROWS, 8), 0)
-    flat = spread(part, COLS, 16).reshape(-1)
-    totals, start = [], 0
-    for v in vectors:
-        totals.append(flat[start : start + v.size])
-        start += v.size
-    return totals
+    return split_back(spread(part, COLS, 16).reshape(-1), vectors)
+
+
+def short_totals(vectors, columns):
+    shared = jnp.concatenate([v.reshape(-1, 128) for v in vectors], 0)
+    rows = shared.shape[0]
+    parts = spread(jnp.concatenate([shared, columns], 0), COLS, 16)
+    part = jnp.concatenate([jnp.sum(parts[:, :rows], 0), parts[:, rows:].reshape(-1, 128)], 0)
+    part = jnp.sum(spread(part, ROWS, 8), 0)
+    placed = part[rows:].reshape(16, -1, 128)
+    return split_back(part[:rows].reshape(-1), vectors) + [
+        placed[:, i].reshape(-1) for i in range(columns.shape[0])
+    ]
 
 
 def shards(
@@ -469,13 +548,16 @@
     own = seqs * own_rows
     full_len = exit_layers.shape[1]
     x_at, y_at = lax.axis_index("x"), lax.axis_index("y")
+    core_at = lax.axis_index("c").astype(jnp.int32).reshape(1)
     head_at = x_at * RING + y_at
     head_cols = q_weight.shape[1]
     ff_cols = up_weight.shape[1]
 
     positions = jnp.arange(full_len)
     live_all = (positions[None, :] < seq_lengths[:, None]) & (exit_layers > layer_index[0])
-    live_counts = jnp.sum(live_all.astype(jnp.int32), 1)
+    live_counts = jnp.concatenate(
+        [jnp.sum(live_all.astype(jnp.int32), 1), y_at.astype(jnp.int32).reshape(1)]
+    )
     live_mine = lax.dynamic_slice_in_dim(live_all, head_at * own_rows, own_rows, 1)
     keep = live_mine.reshape(-1, 1).astype(WIDE)
 
@@ -485,10 +567,10 @@
 
     inputs = tokens.astype(WIDE).reshape(own, width)
     normed1, unit1, inverse1 = norm_parts(inputs, ln1_gain, ln1_shift)
-    norm1 = spread(normed1.astype(LOW), "y", RING).reshape(RING * own, width)
+    norm1 = ring_gather(normed1.astype(LOW))
     grad_y = cotangent.astype(WIDE).reshape(own, width)
     g_ffn = (keep * grad_y).astype(LOW)
-    cot_rows = spread(g_ffn, "y", RING).reshape(RING * own, width)
+    cot_rows = ring_gather(after(g_ffn, norm1))
 
     def mine(vector, cols):
         return lax.dynamic_index_in_dim(vector.reshape(RING, RING, cols), y_at, 1, False)
@@ -496,50 +578,42 @@
     bias = jnp.concatenate(
         [mine(q_bias, head_cols), jnp.zeros((RING, head_cols), WIDE), mine(v_bias, head_cols)], 1
     ).reshape(RING, 1, 3 * head_cols)
-    qkv = qkv_project(norm1, w_qkv, bias)
+    qkv = qkv_project(after(norm1, cot_rows), w_qkv, bias)
     rows5 = (RING, RING, seqs, own_rows)
     qkv = swap(qkv, "x").reshape(rows5 + (3 * head_cols,))
     heads, exact, logs = attend(live_counts, qkv, head_cols)
     heads = swap(heads.reshape(RING, RING * own, head_cols), "x")
-    branch1 = collect(out_project(heads, w_out).reshape(RING, own, width), "y") + out_bias
+    branch1 = ring_sum(out_project(heads, w_out)) + out_bias
     middle = inputs + keep * branch1
     normed2, unit2, inverse2 = norm_parts(middle, ln2_gain, ln2_shift)
-    norm2 = spread(normed2.astype(LOW), "y", RING).reshape(RING * own, width)
-
-    ff_bias = mine(up_bias, ff_cols).reshape(2 * RING, 1, ff_cols // 2)
-    branch2, g_norm2, ff_grad, up_bias_part = feed_forward(norm2, cot_rows, w_ff, ff_bias)
-    g_norm2 = collect(g_norm2.reshape(RING, own, width), "y")
+    norm2 = ring_gather(normed2.astype(LOW))
+
+    ff_bias = mine(up_bias, ff_cols).reshape(RING, 1, ff_cols)
+    hidden, grad_up, g_norm2, up_bias_part = ffn_first(norm2, cot_rows, w_ff, ff_bias)
+    g_norm2 = ring_sum(g_norm2)
+    branch2, ff_grad = ffn_second(norm2, cot_rows, hidden, grad_up, w_ff)
     ff_grad = settle(ff_grad)
     grad_mid = grad_y + norm_back(g_norm2, unit2, inverse2, ln2_gain)
     g_attn = (keep * grad_mid).astype(LOW)
-    attn_rows = spread(g_attn, "y", RING).reshape(RING * own, width)
+    attn_rows = ring_gather(g_attn)
+    branch2 = ring_sum(after(branch2, attn_rows)) + down_bias
+    result = (middle + keep * branch2).astype(LOW).reshape(tokens.shape)
     g_heads = swap(heads_grad(attn_rows, w_out), "x").reshape(rows5 + (head_cols,))
-    out_grad = settle(out_weight_grad(attn_rows, heads))
     d_qkv, d_sums = attend_back(live_counts, qkv, g_heads, exact, logs)
     d_qkv = swap(d_qkv.reshape(RING, RING * own, 3 * head_cols), "x")
-    qkv_weight_grad, g_norm1 = qkv_grad(norm1, d_qkv, w_qkv)
-    qkv_weight_grad = settle(qkv_weight_grad)
-    g_norm1 = collect(g_norm1.reshape(RING, own, width), "y")
+
+    kept, sent = weight_grads(core_at, norm1, d_qkv, attn_rows, heads)
+    other = lax.ppermute(sent, "c", [(0, 1), (1, 0)])
+    g_norm1 = ring_sum(out_project(after(d_qkv, sent), w_qkv))
+    both = (kept.astype(WIDE) + other.astype(WIDE)).astype(LOW)
+    small_grad = collect(both.reshape((16,) + both.shape[2:]), ("z", "x"))
     grad_tokens = (grad_mid + norm_back(g_norm1, unit1, inverse1, ln1_gain)).reshape(tokens.shape)
-
-    branch2 = collect(branch2.reshape(RING, own, width), "y") + down_bias
-    result = (middle + keep * branch2).astype(LOW).reshape(tokens.shape)
-
-    d_sums = jnp.sum(d_sums, 0).reshape(3, head_cols)
-
-    def placed(row):
-        blank = jnp.zeros((RING * RING, head_cols), WIDE)
-        return lax.dynamic_update_slice_in_dim(blank, row[None], head_at, 0)
 
     up_bias_full = lax.dynamic_update_slice_in_dim(
         jnp.zeros((RING, RING, ff_cols), WIDE), up_bias_part.reshape(RING, 1, ff_cols), y_at, 1
     )
-    totals = vector_totals(
+    out_bias_sum, ln2_gain_sum, ln2_shift_sum, up_bias_sum, down_bias_sum = vector_totals(
         (
-            jnp.sum(g_norm1 * unit1, 0),
-            jnp.sum(g_norm1, 0),
-            placed(d_sums[0]),
-            placed(d_sums[2]),
             jnp.sum(g_attn.astype(WIDE), 0),
             jnp.sum(g_norm2 * unit2, 0),
             jnp.sum(g_norm2, 0),
@@ -547,24 +621,28 @@
             jnp.sum(g_ffn.astype(WIDE), 0),
         )
     )
+    d_sums = jnp.sum(d_sums, 0).reshape(3, head_cols)
+    ln1_gain_sum, ln1_shift_sum, q_bias_sum, v_bias_sum = short_totals(
+        (jnp.sum(g_norm1 * unit1, 0), jnp.sum(g_norm1, 0)), d_sums[::2]
+    )
     return (
         result,
         grad_tokens,
-        totals[0],
-        totals[1],
-        qkv_weight_grad[:, :head_cols],
-        totals[2],
-        qkv_weight_grad[:, head_cols : 2 * head_cols],
-        qkv_weight_grad[:, 2 * head_cols :],
-        totals[3],
-        out_grad,
-        totals[4],
-        totals[5],
-        totals[6],
+        ln1_gain_sum,
+        ln1_shift_sum,
+        small_grad[:, :head_cols],
+        q_bias_sum,
+        small_grad[:, head_cols : 2 * head_cols],
+        small_grad[:, 2 * head_cols : 3 * head_cols],
+        v_bias_sum,
+        small_grad[:, 3 * head_cols :],
+        out_bias_sum,
+        ln2_gain_sum,
+        ln2_shift_sum,
         ff_grad[:, :ff_cols],
-        totals[7],
+        up_bias_sum,
         ff_grad[:, ff_cols:],
-        totals[8],
+        down_bias_sum,
     )
 
 

time: 622 us -> 535 us (0.86); the launches traced: 620 us -> 525 us
  blocking collectives: 161 us -> 0 us
  starting transfers between devices: 30 us -> 115 us
  waiting for transfers between devices: 269 us -> 220 us
  local copies, waits for them, and re-layouts: 24.9 us -> 48.4 us
  other arithmetic: 25.5 us -> 37.7 us
    all_to_all x8 -> x0, blocking collectives: 161 us -> none  [the longest x3 80.8 us: spread(): lax.all_to_all(jnp.broadcast_to(array[None], (size,) + array.shape), axes...]
    reduce_scatter x3 -> x1, waiting for transfers between devices: 134 us -> 0.01 us  [settle(): lax.psum_scatter(gradient.reshape((32,) + gradient.shape[2:]), ('z', 'c',...]
    ppermute x0 -> x49, waiting for transfers between devices: none -> 77 us  [the longest x48 77 us: ring(): lax.ppermute(array, 'y', [(i, (i + step) % RING) for i in range(RING)])]
    ppermute x0 -> x49, starting transfers between devices: none -> 58.7 us  [the longest x48 55.4 us: ring(): lax.ppermute(array, 'y', [(i, (i + step) % RING) for i in range(RING)])]
    all_to_all x3 -> x4, waiting for transfers between devices: 51.1 us -> 17 us  [spread(): lax.all_to_all(jnp.broadcast_to(array[None], (size,) + array.shape), axes...]
    all_to_all x2, waiting for transfers between devices: 38.5 us -> 63.7 us  [collect(): return jnp.sum(lax.all_to_all(parts, axes, 0, 0).astype(WIDE), 0)]
    unnamed x73 -> x117, local copies, waits for them, and re-layouts: 15 us -> 30.5 us
    all_to_all x2 -> x4, waiting for transfers between devices: 28.4 us -> 43 us  [swap(): return lax.all_to_all(parts, axes, 0, 0)]
  transfers between devices with their start and end apart: 13 -> 63, of which waited for: 10 -> 38; matrix products, arithmetic and copies ran while one was open for 4% -> 12% of each run, Pallas kernels for 7% -> 9%
where the time goes in v2:
time: 535 us; the launch traced here: 525 us
  waiting for transfers between devices  220 us (41%)
  starting transfers between devices  115 us (21%)
  Pallas kernels  88.2 us (16%)
  local copies, waits for them, and re-layouts  48.4 us (9%)
  other arithmetic  37.7 us (7%)
  between operations  15.5 us (3%)
    ppermute x48, waiting for transfers between devices, ring(): lax.ppermute(array, 'y', [(i, (i + step) % RING) for i in range(RING)])  77 us
    all_to_all x2, waiting for transfers between devices, collect(): return jnp.sum(lax.all_to_all(parts, axes, 0, 0).astype(WIDE), 0)  63.7 us
    ppermute x48, starting transfers between devices, ring(): lax.ppermute(array, 'y', [(i, (i + step) % RING) for i in range(RING)])  55.4 us
    all_to_all x4, waiting for transfers between devices, swap(): return lax.all_to_all(parts, axes, 0, 0)  43 us
    unnamed x117, local copies, waits for them, and re-layouts  30.5 us
    pallas_call x1, Pallas kernels, ffn_second(): call(ffn_second_body, (struct((count, width), LOW), struct(weight.shape,...  21.5 us
    pallas_call x1, Pallas kernels, ffn_first(): call(ffn_first_body, (struct((count, xs * size), LOW), struct((count, xs...  20.7 us
    all_gather x3, waiting for transfers between devices, gather_weight(): full = lax.all_gather(shard, ('z', 'c', 'x'), axis=0)  19.7 us
  transfers between devices with their start and end apart: 63, of which 38 were waited for; matrix products, arithmetic and copies ran while one was open for 12% of the time, Pallas kernels for 9%

profile of v2, /device:TPU:1, one launch (start us, length us, event | category | flops | bytes accessed | tf_op | source)
XLA Modules:
  0.0 524.9 jit_solution(2584337232749835488)
XLA Ops:
  25.2 5.2 collective-permute-done.3
  30.4 2.8 collective-permute-start.5
  52.8 3.4 collective-permute-done.10
  57.7 5.5 %all-gather.5.cloned.1.call-done = bf16[32,256,384]{2,1,0:T(8,128)(2,1)} async-done(((bf16[1,256,384]{2,1,0:T(8,128)(2,1)}), bf16[32,256,384]{2,1,0:T(8,128)(2,1)}) %all-gather.5.cloned.1.call-update) | async-done | bytes 6291472 | tf_op jit(solution)/shard_map/all_gather | solution.py:105
  66.0 6.5 %shard_map.323 = bf16[4,512,384]{2,1,0:T(8,128)(2,1)} custom-call(bf16[512,2048]{1,0:T(8,128)(2,1)S(1)} %constant_dynamic-update-slice_fusion.rows_ref.norm_ref, bf16[8,4,256,384]{3,2,1,0:T(8,128)(2,1)S(1)} %bitcast.102, f32[4,1,384]{2,1,0:T(1,128)S(1)} %reshape.555.bias_ref), custom_call_target="tpu_custom_call" | custom-call | flops 3221225472 | bytes 10485760 | tf_op jit(solution)/shard_map/pallas_call | solution.py:124
  72.4 3.6 all-to-all-start
  76.1 21.1 %all-to-all-done = bf16[4,512,384]{2,1,0:T(8,128)(2,1)S(1)} async-done(((bf16[4,512,384]{2,1,0:T(8,128)(2,1)}), bf16[4,512,384]{2,1,0:T(8,128)(2,1)S(1)}, u32[]{:S(2)}, u32[]{:S(2)}) %all-to-all-start) | async-done | bytes 1572896 | tf_op jit(solution)/shard_map/all_to_all | solution.py:65
  97.2 7.2 %shard_map.324 = (bf16[4,4,2,64,128]{4,3,2,1,0:T(8,128)(2,1)}, f32[2,1024,128]{2,1,0:T(8,128)S(1)}, f32[2,1024,128]{2,1,0:T(8,128)S(1)}) custom-call(s32[3]{0:T(128)S(1)} %pad_add_fusion.live_ref, bf16[4,4,2,64,384]{4,3,2,1,0:T(8,128)(2,1)S(1)} %bitcast.98), custom_call_target="tpu_custom_call" | custom-call | flops 4000000000 | bytes 4194304 | tf_op jit(solution)/shard_map/pallas_call | solution.py:399
  106.4 3.5 all-to-all-start.1
  109.9 12.9 %reduce-scatter.2.cloned.1.call-start = ((), (), s32[]{:S(2)}) async-start(), calls=%async_computation.13 | async-start | bytes 17301504 | tf_op jit(solution)/shard_map/reduce_scatter | solution.py:110
  124.4 2.9 shard_map.325
  131.5 4.1 collective-permute-done.12
  136.9 3.9 collective-permute-done.16
  143.7 4.8 collective-permute-done.15
  164.4 4.0 collective-permute-done.22
  169.8 14.2 %all-gather.7.cloned.1.call-done = bf16[32,256,1024]{2,1,0:T(8,128)(2,1)} async-done(((bf16[1,256,1024]{2,1,0:T(8,128)(2,1)}), bf16[32,256,1024]{2,1,0:T(8,128)(2,1)}) %all-gather.7.cloned.1.call-update) | async-done | bytes 16777232 | tf_op jit(solution)/shard_map/all_gather | solution.py:105
  184.0 20.7 %shard_map.326 = (bf16[512,2048]{1,0:T(8,128)(2,1)}, bf16[512,2048]{1,0:T(8,128)(2,1)}, bf16[512,2048]{1,0:T(8,128)(2,1)}, f32[4,1,512]{2,1,0:T(1,128)}) custom-call(bf16[512,2048]{1,0:T(8,128)(2,1)} %constant_dynamic-update-slice_fusion.14.norm_ref, bf16[512,2048]{1,0:T(8,128)(2,1)} %constant_dynamic-update-slice_fusion.7.cot_ref, ...), custom_call_target="tpu_custom_call" | custom-call | flops 12884901888 | bytes 26214400 | tf_op jit(solution)/shard_map/pallas_call | solution.py:263
  204.7 21.5 %shard_map.327 = (bf16[512,2048]{1,0:T(8,128)(2,1)}, bf16[8,4,256,1024]{3,2,1,0:T(8,128)(2,1)}) custom-call(bf16[512,2048]{1,0:T(8,128)(2,1)} %constant_dynamic-update-slice_fusion.14.norm_ref, bf16[512,2048]{1,0:T(8,128)(2,1)} %constant_dynamic-update-slice_fusion.7.cot_ref, bf16[512,2048]{1,0:T(8,128)(2,1)} %get-tuple-element.37.hidden_ref, ...), custom_call_target="tpu_custom_call" | custom-call | flops 12884901888 | bytes 41943040 | tf_op jit(solution)/shard_map/pallas_call | solution.py:310
  231.6 4.9 collective-permute-done.24
  237.9 3.9 collective-permute-done.28
  241.8 2.8 collective-permute-done.25
  244.9 5.3 %collective-permute-done.27 = bf16[64,2048]{1,0:T(8,128)(2,1)S(1)} collective-permute-done((bf16[64,2048]{1,0:T(8,128)(2,1)S(1)}, bf16[64,2048]{1,0:T(8,128)(2,1)S(1)}, u32[]{:S(2)}, u32[]{:S(2)}) %collective-permute-start.27) | collective-permute-done | bytes 262176 | tf_op jit(solution)/shard_map/ppermute | solution.py:69
  264.9 5.5 %collective-permute-done.34 = bf16[64,2048]{1,0:T(8,128)(2,1)S(1)} collective-permute-done((bf16[64,2048]{1,0:T(8,128)(2,1)S(1)}, bf16[64,2048]{1,0:T(8,128)(2,1)S(1)}, u32[]{:S(2)}, u32[]{:S(2)}) %collective-permute-start.34) | collective-permute-done | bytes 262176 | tf_op jit(solution)/shard_map/ppermute | solution.py:69
  270.5 3.7 shard_map.328
  274.2 4.0 all-to-all-start.2
  285.6 5.6 %all-to-all-done.2 = bf16[4,512,128]{2,1,0:T(8,128)(2,1)S(1)} async-done(((bf16[4,512,128]{2,1,0:T(8,128)(2,1)}), bf16[4,512,128]{2,1,0:T(8,128)(2,1)S(1)}, u32[]{:S(2)}, u32[]{:S(2)}) %all-to-all-start.2) | async-done | bytes 524320 | tf_op jit(solution)/shard_map/all_to_all | solution.py:65
  293.7 10.0 %shard_map.329 = (bf16[4,4,2,64,384]{4,3,2,1,0:T(8,128)(2,1)S(1)}, f32[2,1,384]{2,1,0:T(1,128)S(1)}) custom-call(s32[3]{0:T(128)S(1)} %pad_add_fusion.live_ref, bf16[4,4,2,64,384]{4,3,2,1,0:T(8,128)(2,1)S(1)} %bitcast.99, bf16[4,4,2,64,128]{4,3,2,1,0:T(8,128)(2,1)S(1)} %bitcast.101, f32[2,1024,128]{2,1,0:T(8,128)S(1)} %copy-done.13, ...), custom_call_target="tpu_custom_call" | custom-call | flops 8000000000 | bytes 8388608 | tf_op jit(solution)/shard_map/pallas_call | solution.py:476
  304.9 3.7 all-to-all-start.3
  310.0 6.6 %collective-permute-done.37 = bf16[64,2048]{1,0:T(8,128)(2,1)} collective-permute-done((bf16[64,2048]{1,0:T(8,128)(2,1)S(1)}, bf16[64,2048]{1,0:T(8,128)(2,1)}, u32[]{:S(2)}, u32[]{:S(2)}) %collective-permute-start.37) | collective-permute-done | bytes 262176 | tf_op jit(solution)/shard_map/ppermute | solution.py:69
  319.9 16.3 %all-to-all-done.3.qkv_ref.heads_ref = bf16[4,512,384]{2,1,0:T(8,128)(2,1)S(1)} async-done(((bf16[4,512,384]{2,1,0:T(8,128)(2,1)}), bf16[4,512,384]{2,1,0:T(8,128)(2,1)S(1)}, u32[]{:S(2)}, u32[]{:S(2)}) %all-to-all-start.3) | async-done | bytes 1572896 | tf_op jit(solution)/shard_map/all_to_all | solution.py:65
  338.3 10.7 %shard_map.330 = (bf16[4,4,256,512]{3,2,1,0:T(8,128)(2,1)}, bf16[4,4,256,512]{3,2,1,0:T(8,128)(2,1)}) custom-call(s32[1]{0:T(128)} %bitcast.23.place_ref, bf16[512,2048]{1,0:T(8,128)(2,1)S(1)} %copy-done.9, bf16[4,512,384]{2,1,0:T(8,128)(2,1)S(1)} %all-to-all-done.3.qkv_ref.heads_ref, bf16[512,2048]{1,0:T(8,128)(2,1)} %copy-done.2, ...), custom_call_target="tpu_custom_call" | custom-call | flops 4294967296 | bytes 20971520 | tf_op jit(solution)/shard_map/pallas_call | solution.py:208
  349.0 3.3 collective-permute-start.48
  357.6 5.1 shard_map.331
  375.1 5.6 %collective-permute-done.46 = bf16[64,2048]{1,0:T(8,128)(2,1)S(1)} collective-permute-done((bf16[64,2048]{1,0:T(8,128)(2,1)S(1)}, bf16[64,2048]{1,0:T(8,128)(2,1)S(1)}, u32[]{:S(2)}, u32[]{:S(2)}) %collective-permute-start.46) | collective-permute-done | bytes 262176 | tf_op jit(solution)/shard_map/ppermute | solution.py:69
  381.8 3.2 collective-permute-start.47
  386.2 3.5 all-to-all-start.7
  389.8 6.4 %all-to-all-done.7 = f32[16,8,128]{2,1,0:T(8,128)S(1)} async-done(((f32[16,8,128]{2,1,0:T(8,128)}), f32[16,8,128]{2,1,0:T(8,128)S(1)}, u32[]{:S(2)}, u32[]{:S(2)}) %all-to-all-start.7) | async-done | bytes 65568 | tf_op jit(solution)/shard_map/all_to_all | solution.py:61
  396.8 5.5 %all-to-all-start.8 = ((f32[8,8,128]{2,1,0:T(8,128)}), f32[8,8,128]{2,1,0:T(8,128)S(1)}, u32[]{:S(2)}, u32[]{:S(2)}) async-start(f32[8,8,128]{2,1,0:T(8,128)} %broadcast_in_dim.16), calls=%async_computation.8 | async-start | bytes 65536 | tf_op jit(solution)/shard_map/all_to_all | solution.py:57
  407.8 3.5 all-to-all-start.4
  411.4 7.8 %all-to-all-done.4 = f32[16,34,128]{2,1,0:T(8,128)S(1)} async-done(((f32[16,34,128]{2,1,0:T(8,128)}), f32[16,34,128]{2,1,0:T(8,128)S(1)}, u32[]{:S(2)}, u32[]{:S(2)}) %all-to-all-start.4) | async-done | bytes 278560 | tf_op jit(solution)/shard_map/all_to_all | solution.py:57
  419.9 4.0 all-to-all-start.9
  424.0 6.5 %all-to-all-done.9 = f32[16,8,128]{2,1,0:T(8,128)S(1)} async-done(((f32[16,8,128]{2,1,0:T(8,128)}), f32[16,8,128]{2,1,0:T(8,128)S(1)}, u32[]{:S(2)}, u32[]{:S(2)}) %all-to-all-start.9) | async-done | bytes 65568 | tf_op jit(solution)/shard_map/all_to_all | solution.py:57
  431.1 6.4 %all-to-all-start.5 = ((f32[8,64,128]{2,1,0:T(8,128)}), f32[8,64,128]{2,1,0:T(8,128)S(1)}, u32[]{:S(2)}, u32[]{:S(2)}) async-start(f32[8,64,128]{2,1,0:T(8,128)} %broadcast_in_dim.14), calls=%async_computation.5 | async-start | bytes 524288 | tf_op jit(solution)/shard_map/all_to_all | solution.py:57
  437.5 6.9 %add_convert_fusion = bf16[4,4,256,512]{3,2,1,0:T(8,128)(2,1)} fusion(bf16[4,4,256,512]{3,2,1,0:T(8,128)(2,1)} %collective-permute-done.48, bf16[4,4,256,512]{3,2,1,0:T(8,128)(2,1)} %get-tuple-element.48), kind=kLoop, calls=%fused_computation.1 | loop fusion | flops 8388608 | bytes 12582912 | tf_op jit(solution)/shard_map/convert_element_type | solution.py:608
  444.4 5.1 all-to-all-start.6
  450.9 2.9 fusion.12
  455.1 57.2 %all-to-all-done.6 = bf16[16,256,512]{2,1,0:T(8,128)(2,1)} async-done(((bf16[16,256,512]{2,1,0:T(8,128)(2,1)}), bf16[16,256,512]{2,1,0:T(8,128)(2,1)}, u32[]{:S(2)}, u32[]{:S(2)}) %all-to-all-start.6) | async-done | bytes 4194336 | tf_op jit(solution)/shard_map/all_to_all | solution.py:61
  512.3 2.8 convert_reduce_fusion
  (307 shorter events, 142.8 us)
Async XLA Ops:
  7.2 56.0 %all-gather.5.cloned.1.call-start = ((), (), s32[]{:S(2)}) async-start(), calls=%async_computation.11 | async-start | bytes 6488064 | tf_op jit(solution)/shard_map/all_gather | solution.py:105
  9.9 113.0 %all-gather.9.cloned.1.call-start = ((), (), s32[]{:S(2)}) async-start(), calls=%async_computation.14 | async-start | bytes 2162688 | tf_op jit(solution)/shard_map/all_gather | solution.py:105
  11.5 172.5 %all-gather.7.cloned.1.call-start = ((), (), s32[]{:S(2)}) async-start(), calls=%async_computation.12 | async-start | bytes 17301504 | tf_op jit(solution)/shard_map/all_gather | solution.py:105
  15.5 9.7 %collective-permute-start = (bf16[64,2048]{1,0:T(8,128)(2,1)}, bf16[64,2048]{1,0:T(8,128)(2,1)S(1)}, u32[]{:S(2)}, u32[]{:S(2)}) collective-permute-start(bf16[64,2048]{1,0:T(8,128)(2,1)} %get-tuple-element.108), channel_id=1, source_target_pairs={{0,1},{1,2},{2,3},{3,0},{4,5},{5,6},{6,7},{7,4},{8,9},{9,10},{10,1... | collective-permute-start | bytes 786440 | tf_op jit(solution)/shard_map/ppermute | solution.py:69
  17.6 16.6 %collective-permute-start.2 = (bf16[64,2048]{1,0:T(8,128)(2,1)}, bf16[64,2048]{1,0:T(8,128)(2,1)}, u32[]{:S(2)}, u32[]{:S(2)}) collective-permute-start(bf16[64,2048]{1,0:T(8,128)(2,1)} %get-tuple-element.108), channel_id=1, source_target_pairs={{0,3},{1,0},{2,1},{3,2},{4,7},{5,4},{6,5},{7,6},{8,11},{9,8},{10,9... | collective-permute-start | bytes 786440 | tf_op jit(solution)/shard_map/ppermute | solution.py:69
  19.1 14.2 %collective-permute-start.1 = (bf16[64,2048]{1,0:T(8,128)(2,1)}, bf16[64,2048]{1,0:T(8,128)(2,1)}, u32[]{:S(2)}, u32[]{:S(2)}) collective-permute-start(bf16[64,2048]{1,0:T(8,128)(2,1)} %get-tuple-element.107), channel_id=1, source_target_pairs={{0,1},{1,2},{2,3},{3,0},{4,5},{5,6},{6,7},{7,4},{8,9},{9,10},{10,1... | collective-permute-start | bytes 786440 | tf_op jit(solution)/shard_map/ppermute | solution.py:69
  19.1 11.3 %collective-permute-start.3 = (bf16[64,2048]{1,0:T(8,128)(2,1)}, bf16[64,2048]{1,0:T(8,128)(2,1)}, u32[]{:S(2)}, u32[]{:S(2)}) collective-permute-start(bf16[64,2048]{1,0:T(8,128)(2,1)} %get-tuple-element.107), channel_id=1, source_target_pairs={{0,3},{1,0},{2,1},{3,2},{4,7},{5,4},{6,5},{7,6},{8,11},{9,8},{10,9... | collective-permute-start | bytes 786440 | tf_op jit(solution)/shard_map/ppermute | solution.py:69
  25.2 11.3 %collective-permute-start.4 = (bf16[64,2048]{1,0:T(8,128)(2,1)S(1)}, bf16[64,2048]{1,0:T(8,128)(2,1)S(1)}, u32[]{:S(2)}, u32[]{:S(2)}) collective-permute-start(bf16[64,2048]{1,0:T(8,128)(2,1)S(1)} %collective-permute-done), channel_id=1, source_target_pairs={{0,1},{1,2},{2,3},{3,0},{4,5},{5,6},{6,7},{7,4},{8,9},{9,10},{10,1... | collective-permute-start | bytes 786440 | tf_op jit(solution)/shard_map/ppermute | solution.py:69
  38.1 12.6 %collective-permute-start.7 = (bf16[64,2048]{1,0:T(8,128)(2,1)S(1)}, bf16[64,2048]{1,0:T(8,128)(2,1)S(1)}, u32[]{:S(2)}, u32[]{:S(2)}) collective-permute-start(bf16[64,2048]{1,0:T(8,128)(2,1)S(1)} %get-tuple-element.105), channel_id=1, source_target_pairs={{0,1},{1,2},{2,3},{3,0},{4,5},{5,6},{6,7},{7,4},{8,9},{9,10},{10,1... | collective-permute-start | bytes 786440 | tf_op jit(solution)/shard_map/ppermute | solution.py:69
  41.9 9.4 %collective-permute-start.8 = (bf16[64,2048]{1,0:T(8,128)(2,1)S(1)}, bf16[64,2048]{1,0:T(8,128)(2,1)S(1)}, u32[]{:S(2)}, u32[]{:S(2)}) collective-permute-start(bf16[64,2048]{1,0:T(8,128)(2,1)S(1)} %get-tuple-element.106), channel_id=1, source_target_pairs={{0,3},{1,0},{2,1},{3,2},{4,7},{5,4},{6,5},{7,6},{8,11},{9,8},{10,9... | collective-permute-start | bytes 786440 | tf_op jit(solution)/shard_map/ppermute | solution.py:69
  44.7 11.6 %collective-permute-start.10 = (bf16[64,2048]{1,0:T(8,128)(2,1)S(1)}, bf16[64,2048]{1,0:T(8,128)(2,1)S(1)}, u32[]{:S(2)}, u32[]{:S(2)}) collective-permute-start(bf16[64,2048]{1,0:T(8,128)(2,1)S(1)} %collective-permute-done.6), channel_id=1, source_target_pairs={{0,1},{1,2},{2,3},{3,0},{4,5},{5,6},{6,7},{7,4},{8,9},{9,10},{10,1... | collective-permute-start | bytes 786440 | tf_op jit(solution)/shard_map/ppermute | solution.py:69
  45.9 11.0 %collective-permute-start.11 = (bf16[64,2048]{1,0:T(8,128)(2,1)S(1)}, bf16[64,2048]{1,0:T(8,128)(2,1)S(1)}, u32[]{:S(2)}, u32[]{:S(2)}) collective-permute-start(bf16[64,2048]{1,0:T(8,128)(2,1)S(1)} %collective-permute-done.9), channel_id=1, source_target_pairs={{0,3},{1,0},{2,1},{3,2},{4,7},{5,4},{6,5},{7,6},{8,11},{9,8},{10,9... | collective-permute-start | bytes 786440 | tf_op jit(solution)/shard_map/ppermute | solution.py:69
  72.4 24.8 %all-to-all-start = ((bf16[4,512,384]{2,1,0:T(8,128)(2,1)}), bf16[4,512,384]{2,1,0:T(8,128)(2,1)S(1)}, u32[]{:S(2)}, u32[]{:S(2)}) async-start(bf16[4,512,384]{2,1,0:T(8,128)(2,1)} %shard_map.323), calls=%async_computation | async-start | bytes 3145728 | tf_op jit(solution)/shard_map/all_to_all | solution.py:65
  106.4 16.5 %all-to-all-start.1 = ((bf16[4,512,128]{2,1,0:T(8,128)(2,1)}), bf16[4,512,128]{2,1,0:T(8,128)(2,1)S(1)}, u32[]{:S(2)}, u32[]{:S(2)}) async-start(bf16[4,512,128]{2,1,0:T(8,128)(2,1)} %bitcast.13), calls=%async_computation.1 | async-start | bytes 1048576 | tf_op jit(solution)/shard_map/all_to_all | solution.py:65
  109.9 406.1 %reduce-scatter.2.cloned.1.call-start = ((), (), s32[]{:S(2)}) async-start(), calls=%async_computation.13 | async-start | bytes 17301504 | tf_op jit(solution)/shard_map/reduce_scatter | solution.py:110
  127.4 8.1 %collective-permute-start.12 = (bf16[64,2048]{1,0:T(8,128)(2,1)S(1)}, bf16[64,2048]{1,0:T(8,128)(2,1)S(1)}, u32[]{:S(2)}, u32[]{:S(2)}) collective-permute-start(bf16[64,2048]{1,0:T(8,128)(2,1)S(1)} %get-tuple-element.86), channel_id=1, source_target_pairs={{0,1},{1,2},{2,3},{3,0},{4,5},{5,6},{6,7},{7,4},{8,9},{9,10},{10,1... | collective-permute-start | bytes 786440 | tf_op jit(solution)/shard_map/ppermute | solution.py:69
  128.7 8.2 %collective-permute-start.14 = (bf16[64,2048]{1,0:T(8,128)(2,1)S(1)}, bf16[64,2048]{1,0:T(8,128)(2,1)S(1)}, u32[]{:S(2)}, u32[]{:S(2)}) collective-permute-start(bf16[64,2048]{1,0:T(8,128)(2,1)S(1)} %get-tuple-element.89), channel_id=1, source_target_pairs={{0,3},{1,0},{2,1},{3,2},{4,7},{5,4},{6,5},{7,6},{8,11},{9,8},{10,9... | collective-permute-start | bytes 786440 | tf_op jit(solution)/shard_map/ppermute | solution.py:69
  130.2 10.6 %collective-permute-start.16 = (bf16[64,2048]{1,0:T(8,128)(2,1)S(1)}, bf16[64,2048]{1,0:T(8,128)(2,1)S(1)}, u32[]{:S(2)}, u32[]{:S(2)}) collective-permute-start(bf16[64,2048]{1,0:T(8,128)(2,1)S(1)} %get-tuple-element.87), channel_id=1, source_target_pairs={{0,3},{1,0},{2,1},{3,2},{4,7},{5,4},{6,5},{7,6},{8,11},{9,8},{10,9... | collective-permute-start | bytes 786440 | tf_op jit(solution)/shard_map/ppermute | solution.py:69
  135.7 12.8 %collective-permute-start.15 = (bf16[64,2048]{1,0:T(8,128)(2,1)S(1)}, bf16[64,2048]{1,0:T(8,128)(2,1)S(1)}, u32[]{:S(2)}, u32[]{:S(2)}) collective-permute-start(bf16[64,2048]{1,0:T(8,128)(2,1)S(1)} %get-tuple-element.88), channel_id=1, source_target_pairs={{0,1},{1,2},{2,3},{3,0},{4,5},{5,6},{6,7},{7,4},{8,9},{9,10},{10,1... | collective-permute-start | bytes 786440 | tf_op jit(solution)/shard_map/ppermute | solution.py:69
  151.8 10.4 %collective-permute-start.19 = (bf16[64,2048]{1,0:T(8,128)(2,1)}, bf16[64,2048]{1,0:T(8,128)(2,1)S(1)}, u32[]{:S(2)}, u32[]{:S(2)}) collective-permute-start(bf16[64,2048]{1,0:T(8,128)(2,1)} %get-tuple-element.103), channel_id=1, source_target_pairs={{0,1},{1,2},{2,3},{3,0},{4,5},{5,6},{6,7},{7,4},{8,9},{9,10},{10,1... | collective-permute-start | bytes 786440 | tf_op jit(solution)/shard_map/ppermute | solution.py:69
  158.8 9.6 %collective-permute-start.22 = (bf16[64,2048]{1,0:T(8,128)(2,1)S(1)}, bf16[64,2048]{1,0:T(8,128)(2,1)S(1)}, u32[]{:S(2)}, u32[]{:S(2)}) collective-permute-start(bf16[64,2048]{1,0:T(8,128)(2,1)S(1)} %collective-permute-done.18), channel_id=1, source_target_pairs={{0,1},{1,2},{2,3},{3,0},{4,5},{5,6},{6,7},{7,4},{8,9},{9,10},{10,1... | collective-permute-start | bytes 786440 | tf_op jit(solution)/shard_map/ppermute | solution.py:69
  159.5 9.6 %collective-permute-start.23 = (bf16[64,2048]{1,0:T(8,128)(2,1)S(1)}, bf16[64,2048]{1,0:T(8,128)(2,1)S(1)}, u32[]{:S(2)}, u32[]{:S(2)}) collective-permute-start(bf16[64,2048]{1,0:T(8,128)(2,1)S(1)} %collective-permute-done.21), channel_id=1, source_target_pairs={{0,3},{1,0},{2,1},{3,2},{4,7},{5,4},{6,5},{7,6},{8,11},{9,8},{10,9... | collective-permute-start | bytes 786440 | tf_op jit(solution)/shard_map/ppermute | solution.py:69
  227.6 8.9 %collective-permute-start.24 = (bf16[64,2048]{1,0:T(8,128)(2,1)S(1)}, bf16[64,2048]{1,0:T(8,128)(2,1)S(1)}, u32[]{:S(2)}, u32[]{:S(2)}) collective-permute-start(bf16[64,2048]{1,0:T(8,128)(2,1)S(1)} %get-tuple-element.80), channel_id=1, source_target_pairs={{0,1},{1,2},{2,3},{3,0},{4,5},{5,6},{6,7},{7,4},{8,9},{9,10},{10,1... | collective-permute-start | bytes 786440 | tf_op jit(solution)/shard_map/ppermute | solution.py:69
  228.9 9.0 %collective-permute-start.26 = (bf16[64,2048]{1,0:T(8,128)(2,1)S(1)}, bf16[64,2048]{1,0:T(8,128)(2,1)S(1)}, u32[]{:S(2)}, u32[]{:S(2)}) collective-permute-start(bf16[64,2048]{1,0:T(8,128)(2,1)S(1)} %get-tuple-element.83), channel_id=1, source_target_pairs={{0,3},{1,0},{2,1},{3,2},{4,7},{5,4},{6,5},{7,6},{8,11},{9,8},{10,9... | collective-permute-start | bytes 786440 | tf_op jit(solution)/shard_map/ppermute | solution.py:69
  230.3 11.5 %collective-permute-start.28 = (bf16[64,2048]{1,0:T(8,128)(2,1)S(1)}, bf16[64,2048]{1,0:T(8,128)(2,1)S(1)}, u32[]{:S(2)}, u32[]{:S(2)}) collective-permute-start(bf16[64,2048]{1,0:T(8,128)(2,1)S(1)} %get-tuple-element.81), channel_id=1, source_target_pairs={{0,3},{1,0},{2,1},{3,2},{4,7},{5,4},{6,5},{7,6},{8,11},{9,8},{10,9... | collective-permute-start | bytes 786440 | tf_op jit(solution)/shard_map/ppermute | solution.py:69
  236.7 13.6 %collective-permute-start.27 = (bf16[64,2048]{1,0:T(8,128)(2,1)S(1)}, bf16[64,2048]{1,0:T(8,128)(2,1)S(1)}, u32[]{:S(2)}, u32[]{:S(2)}) collective-permute-start(bf16[64,2048]{1,0:T(8,128)(2,1)S(1)} %get-tuple-element.82), channel_id=1, source_target_pairs={{0,1},{1,2},{2,3},{3,0},{4,5},{5,6},{6,7},{7,4},{8,9},{9,10},{10,1... | collective-permute-start | bytes 786440 | tf_op jit(solution)/shard_map/ppermute | solution.py:69
  260.5 9.9 %collective-permute-start.34 = (bf16[64,2048]{1,0:T(8,128)(2,1)S(1)}, bf16[64,2048]{1,0:T(8,128)(2,1)S(1)}, u32[]{:S(2)}, u32[]{:S(2)}) collective-permute-start(bf16[64,2048]{1,0:T(8,128)(2,1)S(1)} %collective-permute-done.30), channel_id=1, source_target_pairs={{0,1},{1,2},{2,3},{3,0},{4,5},{5,6},{6,7},{7,4},{8,9},{9,10},{10,1... | collective-permute-start | bytes 786440 | tf_op jit(solution)/shard_map/ppermute | solution.py:69
  260.5 9.9 %collective-permute-start.35 = (bf16[64,2048]{1,0:T(8,128)(2,1)S(1)}, bf16[64,2048]{1,0:T(8,128)(2,1)S(1)}, u32[]{:S(2)}, u32[]{:S(2)}) collective-permute-start(bf16[64,2048]{1,0:T(8,128)(2,1)S(1)} %collective-permute-done.33), channel_id=1, source_target_pairs={{0,3},{1,0},{2,1},{3,2},{4,7},{5,4},{6,5},{7,6},{8,11},{9,8},{10,9... | collective-permute-start | bytes 786440 | tf_op jit(solution)/shard_map/ppermute | solution.py:69
  274.2 17.1 %all-to-all-start.2 = ((bf16[4,512,128]{2,1,0:T(8,128)(2,1)}), bf16[4,512,128]{2,1,0:T(8,128)(2,1)S(1)}, u32[]{:S(2)}, u32[]{:S(2)}) async-start(bf16[4,512,128]{2,1,0:T(8,128)(2,1)} %shard_map.328), calls=%async_computation.2 | async-start | bytes 1048576 | tf_op jit(solution)/shard_map/all_to_all | solution.py:65
  280.7 29.3 %collective-permute-start.38 = (bf16[64,2048]{1,0:T(8,128)(2,1)}, bf16[64,2048]{1,0:T(8,128)(2,1)}, u32[]{:S(2)}, u32[]{:S(2)}) collective-permute-start(bf16[64,2048]{1,0:T(8,128)(2,1)} %get-tuple-element.78), channel_id=1, source_target_pairs={{0,3},{1,0},{2,1},{3,2},{4,7},{5,4},{6,5},{7,6},{8,11},{9,8},{10,9... | collective-permute-start | bytes 786440 | tf_op jit(solution)/shard_map/ppermute | solution.py:69
  283.0 25.6 %collective-permute-start.36 = (bf16[64,2048]{1,0:T(8,128)(2,1)}, bf16[64,2048]{1,0:T(8,128)(2,1)}, u32[]{:S(2)}, u32[]{:S(2)}) collective-permute-start(bf16[64,2048]{1,0:T(8,128)(2,1)} %get-tuple-element.75), channel_id=1, source_target_pairs={{0,1},{1,2},{2,3},{3,0},{4,5},{5,6},{6,7},{7,4},{8,9},{9,10},{10,1... | collective-permute-start | bytes 786440 | tf_op jit(solution)/shard_map/ppermute | solution.py:69
  283.0 27.1 %collective-permute-start.40 = (bf16[64,2048]{1,0:T(8,128)(2,1)}, bf16[64,2048]{1,0:T(8,128)(2,1)}, u32[]{:S(2)}, u32[]{:S(2)}) collective-permute-start(bf16[64,2048]{1,0:T(8,128)(2,1)} %get-tuple-element.76), channel_id=1, source_target_pairs={{0,3},{1,0},{2,1},{3,2},{4,7},{5,4},{6,5},{7,6},{8,11},{9,8},{10,9... | collective-permute-start | bytes 786440 | tf_op jit(solution)/shard_map/ppermute | solution.py:69
  304.9 31.3 %all-to-all-start.3 = ((bf16[4,512,384]{2,1,0:T(8,128)(2,1)}), bf16[4,512,384]{2,1,0:T(8,128)(2,1)S(1)}, u32[]{:S(2)}, u32[]{:S(2)}) async-start(bf16[4,512,384]{2,1,0:T(8,128)(2,1)} %bitcast.100), calls=%async_computation.3 | async-start | bytes 3145728 | tf_op jit(solution)/shard_map/all_to_all | solution.py:65
  310.0 42.3 %collective-permute-start.39 = (bf16[64,2048]{1,0:T(8,128)(2,1)}, bf16[64,2048]{1,0:T(8,128)(2,1)S(1)}, u32[]{:S(2)}, u32[]{:S(2)}) collective-permute-start(bf16[64,2048]{1,0:T(8,128)(2,1)} %get-tuple-element.77), channel_id=1, source_target_pairs={{0,1},{1,2},{2,3},{3,0},{4,5},{5,6},{6,7},{7,4},{8,9},{9,10},{10,1... | collective-permute-start | bytes 786440 | tf_op jit(solution)/shard_map/ppermute | solution.py:69
  319.0 33.3 %collective-permute-start.41 = (bf16[64,2048]{1,0:T(8,128)(2,1)}, bf16[64,2048]{1,0:T(8,128)(2,1)S(1)}, u32[]{:S(2)}, u32[]{:S(2)}) collective-permute-start(bf16[64,2048]{1,0:T(8,128)(2,1)} %get-tuple-element.74), channel_id=1, source_target_pairs={{0,3},{1,0},{2,1},{3,2},{4,7},{5,4},{6,5},{7,6},{8,11},{9,8},{10,9... | collective-permute-start | bytes 786440 | tf_op jit(solution)/shard_map/ppermute | solution.py:69
  349.0 88.5 %collective-permute-start.48 = (bf16[4,4,256,512]{3,2,1,0:T(8,128)(2,1)}, bf16[4,4,256,512]{3,2,1,0:T(8,128)(2,1)}, u32[]{:S(2)}, u32[]{:S(2)}) collective-permute-start(bf16[4,4,256,512]{3,2,1,0:T(8,128)(2,1)} %get-tuple-element.45), channel_id=1, source_target_pairs={{0,16},{16,0},{1,17},{17,1},{2,18},{18,2},{3,19},{19,3},{4,20},{20... | collective-permute-start | bytes 12582920 | tf_op jit(solution)/shard_map/ppermute | solution.py:606
  363.5 9.1 %collective-permute-start.42 = (bf16[64,2048]{1,0:T(8,128)(2,1)S(1)}, bf16[64,2048]{1,0:T(8,128)(2,1)S(1)}, u32[]{:S(2)}, u32[]{:S(2)}) collective-permute-start(bf16[64,2048]{1,0:T(8,128)(2,1)S(1)} %get-tuple-element.69), channel_id=1, source_target_pairs={{0,1},{1,2},{2,3},{3,0},{4,5},{5,6},{6,7},{7,4},{8,9},{9,10},{10,1... | collective-permute-start | bytes 786440 | tf_op jit(solution)/shard_map/ppermute | solution.py:69
  366.9 8.1 %collective-permute-start.44 = (bf16[64,2048]{1,0:T(8,128)(2,1)S(1)}, bf16[64,2048]{1,0:T(8,128)(2,1)S(1)}, u32[]{:S(2)}, u32[]{:S(2)}) collective-permute-start(bf16[64,2048]{1,0:T(8,128)(2,1)S(1)} %get-tuple-element.72), channel_id=1, source_target_pairs={{0,3},{1,0},{2,1},{3,2},{4,7},{5,4},{6,5},{7,6},{8,11},{9,8},{10,9... | collective-permute-start | bytes 786440 | tf_op jit(solution)/shard_map/ppermute | solution.py:69
  369.4 11.3 %collective-permute-start.46 = (bf16[64,2048]{1,0:T(8,128)(2,1)S(1)}, bf16[64,2048]{1,0:T(8,128)(2,1)S(1)}, u32[]{:S(2)}, u32[]{:S(2)}) collective-permute-start(bf16[64,2048]{1,0:T(8,128)(2,1)S(1)} %get-tuple-element.70), channel_id=1, source_target_pairs={{0,3},{1,0},{2,1},{3,2},{4,7},{5,4},{6,5},{7,6},{8,11},{9,8},{10,9... | collective-permute-start | bytes 786440 | tf_op jit(solution)/shard_map/ppermute | solution.py:69
  372.7 8.2 %collective-permute-start.43 = (bf16[64,2048]{1,0:T(8,128)(2,1)S(1)}, bf16[64,2048]{1,0:T(8,128)(2,1)S(1)}, u32[]{:S(2)}, u32[]{:S(2)}) collective-permute-start(bf16[64,2048]{1,0:T(8,128)(2,1)S(1)} %add_convert_fusion.4), channel_id=1, source_target_pairs={{0,1},{1,2},{2,3},{3,0},{4,5},{5,6},{6,7},{7,4},{8,9},{9,10},{10,1... | collective-permute-start | bytes 786440 | tf_op jit(solution)/shard_map/ppermute | solution.py:69
  374.0 28.4 %collective-permute-start.45 = (bf16[64,2048]{1,0:T(8,128)(2,1)}, bf16[64,2048]{1,0:T(8,128)(2,1)}, u32[]{:S(2)}, u32[]{:S(2)}) collective-permute-start(bf16[64,2048]{1,0:T(8,128)(2,1)} %get-tuple-element.71), channel_id=1, source_target_pairs={{0,1},{1,2},{2,3},{3,0},{4,5},{5,6},{6,7},{7,4},{8,9},{9,10},{10,1... | collective-permute-start | bytes 786440 | tf_op jit(solution)/shard_map/ppermute | solution.py:69
  381.8 20.6 %collective-permute-start.47 = (bf16[64,2048]{1,0:T(8,128)(2,1)}, bf16[64,2048]{1,0:T(8,128)(2,1)}, u32[]{:S(2)}, u32[]{:S(2)}) collective-permute-start(bf16[64,2048]{1,0:T(8,128)(2,1)} %get-tuple-element.68), channel_id=1, source_target_pairs={{0,3},{1,0},{2,1},{3,2},{4,7},{5,4},{6,5},{7,6},{8,11},{9,8},{10,9... | collective-permute-start | bytes 786440 | tf_op jit(solution)/shard_map/ppermute | solution.py:69
  386.2 10.0 %all-to-all-start.7 = ((f32[16,8,128]{2,1,0:T(8,128)}), f32[16,8,128]{2,1,0:T(8,128)S(1)}, u32[]{:S(2)}, u32[]{:S(2)}) async-start(f32[16,8,128]{2,1,0:T(8,128)} %bitcast.35), calls=%async_computation.7 | async-start | bytes 131072 | tf_op jit(solution)/shard_map/all_to_all | solution.py:61
  396.8 10.3 %all-to-all-start.8 = ((f32[8,8,128]{2,1,0:T(8,128)}), f32[8,8,128]{2,1,0:T(8,128)S(1)}, u32[]{:S(2)}, u32[]{:S(2)}) async-start(f32[8,8,128]{2,1,0:T(8,128)} %broadcast_in_dim.16), calls=%async_computation.8 | async-start | bytes 65536 | tf_op jit(solution)/shard_map/all_to_all | solution.py:57
  407.8 11.4 %all-to-all-start.4 = ((f32[16,34,128]{2,1,0:T(8,128)}), f32[16,34,128]{2,1,0:T(8,128)S(1)}, u32[]{:S(2)}, u32[]{:S(2)}) async-start(f32[16,34,128]{2,1,0:T(8,128)} %broadcast_in_dim.13), calls=%async_computation.4 | async-start | bytes 655360 | tf_op jit(solution)/shard_map/all_to_all | solution.py:57
  419.9 10.6 %all-to-all-start.9 = ((f32[16,8,128]{2,1,0:T(8,128)}), f32[16,8,128]{2,1,0:T(8,128)S(1)}, u32[]{:S(2)}, u32[]{:S(2)}) async-start(f32[16,8,128]{2,1,0:T(8,128)} %broadcast_in_dim.17), calls=%async_computation.9 | async-start | bytes 131072 | tf_op jit(solution)/shard_map/all_to_all | solution.py:57
  431.1 13.2 %all-to-all-start.5 = ((f32[8,64,128]{2,1,0:T(8,128)}), f32[8,64,128]{2,1,0:T(8,128)S(1)}, u32[]{:S(2)}, u32[]{:S(2)}) async-start(f32[8,64,128]{2,1,0:T(8,128)} %broadcast_in_dim.14), calls=%async_computation.5 | async-start | bytes 524288 | tf_op jit(solution)/shard_map/all_to_all | solution.py:57
  444.4 67.9 %all-to-all-start.6 = ((bf16[16,256,512]{2,1,0:T(8,128)(2,1)}), bf16[16,256,512]{2,1,0:T(8,128)(2,1)}, u32[]{:S(2)}, u32[]{:S(2)}) async-start(bf16[16,256,512]{2,1,0:T(8,128)(2,1)} %bitcast.104), calls=%async_computation.6 | async-start | bytes 8388608 | tf_op jit(solution)/shard_map/all_to_all | solution.py:61
  (61 other events, 464.0 us)
Sparse Core Ops, SparseCore 0:
  10.3 52.8 all-gather.4
  66.0 43.1 all-gather.8
  112.1 71.8 all-gather.6
  226.3 127.8 reduce-scatter.1

commit v3 on v2

--- a/solution.py
+++ b/solution.py
@@ -65,8 +65,26 @@
     return lax.all_to_all(parts, axes, 0, 0)
 
 
-def ring(array, step):
-    return lax.ppermute(array, "y", [(i, (i + step) % RING) for i in range(RING)])
+def ring(array, step, axis="y"):
+    return lax.ppermute(array, axis, [(i, (i + step) % RING) for i in range(RING)])
+
+
+def ring_collect(parts, axis, dim):
+    here = lax.axis_index(axis)
+
+    def part(step):
+        return lax.dynamic_index_in_dim(parts, (here + step) % RING, dim, False)
+
+    terms = [part(0)] + [ring(part(step), step, axis) for step in (1, 2, 3)]
+    return sum(term.astype(WIDE) for term in terms)
+
+
+def cube_collect(parts, beside):
+    half = parts.shape[2] // 2
+    first = ring_collect(parts[:, :, :half], "z", 0).astype(LOW)
+    second = ring_collect(parts[:, :, half:], "x", 1).astype(LOW)
+    first, second, beside = tie(first, second, beside)
+    return jnp.concatenate([ring_collect(first, "x", 0), ring_collect(second, "z", 0)], 0), beside
 
 
 def ring_gather(rows):
@@ -84,7 +102,7 @@
     )
 
 
-def ring_sum(rows):
+def ring_sum(rows, beside=None):
     own = rows.shape[0] // RING
     half = own // 2
     start, before, after, across = (rows[i * own : (i + 1) * own] for i in range(RING))
@@ -92,13 +110,17 @@
     second_after, first_before = ring(after[half:], 1), ring(before[:half], -1)
     first_after = ring((after[:half].astype(WIDE) + from_before.astype(WIDE)).astype(LOW), 1)
     second_before = ring((before[half:].astype(WIDE) + from_after.astype(WIDE)).astype(LOW), -1)
-    first = start[:half].astype(WIDE) + first_after.astype(WIDE) + first_before.astype(WIDE)
-    second = start[half:].astype(WIDE) + second_after.astype(WIDE) + second_before.astype(WIDE)
-    return jnp.concatenate([first, second], 0)
-
-
-def after(value, *others):
-    return lax.optimization_barrier((value,) + others)[0]
+    came = (first_after, first_before, second_after, second_before)
+    if beside is not None:
+        came, beside = tie(came, beside)
+    first = start[:half].astype(WIDE) + came[0].astype(WIDE) + came[1].astype(WIDE)
+    second = start[half:].astype(WIDE) + came[2].astype(WIDE) + came[3].astype(WIDE)
+    total = jnp.concatenate([first, second], 0)
+    return total if beside is None else (total, beside)
+
+
+def tie(*arrays):
+    return lax.optimization_barrier(arrays)
 
 
 def gather_weight(shard):
@@ -185,42 +207,35 @@
     )(rows, weight)
 
 
-def weight_grad_body(place_ref, norm_ref, qkv_ref, attn_ref, heads_ref, keep_ref, send_ref):
-    cols = qkv_ref.shape[-1]
-    parts = (
-        (dot_0(norm_ref[...], qkv_ref[...]), slice(0, cols)),
-        (dot_0(attn_ref[...], heads_ref[...]), slice(cols, None)),
-    )
+def weight_grad_body(place_ref, rows_ref, grad_ref, keep_ref, send_ref):
+    value = dot_0(rows_ref[...], grad_ref[...]).astype(LOW)
+    value = value.reshape(4, 2, -1, value.shape[-1])
     first = place_ref[0] == 0
-    for value, where in parts:
-        value = value.astype(LOW).reshape(4, 2, -1, value.shape[-1])
-        keep_ref[:, :, where] = jnp.where(first, value[:, 0], value[:, 1])
-        send_ref[:, :, where] = jnp.where(first, value[:, 1], value[:, 0])
-
-
-def weight_grads(core_at, norm_rows, d_qkv, attn_rows, heads):
-    count, width = norm_rows.shape
-    xs, _, qkv_cols = d_qkv.shape
-    cols = heads.shape[-1]
+    keep_ref[...] = jnp.where(first, value[:, 0], value[:, 1])
+    send_ref[...] = jnp.where(first, value[:, 1], value[:, 0])
+
+
+def weight_grads(core_at, rows, columns):
+    count, width = rows.shape
+    xs, _, cols = columns.shape
     piece = width // 8
-    half = struct((4, xs, piece, qkv_cols + cols), LOW)
-    block = pl.BlockSpec((4, None, piece, qkv_cols + cols), lambda i, *_: (0, i, 0, 0))
+    half = struct((4, xs, piece, cols), LOW)
+    block = pl.BlockSpec((4, None, piece, cols), lambda i, *_: (0, i, 0, 0))
     return call(
         weight_grad_body,
         (half, half),
         (xs,),
-        [
-            whole((count, width)),
-            pl.BlockSpec((None, count, qkv_cols), lambda i, *_: (i, 0, 0)),
-            whole((count, width)),
-            pl.BlockSpec((None, count, cols), lambda i, *_: (i, 0, 0)),
-        ],
+        [whole((count, width)), pl.BlockSpec((None, count, cols), lambda i, *_: (i, 0, 0))],
         (block, block),
-        2 * count * width * xs * (cols + qkv_cols),
-        20 * 2**20,
+        2 * count * width * xs * cols,
+        15 * 2**20,
         prefetch=1,
-        vmem=48,
-    )(core_at, norm_rows, d_qkv, attn_rows, heads)
+    )(core_at, rows, columns)
+
+
+def core_sum(kept, sent):
+    other = lax.ppermute(sent, "c", [(0, 1), (1, 0)])
+    return (kept.astype(WIDE) + other.astype(WIDE)).astype(LOW)
 
 
 def add_up(total, term):
@@ -520,13 +535,6 @@
     return pieces
 
 
-def vector_totals(vectors):
-    flat = jnp.concatenate([v.reshape(-1) for v in vectors])
-    part = collect(flat.reshape(16, -1, 128), COLS)
-    part = jnp.sum(spread(part, ROWS, 8), 0)
-    return split_back(spread(part, COLS, 16).reshape(-1), vectors)
-
-
 def short_totals(vectors, columns):
     shared = jnp.concatenate([v.reshape(-1, 128) for v in vectors], 0)
     rows = shared.shape[0]
@@ -570,7 +578,8 @@
     norm1 = ring_gather(normed1.astype(LOW))
     grad_y = cotangent.astype(WIDE).reshape(own, width)
     g_ffn = (keep * grad_y).astype(LOW)
-    cot_rows = ring_gather(after(g_ffn, norm1))
+    norm1, g_ffn = tie(norm1, g_ffn)
+    norm1, cot_rows = tie(norm1, ring_gather(g_ffn))
 
     def mine(vector, cols):
         return lax.dynamic_index_in_dim(vector.reshape(RING, RING, cols), y_at, 1, False)
@@ -578,7 +587,7 @@
     bias = jnp.concatenate(
         [mine(q_bias, head_cols), jnp.zeros((RING, head_cols), WIDE), mine(v_bias, head_cols)], 1
     ).reshape(RING, 1, 3 * head_cols)
-    qkv = qkv_project(after(norm1, cot_rows), w_qkv, bias)
+    qkv = qkv_project(norm1, w_qkv, bias)
     rows5 = (RING, RING, seqs, own_rows)
     qkv = swap(qkv, "x").reshape(rows5 + (3 * head_cols,))
     heads, exact, logs = attend(live_counts, qkv, head_cols)
@@ -590,37 +599,46 @@
 
     ff_bias = mine(up_bias, ff_cols).reshape(RING, 1, ff_cols)
     hidden, grad_up, g_norm2, up_bias_part = ffn_first(norm2, cot_rows, w_ff, ff_bias)
-    g_norm2 = ring_sum(g_norm2)
     branch2, ff_grad = ffn_second(norm2, cot_rows, hidden, grad_up, w_ff)
+    g_norm2, (branch2, ff_grad) = ring_sum(g_norm2, (branch2, ff_grad))
     ff_grad = settle(ff_grad)
     grad_mid = grad_y + norm_back(g_norm2, unit2, inverse2, ln2_gain)
     g_attn = (keep * grad_mid).astype(LOW)
-    attn_rows = ring_gather(g_attn)
-    branch2 = ring_sum(after(branch2, attn_rows)) + down_bias
-    result = (middle + keep * branch2).astype(LOW).reshape(tokens.shape)
-    g_heads = swap(heads_grad(attn_rows, w_out), "x").reshape(rows5 + (head_cols,))
-    d_qkv, d_sums = attend_back(live_counts, qkv, g_heads, exact, logs)
-    d_qkv = swap(d_qkv.reshape(RING, RING * own, 3 * head_cols), "x")
-
-    kept, sent = weight_grads(core_at, norm1, d_qkv, attn_rows, heads)
-    other = lax.ppermute(sent, "c", [(0, 1), (1, 0)])
-    g_norm1 = ring_sum(out_project(after(d_qkv, sent), w_qkv))
-    both = (kept.astype(WIDE) + other.astype(WIDE)).astype(LOW)
-    small_grad = collect(both.reshape((16,) + both.shape[2:]), ("z", "x"))
-    grad_tokens = (grad_mid + norm_back(g_norm1, unit1, inverse1, ln1_gain)).reshape(tokens.shape)
-
     up_bias_full = lax.dynamic_update_slice_in_dim(
         jnp.zeros((RING, RING, ff_cols), WIDE), up_bias_part.reshape(RING, 1, ff_cols), y_at, 1
     )
-    out_bias_sum, ln2_gain_sum, ln2_shift_sum, up_bias_sum, down_bias_sum = vector_totals(
-        (
-            jnp.sum(g_attn.astype(WIDE), 0),
-            jnp.sum(g_norm2 * unit2, 0),
-            jnp.sum(g_norm2, 0),
-            up_bias_full,
-            jnp.sum(g_ffn.astype(WIDE), 0),
-        )
-    )
+    early = (
+        jnp.sum(g_attn.astype(WIDE), 0),
+        jnp.sum(g_norm2 * unit2, 0),
+        jnp.sum(g_norm2, 0),
+        up_bias_full,
+        jnp.sum(g_ffn.astype(WIDE), 0),
+    )
+    part = collect(jnp.concatenate([v.reshape(-1) for v in early]).reshape(16, -1, 128), COLS)
+    attn_rows = ring_gather(g_attn)
+    attn_rows, part = tie(attn_rows, part)
+    g_heads = swap(heads_grad(attn_rows, w_out), "x").reshape(rows5 + (head_cols,))
+    part = jnp.sum(spread(part, ROWS, 8), 0)
+    g_heads, part = tie(g_heads, part)
+    early_totals = spread(part, COLS, 16).reshape(-1)
+    d_qkv, d_sums = attend_back(live_counts, qkv, g_heads, exact, logs)
+    d_qkv, early_totals, attn_rows, branch2 = tie(d_qkv, early_totals, attn_rows, branch2)
+    out_bias_sum, ln2_gain_sum, ln2_shift_sum, up_bias_sum, down_bias_sum = split_back(
+        early_totals, early
+    )
+    out_both = core_sum(*weight_grads(core_at, attn_rows, heads))
+    branch2 = ring_sum(branch2) + down_bias
+    result = (middle + keep * branch2).astype(LOW).reshape(tokens.shape)
+    d_qkv = swap(d_qkv.reshape(RING, RING * own, 3 * head_cols), "x")
+    d_qkv, out_both, result = tie(d_qkv, out_both, result)
+
+    kept, sent = weight_grads(core_at, norm1, d_qkv)
+    d_qkv, kept, sent = tie(d_qkv, kept, sent)
+    g_norm1 = out_project(d_qkv, w_qkv)
+    both = jnp.concatenate([core_sum(kept, sent), out_both], 3)
+    g_norm1, both = tie(g_norm1, both)
+    small_grad, g_norm1 = cube_collect(both, ring_sum(g_norm1))
+    grad_tokens = (grad_mid + norm_back(g_norm1, unit1, inverse1, ln1_gain)).reshape(tokens.shape)
     d_sums = jnp.sum(d_sums, 0).reshape(3, head_cols)
     ln1_gain_sum, ln1_shift_sum, q_bias_sum, v_bias_sum = short_totals(
         (jnp.sum(g_norm1 * unit1, 0), jnp.sum(g_norm1, 0)), d_sums[::2]

time: 535 us -> 500 us (0.935)
  waiting for transfers between devices: 220 us -> 155 us
  starting transfers between devices: 115 us -> 137 us
  local copies, waits for them, and re-layouts: 48.4 us -> 56.8 us
    all_to_all x2 -> x1, waiting for transfers between devices: 63.7 us -> 3.77 us  [collect(): return jnp.sum(lax.all_to_all(parts, axes, 0, 0).astype(WIDE), 0)]
    ppermute x49 -> x62, starting transfers between devices: 58.7 us -> 84 us  [the longest x60 72.1 us: ring(): lax.ppermute(array, axis, [(i, (i + step) % RING) for i in range(RING)])]
    reduce_scatter x1, starting transfers between devices: 12.9 us -> 0.51 us  [settle(): lax.psum_scatter(gradient.reshape((32,) + gradient.shape[2:]), ('z', 'c',...]
    all_to_all x4, waiting for transfers between devices: 17 us -> 4.67 us  [spread(): lax.all_to_all(jnp.broadcast_to(array[None], (size,) + array.shape), axes...]
    all_to_all x4, starting transfers between devices: 19.4 us -> 30.5 us  [spread(): lax.all_to_all(jnp.broadcast_to(array[None], (size,) + array.shape), axes...]
    unnamed x117 -> x99, local copies, waits for them, and re-layouts: 30.5 us -> 37.4 us
    pallas_call x1 -> x2, Pallas kernels: 10.7 us -> 10.8 us  [weight_grads(): call(weight_grad_body, (half, half), (xs,), [whole((count, width)), pl.Bl...]
    ppermute x49 -> x62, waiting for transfers between devices: 77 us -> 76.8 us  [the longest x60 76.7 us: ring(): lax.ppermute(array, axis, [(i, (i + step) % RING) for i in range(RING)])]
  transfers between devices with their start and end apart: 63 -> 75, of which waited for: 38 -> 35; matrix products, arithmetic and copies ran while one was open for 12% -> 14% of each run, Pallas kernels for 9% -> 14%
where the time goes in v3:
time: 500 us; the launch traced here: 492 us
  waiting for transfers between devices  155 us (31%)
  starting transfers between devices  137 us (27%)
  Pallas kernels  89.7 us (18%)
  local copies, waits for them, and re-layouts  56.8 us (11%)
  other arithmetic  37.4 us (7%)
  between operations  15.7 us (3%)
    ppermute x60, waiting for transfers between devices, ring(): lax.ppermute(array, axis, [(i, (i + step) % RING) for i in range(RING)])  76.7 us
    ppermute x60, starting transfers between devices, ring(): lax.ppermute(array, axis, [(i, (i + step) % RING) for i in range(RING)])  72.1 us
    all_to_all x4, waiting for transfers between devices, swap(): return lax.all_to_all(parts, axes, 0, 0)  48.2 us
    unnamed x99, local copies, waits for them, and re-layouts  37.4 us
    all_to_all x4, starting transfers between devices, spread(): lax.all_to_all(jnp.broadcast_to(array[None], (size,) + array.shape), axes...  30.5 us
    all_gather x3, waiting for transfers between devices, gather_weight(): full = lax.all_gather(shard, ('z', 'c', 'x'), axis=0)  21.8 us
    pallas_call x1, Pallas kernels, ffn_second(): call(ffn_second_body, (struct((count, width), LOW), struct(weight.shape,...  21.4 us
    pallas_call x1, Pallas kernels, ffn_first(): call(ffn_first_body, (struct((count, xs * size), LOW), struct((count, xs...  20.7 us
  transfers between devices with their start and end apart: 75, of which 35 were waited for; matrix products, arithmetic and copies ran while one was open for 14% of the time, Pallas kernels for 14%

profile of v3, /device:TPU:1, one launch (start us, length us, event | category | flops | bytes accessed | tf_op | source)
XLA Modules:
  0.0 491.6 jit_solution(15333103872670305164)
XLA Ops:
  15.5 3.6 collective-permute-start.3
  24.8 2.9 collective-permute-start.5
  27.7 5.4 %collective-permute-done = bf16[64,2048]{1,0:T(8,128)(2,1)} collective-permute-done((bf16[64,2048]{1,0:T(8,128)(2,1)}, bf16[64,2048]{1,0:T(8,128)(2,1)}, u32[]{:S(2)}, u32[]{:S(2)}) %collective-permute-start) | collective-permute-done | bytes 262176 | tf_op jit(solution)/shard_map/ppermute | solution.py:69
  36.1 4.4 collective-permute-done.4
  48.3 4.3 collective-permute-done.7
  54.8 3.5 collective-permute-done.10
  59.7 4.0 all-gather.5.cloned.1.call-done
  66.5 6.4 %shard_map.323 = bf16[4,512,384]{2,1,0:T(8,128)(2,1)} custom-call(bf16[512,2048]{1,0:T(8,128)(2,1)S(1)} %constant_dynamic-update-slice_fusion.rows_ref, bf16[8,4,256,384]{3,2,1,0:T(8,128)(2,1)S(1)} %bitcast.132, f32[4,1,384]{2,1,0:T(1,128)S(1)} %reshape.451.bias_ref), custom_call_target="tpu_custom_call" | custom-call | flops 3221225472 | bytes 10485760 | tf_op jit(solution)/shard_map/pallas_call | solution.py:146
  73.0 3.6 all-to-all-start
  76.6 21.1 %all-to-all-done = bf16[4,512,384]{2,1,0:T(8,128)(2,1)S(1)} async-done(((bf16[4,512,384]{2,1,0:T(8,128)(2,1)}), bf16[4,512,384]{2,1,0:T(8,128)(2,1)S(1)}, u32[]{:S(2)}, u32[]{:S(2)}) %all-to-all-start) | async-done | bytes 1572896 | tf_op jit(solution)/shard_map/all_to_all | solution.py:65
  97.7 7.2 %shard_map.324 = (bf16[4,4,2,64,128]{4,3,2,1,0:T(8,128)(2,1)}, f32[2,1024,128]{2,1,0:T(8,128)S(1)}, f32[2,1024,128]{2,1,0:T(8,128)S(1)}) custom-call(s32[3]{0:T(128)S(1)} %pad_add_fusion.live_ref, bf16[4,4,2,64,384]{4,3,2,1,0:T(8,128)(2,1)S(1)} %bitcast.128), custom_call_target="tpu_custom_call" | custom-call | flops 4000000000 | bytes 4194304 | tf_op jit(solution)/shard_map/pallas_call | solution.py:414
  106.9 3.5 all-to-all-start.1
  110.9 7.5 %all-to-all-done.1.heads_ref.grad_ref = bf16[4,512,128]{2,1,0:T(8,128)(2,1)S(1)} async-done(((bf16[4,512,128]{2,1,0:T(8,128)(2,1)}), bf16[4,512,128]{2,1,0:T(8,128)(2,1)S(1)}, u32[]{:S(2)}, u32[]{:S(2)}) %all-to-all-start.1) | async-done | bytes 524320 | tf_op jit(solution)/shard_map/all_to_all | solution.py:65
  120.0 2.9 shard_map.325
  127.1 2.8 collective-permute-done.12
  131.4 3.8 collective-permute-done.14
  138.0 3.5 collective-permute-done.15
  152.6 3.0 collective-permute-start.23
  160.5 4.8 collective-permute-done.22
  166.8 17.7 %all-gather.7.cloned.1.call-done = bf16[32,256,1024]{2,1,0:T(8,128)(2,1)} async-done(((bf16[1,256,1024]{2,1,0:T(8,128)(2,1)}), bf16[32,256,1024]{2,1,0:T(8,128)(2,1)}) %all-gather.7.cloned.1.call-update) | async-done | bytes 16777232 | tf_op jit(solution)/shard_map/all_gather | solution.py:127
  184.5 20.7 %shard_map.326 = (bf16[512,2048]{1,0:T(8,128)(2,1)}, bf16[512,2048]{1,0:T(8,128)(2,1)}, bf16[512,2048]{1,0:T(8,128)(2,1)}, f32[4,1,512]{2,1,0:T(1,128)}) custom-call(bf16[512,2048]{1,0:T(8,128)(2,1)} %constant_dynamic-update-slice_fusion.14.norm_ref, bf16[512,2048]{1,0:T(8,128)(2,1)} %constant_dynamic-update-slice_fusion.7.cot_ref, ...), custom_call_target="tpu_custom_call" | custom-call | flops 12884901888 | bytes 26214400 | tf_op jit(solution)/shard_map/pallas_call | solution.py:278
  214.5 3.1 collective-permute-done.24
  220.5 21.4 %shard_map.327 = (bf16[512,2048]{1,0:T(8,128)(2,1)}, bf16[8,4,256,1024]{3,2,1,0:T(8,128)(2,1)}) custom-call(bf16[512,2048]{1,0:T(8,128)(2,1)} %constant_dynamic-update-slice_fusion.14.norm_ref, bf16[512,2048]{1,0:T(8,128)(2,1)} %constant_dynamic-update-slice_fusion.7.cot_ref, bf16[512,2048]{1,0:T(8,128)(2,1)} %get-tuple-element.67.hidden_ref, ...), custom_call_target="tpu_custom_call" | custom-call | flops 12884901888 | bytes 41943040 | tf_op jit(solution)/shard_map/pallas_call | solution.py:325
  245.1 3.3 constant_dynamic-update-slice_fusion.27
  254.5 6.5 %all-to-all-start.2 = ((f32[16,8,128]{2,1,0:T(8,128)}), f32[16,8,128]{2,1,0:T(8,128)S(1)}, u32[]{:S(2)}, u32[]{:S(2)}) async-start(f32[16,8,128]{2,1,0:T(8,128)} %bitcast.20), calls=%async_computation.2 | async-start | bytes 131072 | tf_op jit(solution)/shard_map/all_to_all | solution.py:61
  263.8 3.8 all-to-all-done.2
  277.1 9.1 %all-to-all-start.4 = ((f32[8,8,128]{2,1,0:T(8,128)}), f32[8,8,128]{2,1,0:T(8,128)S(1)}, u32[]{:S(2)}, u32[]{:S(2)}) async-start(f32[8,8,128]{2,1,0:T(8,128)} %broadcast_in_dim.14), calls=%async_computation.4 | async-start | bytes 65536 | tf_op jit(solution)/shard_map/all_to_all | solution.py:57
  287.8 3.7 shard_map.328
  291.5 3.5 all-to-all-start.3
  295.0 15.2 %all-to-all-done.3 = bf16[4,512,128]{2,1,0:T(8,128)(2,1)S(1)} async-done(((bf16[4,512,128]{2,1,0:T(8,128)(2,1)}), bf16[4,512,128]{2,1,0:T(8,128)(2,1)S(1)}, u32[]{:S(2)}, u32[]{:S(2)}) %all-to-all-start.3) | async-done | bytes 524320 | tf_op jit(solution)/shard_map/all_to_all | solution.py:65
  310.8 3.7 all-to-all-start.5
  318.4 10.0 %shard_map.329 = (bf16[4,4,2,64,384]{4,3,2,1,0:T(8,128)(2,1)S(1)}, f32[2,1,384]{2,1,0:T(1,128)S(1)}) custom-call(s32[3]{0:T(128)S(1)} %pad_add_fusion.live_ref, bf16[4,4,2,64,384]{4,3,2,1,0:T(8,128)(2,1)S(1)} %bitcast.129, bf16[4,4,2,64,128]{4,3,2,1,0:T(8,128)(2,1)S(1)} %bitcast.131, f32[2,1024,128]{2,1,0:T(8,128)S(1)} %copy-done.12, ...), custom_call_target="tpu_custom_call" | custom-call | flops 8000000000 | bytes 8388608 | tf_op jit(solution)/shard_map/pallas_call | solution.py:491
  335.8 3.8 collective-permute-done.37
  341.4 3.8 collective-permute-done.39
  349.9 4.5 all-to-all-start.6
  354.4 3.4 shard_map.330
  357.8 6.0 %collective-permute-start.36 = (bf16[4,4,256,128]{3,2,1,0:T(8,128)(2,1)S(1)}, bf16[4,4,256,128]{3,2,1,0:T(8,128)(2,1)S(1)}, u32[]{:S(2)}, u32[]{:S(2)}) collective-permute-start(bf16[4,4,256,128]{3,2,1,0:T(8,128)(2,1)S(1)} %get-tuple-element.87), channel_id=1, source_target_pairs={{0,16},{16,0},{1,17},{17,1},{2,18},{18,2},{3,19},{19,3},{4,20},{20... | collective-permute-start | bytes 3145736 | tf_op jit(solution)/shard_map/ppermute | solution.py:237
  367.3 4.5 all-to-all-done.6.grad_ref.heads_ref
  373.4 7.4 %shard_map.331 = (bf16[4,4,256,384]{3,2,1,0:T(8,128)(2,1)S(1)}, bf16[4,4,256,384]{3,2,1,0:T(8,128)(2,1)}) custom-call(s32[1]{0:T(128)} %bitcast.24.place_ref, bf16[512,2048]{1,0:T(8,128)(2,1)S(1)} %copy-done.8, bf16[4,512,384]{2,1,0:T(8,128)(2,1)} %all-to-all-done.6.grad_ref.heads_ref), custom_call_target="tpu_custom_call" | custom-call | flops 3221225472 | bytes 15728640 | tf_op jit(solution)/shard_map/pallas_call | solution.py:224
  380.8 6.0 %collective-permute-start.43 = (bf16[4,4,256,384]{3,2,1,0:T(8,128)(2,1)}, bf16[4,4,256,384]{3,2,1,0:T(8,128)(2,1)}, u32[]{:S(2)}, u32[]{:S(2)}) collective-permute-start(bf16[4,4,256,384]{3,2,1,0:T(8,128)(2,1)} %get-tuple-element.95), channel_id=1, source_target_pairs={{0,16},{16,0},{1,17},{17,1},{2,18},{18,2},{3,19},{19,3},{4,20},{20... | collective-permute-start | bytes 9437192 | tf_op jit(solution)/shard_map/ppermute | solution.py:237
  389.6 6.6 %shard_map.332 = bf16[512,2048]{1,0:T(8,128)(2,1)S(1)} custom-call(bf16[4,512,384]{2,1,0:T(8,128)(2,1)} %all-to-all-done.6.grad_ref.heads_ref, bf16[8,4,256,384]{3,2,1,0:T(8,128)(2,1)S(1)} %bitcast.133), custom_call_target="tpu_custom_call" | custom-call | flops 3221225472 | bytes 5242880 | tf_op jit(solution)/shard_map/pallas_call | solution.py:173
  396.2 3.0 add_convert_fusion
  404.4 4.5 collective-permute-done.50
  419.3 5.6 %collective-permute-start.45 = (bf16[4,128,512]{2,1,0:T(8,128)(2,1)S(1)}, bf16[4,128,512]{2,1,0:T(8,128)(2,1)S(1)}, u32[]{:S(2)}, u32[]{:S(2)}) collective-permute-start(bf16[4,128,512]{2,1,0:T(8,128)(2,1)S(1)} %get-tuple-element.134), channel_id=1, source_target_pairs={{0,64},{32,96},{64,0},{96,32},{1,65},{33,97},{65,1},{97,33},{2,66}... | collective-permute-start | bytes 1572872 | tf_op jit(solution)/shard_map/ppermute | solution.py:69
  431.2 8.2 %collective-permute-done.45 = bf16[4,128,512]{2,1,0:T(8,128)(2,1)S(1)} collective-permute-done((bf16[4,128,512]{2,1,0:T(8,128)(2,1)S(1)}, bf16[4,128,512]{2,1,0:T(8,128)(2,1)S(1)}, u32[]{:S(2)}, u32[]{:S(2)}) %collective-permute-start.45) | collective-permute-done | bytes 524320 | tf_op jit(solution)/shard_map/ppermute | solution.py:69
  442.7 9.1 %all-to-all-start.7 = ((f32[16,34,128]{2,1,0:T(8,128)}), f32[16,34,128]{2,1,0:T(8,128)S(1)}, u32[]{:S(2)}, u32[]{:S(2)}) async-start(f32[16,34,128]{2,1,0:T(8,128)} %broadcast_in_dim.16), calls=%async_computation.7 | async-start | bytes 655360 | tf_op jit(solution)/shard_map/all_to_all | solution.py:57
  466.0 8.6 %all-to-all-start.8 = ((f32[8,64,128]{2,1,0:T(8,128)}), f32[8,64,128]{2,1,0:T(8,128)S(1)}, u32[]{:S(2)}, u32[]{:S(2)}) async-start(f32[8,64,128]{2,1,0:T(8,128)} %broadcast_in_dim.17), calls=%async_computation.8 | async-start | bytes 524288 | tf_op jit(solution)/shard_map/all_to_all | solution.py:57
  476.5 4.7 all-to-all-done.8
  (324 shorter events, 166.7 us)
Async XLA Ops:
  7.2 56.6 %all-gather.5.cloned.1.call-start = ((), (), s32[]{:S(2)}) async-start(), calls=%async_computation.10 | async-start | bytes 6488064 | tf_op jit(solution)/shard_map/all_gather | solution.py:127
  9.9 101.0 %all-gather.9.cloned.1.call-start = ((), (), s32[]{:S(2)}) async-start(), calls=%async_computation.13 | async-start | bytes 2162688 | tf_op jit(solution)/shard_map/all_gather | solution.py:127
  11.5 173.0 %all-gather.7.cloned.1.call-start = ((), (), s32[]{:S(2)}) async-start(), calls=%async_computation.11 | async-start | bytes 17301504 | tf_op jit(solution)/shard_map/all_gather | solution.py:127
  19.1 15.0 %collective-permute-start.1 = (bf16[64,2048]{1,0:T(8,128)(2,1)}, bf16[64,2048]{1,0:T(8,128)(2,1)}, u32[]{:S(2)}, u32[]{:S(2)}) collective-permute-start(bf16[64,2048]{1,0:T(8,128)(2,1)} %get-tuple-element.175), channel_id=1, source_target_pairs={{0,1},{1,2},{2,3},{3,0},{4,5},{5,6},{6,7},{7,4},{8,9},{9,10},{10,1... | collective-permute-start | bytes 786440 | tf_op jit(solution)/shard_map/ppermute | solution.py:69
  19.1 16.0 %collective-permute-start.2 = (bf16[64,2048]{1,0:T(8,128)(2,1)}, bf16[64,2048]{1,0:T(8,128)(2,1)}, u32[]{:S(2)}, u32[]{:S(2)}) collective-permute-start(bf16[64,2048]{1,0:T(8,128)(2,1)} %get-tuple-element.176), channel_id=1, source_target_pairs={{0,3},{1,0},{2,1},{3,2},{4,7},{5,4},{6,5},{7,6},{8,11},{9,8},{10,9... | collective-permute-start | bytes 786440 | tf_op jit(solution)/shard_map/ppermute | solution.py:69
  21.8 11.3 %collective-permute-start = (bf16[64,2048]{1,0:T(8,128)(2,1)}, bf16[64,2048]{1,0:T(8,128)(2,1)}, u32[]{:S(2)}, u32[]{:S(2)}) collective-permute-start(bf16[64,2048]{1,0:T(8,128)(2,1)} %get-tuple-element.176), channel_id=1, source_target_pairs={{0,1},{1,2},{2,3},{3,0},{4,5},{5,6},{6,7},{7,4},{8,9},{9,10},{10,1... | collective-permute-start | bytes 786440 | tf_op jit(solution)/shard_map/ppermute | solution.py:69
  24.8 15.7 %collective-permute-start.5 = (bf16[64,2048]{1,0:T(8,128)(2,1)S(1)}, bf16[64,2048]{1,0:T(8,128)(2,1)S(1)}, u32[]{:S(2)}, u32[]{:S(2)}) collective-permute-start(bf16[64,2048]{1,0:T(8,128)(2,1)S(1)} %collective-permute-done.3), channel_id=1, source_target_pairs={{0,3},{1,0},{2,1},{3,2},{4,7},{5,4},{6,5},{7,6},{8,11},{9,8},{10,9... | collective-permute-start | bytes 786440 | tf_op jit(solution)/shard_map/ppermute | solution.py:69
  42.1 10.5 %collective-permute-start.7 = (bf16[64,2048]{1,0:T(8,128)(2,1)S(1)}, bf16[64,2048]{1,0:T(8,128)(2,1)S(1)}, u32[]{:S(2)}, u32[]{:S(2)}) collective-permute-start(bf16[64,2048]{1,0:T(8,128)(2,1)S(1)} %get-tuple-element.173), channel_id=1, source_target_pairs={{0,1},{1,2},{2,3},{3,0},{4,5},{5,6},{6,7},{7,4},{8,9},{9,10},{10,1... | collective-permute-start | bytes 786440 | tf_op jit(solution)/shard_map/ppermute | solution.py:69
  42.2 11.2 %collective-permute-start.8 = (bf16[64,2048]{1,0:T(8,128)(2,1)S(1)}, bf16[64,2048]{1,0:T(8,128)(2,1)S(1)}, u32[]{:S(2)}, u32[]{:S(2)}) collective-permute-start(bf16[64,2048]{1,0:T(8,128)(2,1)S(1)} %get-tuple-element.174), channel_id=1, source_target_pairs={{0,3},{1,0},{2,1},{3,2},{4,7},{5,4},{6,5},{7,6},{8,11},{9,8},{10,9... | collective-permute-start | bytes 786440 | tf_op jit(solution)/shard_map/ppermute | solution.py:69
  45.8 13.1 %collective-permute-start.11 = (bf16[64,2048]{1,0:T(8,128)(2,1)S(1)}, bf16[64,2048]{1,0:T(8,128)(2,1)S(1)}, u32[]{:S(2)}, u32[]{:S(2)}) collective-permute-start(bf16[64,2048]{1,0:T(8,128)(2,1)S(1)} %collective-permute-done.9), channel_id=1, source_target_pairs={{0,3},{1,0},{2,1},{3,2},{4,7},{5,4},{6,5},{7,6},{8,11},{9,8},{10,9... | collective-permute-start | bytes 786440 | tf_op jit(solution)/shard_map/ppermute | solution.py:69
  47.1 11.1 %collective-permute-start.10 = (bf16[64,2048]{1,0:T(8,128)(2,1)S(1)}, bf16[64,2048]{1,0:T(8,128)(2,1)S(1)}, u32[]{:S(2)}, u32[]{:S(2)}) collective-permute-start(bf16[64,2048]{1,0:T(8,128)(2,1)S(1)} %collective-permute-done.6), channel_id=1, source_target_pairs={{0,1},{1,2},{2,3},{3,0},{4,5},{5,6},{6,7},{7,4},{8,9},{9,10},{10,1... | collective-permute-start | bytes 786440 | tf_op jit(solution)/shard_map/ppermute | solution.py:69
  73.0 24.7 %all-to-all-start = ((bf16[4,512,384]{2,1,0:T(8,128)(2,1)}), bf16[4,512,384]{2,1,0:T(8,128)(2,1)S(1)}, u32[]{:S(2)}, u32[]{:S(2)}) async-start(bf16[4,512,384]{2,1,0:T(8,128)(2,1)} %shard_map.323), calls=%async_computation | async-start | bytes 3145728 | tf_op jit(solution)/shard_map/all_to_all | solution.py:65
  106.9 11.5 %all-to-all-start.1 = ((bf16[4,512,128]{2,1,0:T(8,128)(2,1)}), bf16[4,512,128]{2,1,0:T(8,128)(2,1)S(1)}, u32[]{:S(2)}, u32[]{:S(2)}) async-start(bf16[4,512,128]{2,1,0:T(8,128)(2,1)} %bitcast.13), calls=%async_computation.1 | async-start | bytes 1048576 | tf_op jit(solution)/shard_map/all_to_all | solution.py:65
  110.4 372.1 %reduce-scatter.2.cloned.1.call-start = ((), (), s32[]{:S(2)}) async-start(), calls=%async_computation.12 | async-start | bytes 17301504 | tf_op jit(solution)/shard_map/reduce_scatter | solution.py:132
  130.2 11.3 %collective-permute-start.15 = (bf16[64,2048]{1,0:T(8,128)(2,1)S(1)}, bf16[64,2048]{1,0:T(8,128)(2,1)S(1)}, u32[]{:S(2)}, u32[]{:S(2)}) collective-permute-start(bf16[64,2048]{1,0:T(8,128)(2,1)S(1)} %get-tuple-element.153), channel_id=1, source_target_pairs={{0,1},{1,2},{2,3},{3,0},{4,5},{5,6},{6,7},{7,4},{8,9},{9,10},{10,1... | collective-permute-start | bytes 786440 | tf_op jit(solution)/shard_map/ppermute | solution.py:69
  149.2 9.8 %collective-permute-start.20 = (bf16[64,2048]{1,0:T(8,128)(2,1)}, bf16[64,2048]{1,0:T(8,128)(2,1)S(1)}, u32[]{:S(2)}, u32[]{:S(2)}) collective-permute-start(bf16[64,2048]{1,0:T(8,128)(2,1)} %get-tuple-element.172), channel_id=1, source_target_pairs={{0,3},{1,0},{2,1},{3,2},{4,7},{5,4},{6,5},{7,6},{8,11},{9,8},{10,9... | collective-permute-start | bytes 786440 | tf_op jit(solution)/shard_map/ppermute | solution.py:69
  152.6 13.5 %collective-permute-start.23 = (bf16[64,2048]{1,0:T(8,128)(2,1)S(1)}, bf16[64,2048]{1,0:T(8,128)(2,1)S(1)}, u32[]{:S(2)}, u32[]{:S(2)}) collective-permute-start(bf16[64,2048]{1,0:T(8,128)(2,1)S(1)} %collective-permute-done.21), channel_id=1, source_target_pairs={{0,3},{1,0},{2,1},{3,2},{4,7},{5,4},{6,5},{7,6},{8,11},{9,8},{10,9... | collective-permute-start | bytes 786440 | tf_op jit(solution)/shard_map/ppermute | solution.py:69
  209.1 32.8 %collective-permute-start.27 = (bf16[64,2048]{1,0:T(8,128)(2,1)S(1)}, bf16[64,2048]{1,0:T(8,128)(2,1)S(1)}, u32[]{:S(2)}, u32[]{:S(2)}) collective-permute-start(bf16[64,2048]{1,0:T(8,128)(2,1)S(1)} %get-tuple-element.146), channel_id=1, source_target_pairs={{0,1},{1,2},{2,3},{3,0},{4,5},{5,6},{6,7},{7,4},{8,9},{9,10},{10,1... | collective-permute-start | bytes 786440 | tf_op jit(solution)/shard_map/ppermute | solution.py:69
  209.3 32.6 %collective-permute-start.26 = (bf16[64,2048]{1,0:T(8,128)(2,1)S(1)}, bf16[64,2048]{1,0:T(8,128)(2,1)S(1)}, u32[]{:S(2)}, u32[]{:S(2)}) collective-permute-start(bf16[64,2048]{1,0:T(8,128)(2,1)S(1)} %get-tuple-element.147), channel_id=1, source_target_pairs={{0,3},{1,0},{2,1},{3,2},{4,7},{5,4},{6,5},{7,6},{8,11},{9,8},{10,9... | collective-permute-start | bytes 786440 | tf_op jit(solution)/shard_map/ppermute | solution.py:69
  218.8 23.1 %collective-permute-start.29 = (bf16[64,2048]{1,0:T(8,128)(2,1)S(1)}, bf16[64,2048]{1,0:T(8,128)(2,1)S(1)}, u32[]{:S(2)}, u32[]{:S(2)}) collective-permute-start(bf16[64,2048]{1,0:T(8,128)(2,1)S(1)} %get-tuple-element.143), channel_id=1, source_target_pairs={{0,3},{1,0},{2,1},{3,2},{4,7},{5,4},{6,5},{7,6},{8,11},{9,8},{10,9... | collective-permute-start | bytes 786440 | tf_op jit(solution)/shard_map/ppermute | solution.py:69
  219.2 22.8 %collective-permute-start.25 = (bf16[64,2048]{1,0:T(8,128)(2,1)S(1)}, bf16[64,2048]{1,0:T(8,128)(2,1)}, u32[]{:S(2)}, u32[]{:S(2)}) collective-permute-start(bf16[64,2048]{1,0:T(8,128)(2,1)S(1)} %get-tuple-element.144), channel_id=1, source_target_pairs={{0,1},{1,2},{2,3},{3,0},{4,5},{5,6},{6,7},{7,4},{8,9},{9,10},{10,1... | collective-permute-start | bytes 786440 | tf_op jit(solution)/shard_map/ppermute | solution.py:69
  249.3 18.3 %collective-permute-start.33 = (bf16[64,2048]{1,0:T(8,128)(2,1)}, bf16[64,2048]{1,0:T(8,128)(2,1)S(1)}, u32[]{:S(2)}, u32[]{:S(2)}) collective-permute-start(bf16[64,2048]{1,0:T(8,128)(2,1)} %get-tuple-element.169), channel_id=1, source_target_pairs={{0,3},{1,0},{2,1},{3,2},{4,7},{5,4},{6,5},{7,6},{8,11},{9,8},{10,9... | collective-permute-start | bytes 786440 | tf_op jit(solution)/shard_map/ppermute | solution.py:69
  250.8 17.8 %collective-permute-start.30 = (bf16[64,2048]{1,0:T(8,128)(2,1)}, bf16[64,2048]{1,0:T(8,128)(2,1)S(1)}, u32[]{:S(2)}, u32[]{:S(2)}) collective-permute-start(bf16[64,2048]{1,0:T(8,128)(2,1)} %get-tuple-element.170), channel_id=1, source_target_pairs={{0,1},{1,2},{2,3},{3,0},{4,5},{5,6},{6,7},{7,4},{8,9},{9,10},{10,1... | collective-permute-start | bytes 786440 | tf_op jit(solution)/shard_map/ppermute | solution.py:69
  254.5 13.0 %all-to-all-start.2 = ((f32[16,8,128]{2,1,0:T(8,128)}), f32[16,8,128]{2,1,0:T(8,128)S(1)}, u32[]{:S(2)}, u32[]{:S(2)}) async-start(f32[16,8,128]{2,1,0:T(8,128)} %bitcast.20), calls=%async_computation.2 | async-start | bytes 131072 | tf_op jit(solution)/shard_map/all_to_all | solution.py:61
  277.1 14.4 %all-to-all-start.4 = ((f32[8,8,128]{2,1,0:T(8,128)}), f32[8,8,128]{2,1,0:T(8,128)S(1)}, u32[]{:S(2)}, u32[]{:S(2)}) async-start(f32[8,8,128]{2,1,0:T(8,128)} %broadcast_in_dim.14), calls=%async_computation.4 | async-start | bytes 65536 | tf_op jit(solution)/shard_map/all_to_all | solution.py:57
  291.5 18.7 %all-to-all-start.3 = ((bf16[4,512,128]{2,1,0:T(8,128)(2,1)}), bf16[4,512,128]{2,1,0:T(8,128)(2,1)S(1)}, u32[]{:S(2)}, u32[]{:S(2)}) async-start(bf16[4,512,128]{2,1,0:T(8,128)(2,1)} %shard_map.328), calls=%async_computation.3 | async-start | bytes 1048576 | tf_op jit(solution)/shard_map/all_to_all | solution.py:65
  310.8 18.8 %all-to-all-start.5 = ((f32[16,8,128]{2,1,0:T(8,128)}), f32[16,8,128]{2,1,0:T(8,128)S(1)}, u32[]{:S(2)}, u32[]{:S(2)}) async-start(f32[16,8,128]{2,1,0:T(8,128)} %broadcast_in_dim.15), calls=%async_computation.5 | async-start | bytes 131072 | tf_op jit(solution)/shard_map/all_to_all | solution.py:57
  334.3 10.9 %collective-permute-start.39 = (bf16[64,2048]{1,0:T(8,128)(2,1)S(1)}, bf16[64,2048]{1,0:T(8,128)(2,1)S(1)}, u32[]{:S(2)}, u32[]{:S(2)}) collective-permute-start(bf16[64,2048]{1,0:T(8,128)(2,1)S(1)} %get-tuple-element.140), channel_id=1, source_target_pairs={{0,3},{1,0},{2,1},{3,2},{4,7},{5,4},{6,5},{7,6},{8,11},{9,8},{10,9... | collective-permute-start | bytes 786440 | tf_op jit(solution)/shard_map/ppermute | solution.py:69
  341.0 22.7 %collective-permute-start.40 = (bf16[64,2048]{1,0:T(8,128)(2,1)}, bf16[64,2048]{1,0:T(8,128)(2,1)S(1)}, u32[]{:S(2)}, u32[]{:S(2)}) collective-permute-start(bf16[64,2048]{1,0:T(8,128)(2,1)} %get-tuple-element.139), channel_id=1, source_target_pairs={{0,1},{1,2},{2,3},{3,0},{4,5},{5,6},{6,7},{7,4},{8,9},{9,10},{10,1... | collective-permute-start | bytes 786440 | tf_op jit(solution)/shard_map/ppermute | solution.py:69
  349.9 13.9 %collective-permute-start.42 = (bf16[64,2048]{1,0:T(8,128)(2,1)}, bf16[64,2048]{1,0:T(8,128)(2,1)S(1)}, u32[]{:S(2)}, u32[]{:S(2)}) collective-permute-start(bf16[64,2048]{1,0:T(8,128)(2,1)} %get-tuple-element.136), channel_id=1, source_target_pairs={{0,3},{1,0},{2,1},{3,2},{4,7},{5,4},{6,5},{7,6},{8,11},{9,8},{10,9... | collective-permute-start | bytes 786440 | tf_op jit(solution)/shard_map/ppermute | solution.py:69
  349.9 21.9 %all-to-all-start.6 = ((bf16[4,512,384]{2,1,0:T(8,128)(2,1)}), bf16[4,512,384]{2,1,0:T(8,128)(2,1)}, u32[]{:S(2)}, u32[]{:S(2)}) async-start(bf16[4,512,384]{2,1,0:T(8,128)(2,1)} %bitcast.130), calls=%async_computation.6 | async-start | bytes 3145728 | tf_op jit(solution)/shard_map/all_to_all | solution.py:65
  380.8 15.4 %collective-permute-start.43 = (bf16[4,4,256,384]{3,2,1,0:T(8,128)(2,1)}, bf16[4,4,256,384]{3,2,1,0:T(8,128)(2,1)}, u32[]{:S(2)}, u32[]{:S(2)}) collective-permute-start(bf16[4,4,256,384]{3,2,1,0:T(8,128)(2,1)} %get-tuple-element.95), channel_id=1, source_target_pairs={{0,16},{16,0},{1,17},{17,1},{2,18},{18,2},{3,19},{19,3},{4,20},{20... | collective-permute-start | bytes 9437192 | tf_op jit(solution)/shard_map/ppermute | solution.py:237
  401.4 10.1 %collective-permute-start.54 = (bf16[64,2048]{1,0:T(8,128)(2,1)S(1)}, bf16[64,2048]{1,0:T(8,128)(2,1)S(1)}, u32[]{:S(2)}, u32[]{:S(2)}) collective-permute-start(bf16[64,2048]{1,0:T(8,128)(2,1)S(1)} %get-tuple-element.126), channel_id=1, source_target_pairs={{0,3},{1,0},{2,1},{3,2},{4,7},{5,4},{6,5},{7,6},{8,11},{9,8},{10,9... | collective-permute-start | bytes 786440 | tf_op jit(solution)/shard_map/ppermute | solution.py:69
  403.0 11.6 %collective-permute-start.52 = (bf16[64,2048]{1,0:T(8,128)(2,1)S(1)}, bf16[64,2048]{1,0:T(8,128)(2,1)S(1)}, u32[]{:S(2)}, u32[]{:S(2)}) collective-permute-start(bf16[64,2048]{1,0:T(8,128)(2,1)S(1)} %get-tuple-element.128), channel_id=1, source_target_pairs={{0,3},{1,0},{2,1},{3,2},{4,7},{5,4},{6,5},{7,6},{8,11},{9,8},{10,9... | collective-permute-start | bytes 786440 | tf_op jit(solution)/shard_map/ppermute | solution.py:69
  404.0 15.2 %collective-permute-start.47 = (bf16[4,128,512]{2,1,0:T(8,128)(2,1)S(1)}, bf16[4,128,512]{2,1,0:T(8,128)(2,1)S(1)}, u32[]{:S(2)}, u32[]{:S(2)}) collective-permute-start(bf16[4,128,512]{2,1,0:T(8,128)(2,1)S(1)} %get-tuple-element.129), channel_id=1, source_target_pairs={{0,4},{4,8},{8,12},{12,0},{1,5},{5,9},{9,13},{13,1},{2,6},{6,10},{... | collective-permute-start | bytes 1572872 | tf_op jit(solution)/shard_map/ppermute | solution.py:69
  410.3 14.7 %collective-permute-start.49 = (bf16[4,128,512]{2,1,0:T(8,128)(2,1)S(1)}, bf16[4,128,512]{2,1,0:T(8,128)(2,1)S(1)}, u32[]{:S(2)}, u32[]{:S(2)}) collective-permute-start(bf16[4,128,512]{2,1,0:T(8,128)(2,1)S(1)} %get-tuple-element.130), channel_id=1, source_target_pairs={{0,12},{4,0},{8,4},{12,8},{1,13},{5,1},{9,5},{13,9},{2,14},{6,2},{... | collective-permute-start | bytes 1572872 | tf_op jit(solution)/shard_map/ppermute | solution.py:69
  411.5 16.9 %collective-permute-start.48 = (bf16[4,128,512]{2,1,0:T(8,128)(2,1)S(1)}, bf16[4,128,512]{2,1,0:T(8,128)(2,1)S(1)}, u32[]{:S(2)}, u32[]{:S(2)}) collective-permute-start(bf16[4,128,512]{2,1,0:T(8,128)(2,1)S(1)} %get-tuple-element.131), channel_id=1, source_target_pairs={{0,8},{4,12},{8,0},{12,4},{1,9},{5,13},{9,1},{13,5},{2,10},{6,14},... | collective-permute-start | bytes 1572872 | tf_op jit(solution)/shard_map/ppermute | solution.py:69
  414.6 15.1 %collective-permute-start.44 = (bf16[4,128,512]{2,1,0:T(8,128)(2,1)S(1)}, bf16[4,128,512]{2,1,0:T(8,128)(2,1)S(1)}, u32[]{:S(2)}, u32[]{:S(2)}) collective-permute-start(bf16[4,128,512]{2,1,0:T(8,128)(2,1)S(1)} %get-tuple-element.132), channel_id=1, source_target_pairs={{0,32},{32,64},{64,96},{96,0},{1,33},{33,65},{65,97},{97,1},{2,34}... | collective-permute-start | bytes 1572872 | tf_op jit(solution)/shard_map/ppermute | solution.py:69
  417.1 14.1 %collective-permute-start.46 = (bf16[4,128,512]{2,1,0:T(8,128)(2,1)S(1)}, bf16[4,128,512]{2,1,0:T(8,128)(2,1)S(1)}, u32[]{:S(2)}, u32[]{:S(2)}) collective-permute-start(bf16[4,128,512]{2,1,0:T(8,128)(2,1)S(1)} %get-tuple-element.133), channel_id=1, source_target_pairs={{0,96},{32,0},{64,32},{96,64},{1,97},{33,1},{65,33},{97,65},{2,98}... | collective-permute-start | bytes 1572872 | tf_op jit(solution)/shard_map/ppermute | solution.py:69
  419.3 20.1 %collective-permute-start.45 = (bf16[4,128,512]{2,1,0:T(8,128)(2,1)S(1)}, bf16[4,128,512]{2,1,0:T(8,128)(2,1)S(1)}, u32[]{:S(2)}, u32[]{:S(2)}) collective-permute-start(bf16[4,128,512]{2,1,0:T(8,128)(2,1)S(1)} %get-tuple-element.134), channel_id=1, source_target_pairs={{0,64},{32,96},{64,0},{96,32},{1,65},{33,97},{65,1},{97,33},{2,66}... | collective-permute-start | bytes 1572872 | tf_op jit(solution)/shard_map/ppermute | solution.py:69
  425.0 15.5 %collective-permute-start.53 = (bf16[64,2048]{1,0:T(8,128)(2,1)S(1)}, bf16[64,2048]{1,0:T(8,128)(2,1)S(1)}, u32[]{:S(2)}, u32[]{:S(2)}) collective-permute-start(bf16[64,2048]{1,0:T(8,128)(2,1)S(1)} %get-tuple-element.127), channel_id=1, source_target_pairs={{0,1},{1,2},{2,3},{3,0},{4,5},{5,6},{6,7},{7,4},{8,9},{9,10},{10,1... | collective-permute-start | bytes 786440 | tf_op jit(solution)/shard_map/ppermute | solution.py:69
  428.4 12.0 %collective-permute-start.55 = (bf16[64,2048]{1,0:T(8,128)(2,1)S(1)}, bf16[64,2048]{1,0:T(8,128)(2,1)S(1)}, u32[]{:S(2)}, u32[]{:S(2)}) collective-permute-start(bf16[64,2048]{1,0:T(8,128)(2,1)S(1)} %get-tuple-element.124), channel_id=1, source_target_pairs={{0,3},{1,0},{2,1},{3,2},{4,7},{5,4},{6,5},{7,6},{8,11},{9,8},{10,9... | collective-permute-start | bytes 786440 | tf_op jit(solution)/shard_map/ppermute | solution.py:69
  442.7 22.5 %all-to-all-start.7 = ((f32[16,34,128]{2,1,0:T(8,128)}), f32[16,34,128]{2,1,0:T(8,128)S(1)}, u32[]{:S(2)}, u32[]{:S(2)}) async-start(f32[16,34,128]{2,1,0:T(8,128)} %broadcast_in_dim.16), calls=%async_computation.7 | async-start | bytes 655360 | tf_op jit(solution)/shard_map/all_to_all | solution.py:57
  454.3 10.0 %collective-permute-start.58 = (bf16[128,512]{1,0:T(8,128)(2,1)S(1)}, bf16[128,512]{1,0:T(8,128)(2,1)S(1)}, u32[]{:S(2)}, u32[]{:S(2)}) collective-permute-start(bf16[128,512]{1,0:T(8,128)(2,1)S(1)} %get-tuple-element.167), channel_id=1, source_target_pairs={{0,12},{4,0},{8,4},{12,8},{1,13},{5,1},{9,5},{13,9},{2,14},{6,2},{... | collective-permute-start | bytes 393224 | tf_op jit(solution)/shard_map/ppermute | solution.py:69
  458.0 16.6 %collective-permute-start.59 = (bf16[128,512]{1,0:T(8,128)(2,1)}, bf16[128,512]{1,0:T(8,128)(2,1)}, u32[]{:S(2)}, u32[]{:S(2)}) collective-permute-start(bf16[128,512]{1,0:T(8,128)(2,1)} %get-tuple-element.163), channel_id=1, source_target_pairs={{0,32},{32,64},{64,96},{96,0},{1,33},{33,65},{65,97},{97,1},{2,34}... | collective-permute-start | bytes 393224 | tf_op jit(solution)/shard_map/ppermute | solution.py:69
  459.3 15.3 %collective-permute-start.61 = (bf16[128,512]{1,0:T(8,128)(2,1)}, bf16[128,512]{1,0:T(8,128)(2,1)}, u32[]{:S(2)}, u32[]{:S(2)}) collective-permute-start(bf16[128,512]{1,0:T(8,128)(2,1)} %get-tuple-element.164), channel_id=1, source_target_pairs={{0,96},{32,0},{64,32},{96,64},{1,97},{33,1},{65,33},{97,65},{2,98}... | collective-permute-start | bytes 393224 | tf_op jit(solution)/shard_map/ppermute | solution.py:69
  462.1 12.5 %collective-permute-start.60 = (bf16[128,512]{1,0:T(8,128)(2,1)}, bf16[128,512]{1,0:T(8,128)(2,1)S(1)}, u32[]{:S(2)}, u32[]{:S(2)}) collective-permute-start(bf16[128,512]{1,0:T(8,128)(2,1)} %get-tuple-element.165), channel_id=1, source_target_pairs={{0,64},{32,96},{64,0},{96,32},{1,65},{33,97},{65,1},{97,33},{2,66}... | collective-permute-start | bytes 393224 | tf_op jit(solution)/shard_map/ppermute | solution.py:69
  466.0 15.1 %all-to-all-start.8 = ((f32[8,64,128]{2,1,0:T(8,128)}), f32[8,64,128]{2,1,0:T(8,128)S(1)}, u32[]{:S(2)}, u32[]{:S(2)}) async-start(f32[8,64,128]{2,1,0:T(8,128)} %broadcast_in_dim.17), calls=%async_computation.8 | async-start | bytes 524288 | tf_op jit(solution)/shard_map/all_to_all | solution.py:57
  (64 other events, 533.3 us)
Sparse Core Ops, SparseCore 0:
  10.8 52.8 all-gather.4
  66.6 43.1 all-gather.8
  112.6 71.8 all-gather.6
  242.1 117.7 reduce-scatter.1
